TPU v7x, 256 devices: a whole 4x4x8 slice. The times are simulated.
256 devices in a mesh: dp: 32 (over y_lo, z, core), inner: 8 (over x, y_hi).
Axes of the slice: x: 4, y: 4 (y_hi: 2, y_lo: 2; y = y_hi * 2 + y_lo), z: 8, core: 2. Of those that a mesh axis runs over, the one named last changes fastest.
Arguments:
- queries: bfloat16 [65536, 4096], P(('dp', 'inner')), may hold values from -8 to 8
- documents: bfloat16 [65536, 4096], P(('dp', 'inner')), may hold values from -4 to 4
- positives: int32 [65536], P(('dp', 'inner')), may hold values from 0 to 65535, as said below
Outputs:
- row_terms: float32 [65536], P(('dp', 'inner'))
- query_grad: float32 [65536, 4096], P(('dp', 'inner'))
- doc_grad: float32 [65536, 4096], P(('dp', 'inner'))
Inputs may be any that keep to these rules, and one draw needn't show every extreme that they name: positives maps each aligned block of 256 rows onto the same block, each row of it once.
All inputs are finite; a program needn't handle non-finite values.
Results may differ from a plain program's by a relative error of at most 0.0011.
Values may be sent and summed in bfloat16 or wider, within the bound.
No kernel may reach another device: no remote copies, remote signals or barrier semaphores. Data moves between devices by JAX's collectives and lax.ppermute only.
A program may use at most 128 MiB of HBM per device.

v0:
```python
import math

import jax
import jax.numpy as jnp
from jax import lax
from jax.sharding import PartitionSpec as P

STEPS = 3


NEGATIVE = -1e30


def passed_along(value, axis, by):
    length = lax.axis_size(axis)
    return lax.ppermute(value, axis, [(i, (i + by) % length) for i in range(length)])


def contract(left_rows, right_rows):
    return lax.dot_general(
        left_rows, right_rows, (((1,), (1,)), ((), ())), preferred_element_type=jnp.float32
    )


def transposed(coef, embed):
    return lax.dot_general(
        coef, embed, (((0,), (0,)), ((), ())), preferred_element_type=jnp.float32
    )


def combine_stats(first_max, first_sum, second_max, second_sum):
    largest = jnp.maximum(first_max, second_max)
    summed = first_sum * jnp.exp(first_max - largest) + second_sum * jnp.exp(second_max - largest)
    return (largest, summed)


def row_stats(scores):
    largest = jnp.max(scores, axis=1)
    return (largest, jnp.sum(jnp.exp(scores - largest[:, None]), axis=1))


def column_stats(scores):
    largest = jnp.max(scores, axis=0)
    return (largest, jnp.sum(jnp.exp(scores - largest[None, :]), axis=0))


def add_rows(stats, scores):
    tile_max, tile_sum = row_stats(scores)
    return combine_stats(stats[0], stats[1], tile_max, tile_sum)


def ahead_lse(query_lse, doc_lse, offset):
    return passed_along((query_lse, doc_lse), ("dp", "inner"), -offset)


def per_device(queries, documents, positives):
    row_count = queries.shape[0]
    feat_width = queries.shape[1]
    total_rows = row_count * lax.axis_size("dp") * lax.axis_size("inner")
    logit_scale = 2.0 / math.sqrt(feat_width)
    own_block = lax.axis_index("dp") * lax.axis_size("inner") + lax.axis_index("inner")
    columns = jnp.arange(row_count, dtype=jnp.int32)
    same_row = columns[:, None] == columns[None, :]
    is_positive = (positives - own_block * row_count)[:, None] == columns[None, :]
    positive_mask = is_positive.astype(jnp.float32)
    fetched = [(queries, documents)]
    for offset in range(1, STEPS):
        fetched.append(passed_along((queries, documents), ("dp", "inner"), -offset))
    cross0 = logit_scale * contract(queries, documents)
    query_pair0 = jnp.where(same_row, NEGATIVE, logit_scale * contract(queries, queries))
    doc_pair0 = jnp.where(same_row, NEGATIVE, logit_scale * contract(documents, documents))
    positive = jnp.sum(jnp.where(is_positive, cross0, 0.0), axis=1)
    start = (jnp.full((row_count,), NEGATIVE, jnp.float32), jnp.zeros((row_count,), jnp.float32))
    query_stats = add_rows(add_rows(start, cross0), query_pair0)
    doc_stats = add_rows(start, doc_pair0)
    col_max, col_sum = column_stats(cross0)
    doc_stats = combine_stats(doc_stats[0], doc_stats[1], col_max, col_sum)
    stored = []
    for offset in range(1, STEPS):
        far_q, far_d = fetched[offset]
        cross = logit_scale * contract(queries, far_d)
        query_pair = logit_scale * contract(queries, far_q)
        doc_pair = logit_scale * contract(documents, far_d)
        query_stats = add_rows(add_rows(query_stats, cross), query_pair)
        doc_stats = add_rows(doc_stats, doc_pair)
        col_max, col_sum = column_stats(cross)
        pair_max, pair_sum = column_stats(query_pair)
        docs_max, docs_sum = column_stats(doc_pair)
        col_max, col_sum = combine_stats(col_max, col_sum, docs_max, docs_sum)
        returned = passed_along((pair_max, pair_sum, col_max, col_sum), ("dp", "inner"), offset)
        query_stats = combine_stats(query_stats[0], query_stats[1], returned[0], returned[1])
        doc_stats = combine_stats(doc_stats[0], doc_stats[1], returned[2], returned[3])
        stored.append((cross, query_pair, doc_pair))
    query_lse = query_stats[0] + jnp.log(query_stats[1])
    doc_lse = doc_stats[0] + jnp.log(doc_stats[1])
    row_terms = query_lse + doc_lse - 2.0 * positive
    weight = (
        jnp.exp(cross0 - query_lse[:, None])
        + jnp.exp(cross0 - doc_lse[None, :])
        - 2.0 * positive_mask
    )
    coef_qq = 0.5 * (
        jnp.exp(query_pair0 - query_lse[:, None]) + jnp.exp(query_pair0 - query_lse[None, :])
    )
    coef_dd = 0.5 * (jnp.exp(doc_pair0 - doc_lse[:, None]) + jnp.exp(doc_pair0 - doc_lse[None, :]))
    weight = weight.astype(jnp.bfloat16)
    coef_qq = coef_qq.astype(jnp.bfloat16)
    coef_dd = coef_dd.astype(jnp.bfloat16)
    grad_q = jnp.dot(weight, documents, preferred_element_type=jnp.float32) + jnp.dot(
        coef_qq, queries, preferred_element_type=jnp.float32
    )
    grad_d = jnp.dot(coef_dd, documents, preferred_element_type=jnp.float32)
    grad_q = grad_q + transposed(coef_qq, queries)
    grad_d = grad_d + transposed(weight, queries) + transposed(coef_dd, documents)
    outgoing = []
    for offset in range(1, STEPS):
        far_q, far_d = fetched[offset]
        cross, query_pair, doc_pair = stored[offset - 1]
        far_qlse, far_dlse = ahead_lse(query_lse, doc_lse, offset)
        weight = (jnp.exp(cross - query_lse[:, None]) + jnp.exp(cross - far_dlse[None, :])).astype(
            jnp.bfloat16
        )
        coef_qq = (
            jnp.exp(query_pair - query_lse[:, None]) + jnp.exp(query_pair - far_qlse[None, :])
        ).astype(jnp.bfloat16)
        coef_dd = (
            jnp.exp(doc_pair - doc_lse[:, None]) + jnp.exp(doc_pair - far_dlse[None, :])
        ).astype(jnp.bfloat16)
        grad_q = (
            grad_q
            + jnp.dot(weight, far_d, preferred_element_type=jnp.float32)
            + jnp.dot(coef_qq, far_q, preferred_element_type=jnp.float32)
        )
        grad_d = grad_d + jnp.dot(coef_dd, far_d, preferred_element_type=jnp.float32)
        back_q = transposed(coef_qq, queries)
        back_d = transposed(weight, queries) + transposed(coef_dd, documents)
        outgoing.append((back_q, back_d))
    for offset in range(1, STEPS):
        arrived = passed_along(
            (outgoing[offset - 1][0], outgoing[offset - 1][1]), ("dp", "inner"), offset
        )
        grad_q = grad_q + arrived[0]
        grad_d = grad_d + arrived[1]
    factor = logit_scale / (2.0 * total_rows)
    return (row_terms, grad_q * factor, grad_d * factor)


def solution(mesh):
    placed = (P(("dp", "inner"), None), P(("dp", "inner"), None), P(("dp", "inner")))
    return jax.shard_map(
        per_device,
        mesh=mesh,
        in_specs=placed,
        out_specs=(P(("dp", "inner")), P(("dp", "inner"), None), P(("dp", "inner"), None)),
        check_vma=False,
    )
```

profile of v0, /device:TPU:1, one launch (start us, length us, event | category | flops | bytes accessed | tf_op | source)
XLA Modules:
  0.0 585.9 jit_solution(6934487492083425629)
XLA Ops:
  0.7 4.0 collective-permute-start.3
  4.6 3.5 collective-permute-start
  8.9 3.0 fusion.56
  14.6 103.2 %collective-permute-done.3 = bf16[256,4096]{1,0:T(8,128)(2,1)} collective-permute-done((bf16[256,4096]{1,0:T(8,128)(2,1)}, bf16[256,4096]{1,0:T(8,128)(2,1)}, u32[]{:S(2)}, u32[]{:S(2)}) %collective-permute-start.3) | collective-permute-done | bytes 2097184 | tf_op jit(solution)/shard_map/ppermute | solution.py:16
  117.8 2.4 fusion.60
  123.1 17.1 %collective-permute-done = bf16[256,4096]{1,0:T(8,128)(2,1)} collective-permute-done((bf16[256,4096]{1,0:T(8,128)(2,1)}, bf16[256,4096]{1,0:T(8,128)(2,1)}, u32[]{:S(2)}, u32[]{:S(2)}) %collective-permute-start) | collective-permute-done | bytes 2097184 | tf_op jit(solution)/shard_map/ppermute | solution.py:16
  140.3 2.4 fusion.58
  145.9 16.8 %collective-permute-done.4 = bf16[256,4096]{1,0:T(8,128)(2,1)} collective-permute-done((bf16[256,4096]{1,0:T(8,128)(2,1)}, bf16[256,4096]{1,0:T(8,128)(2,1)}, u32[]{:S(2)}, u32[]{:S(2)}) %collective-permute-start.4) | collective-permute-done | bytes 2097184 | tf_op jit(solution)/shard_map/ppermute | solution.py:16
  162.7 2.4 fusion.62
  165.2 20.0 %collective-permute-done.1 = bf16[256,4096]{1,0:T(8,128)(2,1)} collective-permute-done((bf16[256,4096]{1,0:T(8,128)(2,1)}, bf16[256,4096]{1,0:T(8,128)(2,1)}, u32[]{:S(2)}, u32[]{:S(2)}) %collective-permute-start.1) | collective-permute-done | bytes 2097184 | tf_op jit(solution)/shard_map/ppermute | solution.py:16
  190.2 3.8 collective-permute-start.6
  197.4 4.2 collective-permute-start.15
  201.6 3.4 collective-permute-start.13
  215.4 2.8 fusion.51
  218.2 2.7 fusion.47
  225.2 2.4 fusion.52
  227.7 2.4 fusion.50
  230.1 2.4 fusion.48
  232.5 2.4 fusion.53
  234.9 114.9 %collective-permute-done.19 = f32[256,4096]{1,0:T(8,128)} collective-permute-done((f32[256,4096]{1,0:T(8,128)S(1)}, f32[256,4096]{1,0:T(8,128)}, u32[]{:S(2)}, u32[]{:S(2)}) %collective-permute-start.19) | collective-permute-done | bytes 4194336 | tf_op jit(solution)/shard_map/ppermute | solution.py:16
  349.9 137.5 %collective-permute-done.18 = f32[256,4096]{1,0:T(8,128)} collective-permute-done((f32[256,4096]{1,0:T(8,128)S(1)}, f32[256,4096]{1,0:T(8,128)}, u32[]{:S(2)}, u32[]{:S(2)}) %collective-permute-start.18) | collective-permute-done | bytes 4194336 | tf_op jit(solution)/shard_map/ppermute | solution.py:16
  487.4 7.9 %fusion.6 = f32[256,4096]{1,0:T(8,128)} fusion(f32[256,4096]{1,0:T(8,128)} %collective-permute-done.19, f32[256,4096]{1,0:T(8,128)} %collective-permute-done.18, f32[256,4096]{1,0:T(8,128)S(1)} %fusion.53, f32[256,4096]{1,0:T(8,128)S(1)} %convolution_add_fusion.3, bf16[256,4096]{1,0:T(8,128)(2,1)} %collective-permute-done, ...), kind=kOutput, calls=%fused_computation.14 | convolution fusion | flops 542375936 | bytes 23332864 | tf_op jit(solution)/shard_map/dot_general | solution.py:134
  495.3 82.0 %collective-permute-done.16 = f32[256,4096]{1,0:T(8,128)} collective-permute-done((f32[256,4096]{1,0:T(8,128)}, f32[256,4096]{1,0:T(8,128)}, u32[]{:S(2)}, u32[]{:S(2)}) %collective-permute-start.16) | collective-permute-done | bytes 4194336 | tf_op jit(solution)/shard_map/ppermute | solution.py:16
  577.2 8.5 %fusion.9 = f32[256,4096]{1,0:T(8,128)} fusion(f32[256,4096]{1,0:T(8,128)} %collective-permute-done.17, f32[256,4096]{1,0:T(8,128)} %collective-permute-done.16, f32[256,4096]{1,0:T(8,128)S(1)} %fusion.52, f32[256,4096]{1,0:T(8,128)S(1)} %fusion.50, f32[256,4096]{1,0:T(8,128)S(1)} %fusion.48, f32[256,4096]{1,0:T(8,128)S(1)} %convolution_add_fusion.6, ...), kind=kOutput, calls=%fused_computation.17 | convolution fusion | flops 544473088 | bytes 31721472 | tf_op jit(solution)/shard_map/dot_general | solution.py:131
  (59 shorter events, 32.7 us)
Async XLA Ops:
  0.6 11.4 %copy-start.1 = (bf16[256,4096]{1,0:T(8,128)(2,1)S(1)}, bf16[256,4096]{1,0:T(8,128)(2,1)}, u32[]{:S(2)}) copy-start(bf16[256,4096]{1,0:T(8,128)(2,1)} %param.4) | copy-start | bytes 6291460
  0.6 11.3 %copy-start.2 = (s32[256]{0:T(256)S(1)}, s32[256]{0:T(256)}, u32[]{:S(2)}) copy-start(s32[256]{0:T(256)} %param.5) | copy-start | bytes 3076
  0.7 117.1 %collective-permute-start.3 = (bf16[256,4096]{1,0:T(8,128)(2,1)}, bf16[256,4096]{1,0:T(8,128)(2,1)}, u32[]{:S(2)}, u32[]{:S(2)}) collective-permute-start(bf16[256,4096]{1,0:T(8,128)(2,1)} %param.4), channel_id=1, source_target_pairs={{0,254},{1,255},{2,0},{3,1},{4,2},{5,3},{6,4},{7,5},{8,6},{9,7},{1... | collective-permute-start | bytes 6291464 | tf_op jit(solution)/shard_map/ppermute | solution.py:16
  4.6 135.6 %collective-permute-start = (bf16[256,4096]{1,0:T(8,128)(2,1)}, bf16[256,4096]{1,0:T(8,128)(2,1)}, u32[]{:S(2)}, u32[]{:S(2)}) collective-permute-start(bf16[256,4096]{1,0:T(8,128)(2,1)} %param.4), channel_id=1, source_target_pairs={{0,255},{1,0},{2,1},{3,2},{4,3},{5,4},{6,5},{7,6},{8,7},{9,8},{10,... | collective-permute-start | bytes 6291464 | tf_op jit(solution)/shard_map/ppermute | solution.py:16
  8.1 154.7 %collective-permute-start.4 = (bf16[256,4096]{1,0:T(8,128)(2,1)}, bf16[256,4096]{1,0:T(8,128)(2,1)}, u32[]{:S(2)}, u32[]{:S(2)}) collective-permute-start(bf16[256,4096]{1,0:T(8,128)(2,1)} %param.3), channel_id=1, source_target_pairs={{0,254},{1,255},{2,0},{3,1},{4,2},{5,3},{6,4},{7,5},{8,6},{9,7},{1... | collective-permute-start | bytes 6291464 | tf_op jit(solution)/shard_map/ppermute | solution.py:16
  8.6 176.6 %collective-permute-start.1 = (bf16[256,4096]{1,0:T(8,128)(2,1)}, bf16[256,4096]{1,0:T(8,128)(2,1)}, u32[]{:S(2)}, u32[]{:S(2)}) collective-permute-start(bf16[256,4096]{1,0:T(8,128)(2,1)} %param.3), channel_id=1, source_target_pairs={{0,255},{1,0},{2,1},{3,2},{4,3},{5,4},{6,5},{7,6},{8,7},{9,8},{10,... | collective-permute-start | bytes 6291464 | tf_op jit(solution)/shard_map/ppermute | solution.py:16
  12.0 1.6 copy-start
  122.9 65.2 %collective-permute-start.11 = (f32[256]{0:T(256)S(1)}, f32[256]{0:T(256)S(1)}, u32[]{:S(2)}, u32[]{:S(2)}) collective-permute-start(f32[256]{0:T(256)S(1)} %get-tuple-element.37), channel_id=1, source_target_pairs={{0,2},{1,3},{2,4},{3,5},{4,6},{5,7},{6,8},{7,9},{8,10},{9,11},{10,... | collective-permute-start | bytes 3080 | tf_op jit(solution)/shard_map/ppermute | solution.py:16
  123.0 65.2 %collective-permute-start.9 = (f32[256]{0:T(256)S(1)}, f32[256]{0:T(256)S(1)}, u32[]{:S(2)}, u32[]{:S(2)}) collective-permute-start(f32[256]{0:T(256)S(1)} %get-tuple-element.38), channel_id=1, source_target_pairs={{0,2},{1,3},{2,4},{3,5},{4,6},{5,7},{6,8},{7,9},{8,10},{9,11},{10,... | collective-permute-start | bytes 3080 | tf_op jit(solution)/shard_map/ppermute | solution.py:16
  145.4 44.8 %collective-permute-start.10 = (f32[256]{0:T(256)S(1)}, f32[256]{0:T(256)S(1)}, u32[]{:S(2)}, u32[]{:S(2)}) collective-permute-start(f32[256]{0:T(256)S(1)} %get-tuple-element.35), channel_id=1, source_target_pairs={{0,1},{1,2},{2,3},{3,4},{4,5},{5,6},{6,7},{7,8},{8,9},{9,10},{10,1... | collective-permute-start | bytes 3080 | tf_op jit(solution)/shard_map/ppermute | solution.py:16
  165.1 31.4 %collective-permute-start.5 = (f32[256]{0:T(256)S(1)}, f32[256]{0:T(256)S(1)}, u32[]{:S(2)}, u32[]{:S(2)}) collective-permute-start(f32[256]{0:T(256)S(1)} %get-tuple-element.31), channel_id=1, source_target_pairs={{0,2},{1,3},{2,4},{3,5},{4,6},{5,7},{6,8},{7,9},{8,10},{9,11},{10,... | collective-permute-start | bytes 3080 | tf_op jit(solution)/shard_map/ppermute | solution.py:16
  187.6 9.2 %collective-permute-start.2 = (f32[256]{0:T(256)S(1)}, f32[256]{0:T(256)S(1)}, u32[]{:S(2)}, u32[]{:S(2)}) collective-permute-start(f32[256]{0:T(256)S(1)} %get-tuple-element.27), channel_id=1, source_target_pairs={{0,1},{1,2},{2,3},{3,4},{4,5},{5,6},{6,7},{7,8},{8,9},{9,10},{10,1... | collective-permute-start | bytes 3080 | tf_op jit(solution)/shard_map/ppermute | solution.py:16
  188.1 7.4 %collective-permute-start.8 = (f32[256]{0:T(256)S(1)}, f32[256]{0:T(256)S(1)}, u32[]{:S(2)}, u32[]{:S(2)}) collective-permute-start(f32[256]{0:T(256)S(1)} %get-tuple-element.36), channel_id=1, source_target_pairs={{0,1},{1,2},{2,3},{3,4},{4,5},{5,6},{6,7},{7,8},{8,9},{9,10},{10,1... | collective-permute-start | bytes 3080 | tf_op jit(solution)/shard_map/ppermute | solution.py:16
  188.2 8.3 %collective-permute-start.7 = (f32[256]{0:T(256)S(1)}, f32[256]{0:T(256)S(1)}, u32[]{:S(2)}, u32[]{:S(2)}) collective-permute-start(f32[256]{0:T(256)S(1)} %get-tuple-element.29), channel_id=1, source_target_pairs={{0,2},{1,3},{2,4},{3,5},{4,6},{5,7},{6,8},{7,9},{8,10},{9,11},{10,... | collective-permute-start | bytes 3080 | tf_op jit(solution)/shard_map/ppermute | solution.py:16
  190.2 6.6 %collective-permute-start.6 = (f32[256]{0:T(256)S(1)}, f32[256]{0:T(256)S(1)}, u32[]{:S(2)}, u32[]{:S(2)}) collective-permute-start(f32[256]{0:T(256)S(1)} %get-tuple-element.25), channel_id=1, source_target_pairs={{0,1},{1,2},{2,3},{3,4},{4,5},{5,6},{6,7},{7,8},{8,9},{9,10},{10,1... | collective-permute-start | bytes 3080 | tf_op jit(solution)/shard_map/ppermute | solution.py:16
  197.4 18.0 %collective-permute-start.15 = (f32[256]{0:T(256)S(1)}, f32[256]{0:T(256)S(1)}, u32[]{:S(2)}, u32[]{:S(2)}) collective-permute-start(f32[256]{0:T(256)S(1)} %get-tuple-element.34), channel_id=1, source_target_pairs={{0,254},{1,255},{2,0},{3,1},{4,2},{5,3},{6,4},{7,5},{8,6},{9,7},{1... | collective-permute-start | bytes 3080 | tf_op jit(solution)/shard_map/ppermute | solution.py:16
  201.6 16.6 %collective-permute-start.13 = (f32[256]{0:T(256)S(1)}, f32[256]{0:T(256)S(1)}, u32[]{:S(2)}, u32[]{:S(2)}) collective-permute-start(f32[256]{0:T(256)S(1)} %get-tuple-element.34), channel_id=1, source_target_pairs={{0,255},{1,0},{2,1},{3,2},{4,3},{5,4},{6,5},{7,6},{8,7},{9,8},{10,... | collective-permute-start | bytes 3080 | tf_op jit(solution)/shard_map/ppermute | solution.py:16
  205.0 4.0 collective-permute-start.14
  207.8 4.2 collective-permute-start.12
  210.6 139.2 %collective-permute-start.19 = (f32[256,4096]{1,0:T(8,128)S(1)}, f32[256,4096]{1,0:T(8,128)}, u32[]{:S(2)}, u32[]{:S(2)}) collective-permute-start(f32[256,4096]{1,0:T(8,128)S(1)} %convolution_add_fusion), channel_id=1, source_target_pairs={{0,2},{1,3},{2,4},{3,5},{4,6},{5,7},{6,8},{7,9},{8,10},{9,11},{10,... | collective-permute-start | bytes 12582920 | tf_op jit(solution)/shard_map/ppermute | solution.py:16
  213.7 273.7 %collective-permute-start.18 = (f32[256,4096]{1,0:T(8,128)S(1)}, f32[256,4096]{1,0:T(8,128)}, u32[]{:S(2)}, u32[]{:S(2)}) collective-permute-start(f32[256,4096]{1,0:T(8,128)S(1)} %convolution_add_fusion.1), channel_id=1, source_target_pairs={{0,1},{1,2},{2,3},{3,4},{4,5},{5,6},{6,7},{7,8},{8,9},{9,10},{10,1... | collective-permute-start | bytes 12582920 | tf_op jit(solution)/shard_map/ppermute | solution.py:16
  218.2 277.0 %collective-permute-start.17 = (f32[256,4096]{1,0:T(8,128)}, f32[256,4096]{1,0:T(8,128)}, u32[]{:S(2)}, u32[]{:S(2)}) collective-permute-start(f32[256,4096]{1,0:T(8,128)} %fusion.51), channel_id=1, source_target_pairs={{0,2},{1,3},{2,4},{3,5},{4,6},{5,7},{6,8},{7,9},{8,10},{9,11},{10,... | collective-permute-start | bytes 12582920 | tf_op jit(solution)/shard_map/ppermute | solution.py:16
  220.9 356.3 %collective-permute-start.16 = (f32[256,4096]{1,0:T(8,128)}, f32[256,4096]{1,0:T(8,128)}, u32[]{:S(2)}, u32[]{:S(2)}) collective-permute-start(f32[256,4096]{1,0:T(8,128)} %fusion.47), channel_id=1, source_target_pairs={{0,1},{1,2},{2,3},{3,4},{4,5},{5,6},{6,7},{7,8},{8,9},{9,10},{10,1... | collective-permute-start | bytes 12582920 | tf_op jit(solution)/shard_map/ppermute | solution.py:16
where the time goes:
time: 594 us; the launch traced here: 586 us
  waiting for transfers between devices  495 us (83%)
  matrix products  59 us (10%)
  starting transfers between devices  28.7 us (5%)
    ppermute x20, waiting for transfers between devices, passed_along(): lax.ppermute(value, axis, [(i, (i + by) % length) for i in range(length)])  495 us
    ppermute x20, starting transfers between devices, passed_along(): lax.ppermute(value, axis, [(i, (i + by) % length) for i in range(length)])  28.7 us
    dot_general x9, matrix products, contract(): lax.dot_general(left_rows, right_rows, (((1,), (1,)), ((), ())), preferre...  19.1 us
  transfers between devices with their start and end apart: 20, of which 11 were waited for; matrix products, arithmetic and copies ran while one was open for 9% of the time, Pallas kernels for 0%

commit v1 on v0

v1 whole, which is shorter than its diff:
```python
import math

import jax
import jax.numpy as jnp
from jax import lax
from jax.experimental import pallas as pl
from jax.experimental.pallas import tpu as pltpu
from jax.sharding import PartitionSpec as P

AXES = ("dp", "inner")
NEGATIVE = -1e30
CHUNK = 512
VMEM_LIMIT = 50 * 1024 * 1024


def contract(left_rows, right_rows):
    return lax.dot_general(
        left_rows, right_rows, (((1,), (1,)), ((), ())), preferred_element_type=jnp.float32
    )


def sent(value, target, senders=None):
    count = lax.axis_size(AXES)
    senders = range(count) if senders is None else senders
    return lax.ppermute(value, AXES, [(i, target(i) % count) for i in senders])


def down_hop(half):
    return lambda i: i - half if i >= half else (i ^ 1) + half


def up_hop(half):
    return lambda i: (i - half) ^ 1 if i >= half else i + half


def within_half(half, step):
    return lambda i: i - i % half + (i + step) % half


def as_columns(row):
    size = row.shape[1]
    return jnp.broadcast_to(row, (size, size)).T


def statistics(tiles):
    largest = tiles[0]
    for tile in tiles[1:]:
        largest = jnp.maximum(largest, tile)
    largest = jnp.max(largest, axis=1, keepdims=True)
    total = jnp.exp(tiles[0] - largest)
    for tile in tiles[1:]:
        total = total + jnp.exp(tile - largest)
    lse = largest + jnp.log(jnp.sum(total, axis=1, keepdims=True))
    return jnp.broadcast_to(lse, tiles[0].shape).T[:1]


TILES = 24


def read_tiles(place, *refs):
    even, first, last, edge = [place[k] == 1 for k in range(4)]
    qq, qd, dq, dd, qq_n2, qd_n2, dd_n2, dq_p2, dd_p2, qq_p2 = [ref[...] for ref in refs[:10]]
    qq_pair, dq_pair, qd_pair, dd_pair, qq_edge, dq_edge = [ref[...] for ref in refs[10:16]]
    qd_low, dd_low, qd_high, dd_high, qq_diag, dq_diag, qq_swap, dq_swap = [
        ref[...] for ref in refs[16:]
    ]
    qd_diag = jnp.concatenate([qd_low, qd_high], axis=1)
    dd_diag = jnp.concatenate([dd_low, dd_high], axis=1)
    qq_diag = jnp.where(edge, qq_edge, qq_diag)
    dq_diag = jnp.where(edge, dq_edge, dq_diag)
    q_tiles = [
        jnp.where(last, qq_swap, qq_n2),
        jnp.where(even, qq_pair, qq_diag),
        qd,
        qq,
        qd_n2,
        jnp.where(first, qq_swap, qq_p2),
        jnp.where(even, qd_pair, qd_diag),
        jnp.where(even, qq_diag, qq_pair),
    ]
    d_tiles = [
        dd,
        dq,
        dd_n2,
        jnp.where(first, dq_swap, dq_p2),
        jnp.where(even, dd_pair, dd_diag),
        jnp.where(even, dq_diag, dq_pair),
        dd_p2,
        jnp.where(even, dd_diag, dd_pair),
    ]
    return q_tiles, d_tiles


def lse_kernel(place, pos, *refs):
    lse, row_terms = refs[TILES:]
    q_tiles, d_tiles = read_tiles(place, *refs[:TILES])
    q_row = statistics(q_tiles)
    d_row = statistics(d_tiles)
    lse[0:1, :] = q_row
    lse[1:2, :] = d_row
    cross = d_tiles[1]
    doc = lax.broadcasted_iota(jnp.int32, cross.shape, 0)
    positive = jnp.sum(jnp.where(doc == pos[...], cross, 0.0), axis=0, keepdims=True)
    row_terms[...] = q_row + d_row - 2.0 * positive


def grad_kernel(factor, place, pos, *refs):
    tiles, refs = refs[:TILES], refs[TILES:]
    lse, lse_n1, lse_p1, lse_n2, lse_p2 = refs[:5]
    own_q, own_d, q_n2, d_n2, q_p2, d_p2, q_pair, d_pair = refs[5:13]
    q_edge, d_low, d_high, q_diag, q_swap = refs[13:18]
    grad_q, grad_d, coef_q, coef_d, rows, arrived = refs[18:]
    step = pl.program_id(0)
    size = grad_q.shape[0]
    width = own_q.shape[1]
    chunk = rows.shape[2]
    even, first, last, edge = [place[k] == 1 for k in range(4)]

    def bring(source, slot, offset=0, taken=None):
        def start():
            for part in range(width // chunk):
                pltpu.make_async_copy(
                    source.at[:, pl.ds(part * chunk, chunk)],
                    rows.at[part, pl.ds(slot * size + offset, source.shape[0]), :],
                    arrived.at[part],
                ).start()

        if taken is None:
            start()
        else:
            pl.when(taken)(start)

    @pl.when(step == 0)
    def _():
        half = size // 2
        odd = jnp.logical_not(even)
        bring(own_d, 2)
        bring(own_q, 3)
        bring(d_n2, 4)
        bring(d_p2, 8)
        bring(q_n2, 0, taken=jnp.logical_not(last))
        bring(q_swap, 0, taken=last)
        bring(q_p2, 5, taken=jnp.logical_not(first))
        bring(q_swap, 5, taken=first)
        for turn, pair_slots, diag_slots in ((even, (1, 6), (7, 9)), (odd, (7, 9), (1, 6))):
            bring(q_pair, pair_slots[0], taken=turn)
            bring(d_pair, pair_slots[1], taken=turn)
            bring(q_diag, diag_slots[0], taken=turn & jnp.logical_not(edge))
            bring(q_edge, diag_slots[0], taken=turn & edge)
            bring(d_low, diag_slots[1], taken=turn)
            bring(d_high, diag_slots[1], half, taken=turn)

        q_tiles, d_tiles = read_tiles(place, *tiles)
        q_col = as_columns(lse[0:1, :])
        d_col = as_columns(lse[1:2, :])
        lane = lax.broadcasted_iota(jnp.int32, (size, size), 1)
        sublane = lax.broadcasted_iota(jnp.int32, (size, size), 0)
        pos_col = as_columns(pos[...])

        def put(target, slot, tile, column, row, taken=None):
            value = jnp.exp(tile - column) + jnp.exp(tile - row)
            if taken is not None:
                value = value - jnp.where(taken, 2.0, 0.0)
            target[:, slot * size : (slot + 1) * size] = value.astype(jnp.bfloat16)

        q_of = [ref[0:1, :] for ref in (lse_n2, lse_n1, lse, lse, lse_n2, lse_p2, lse_n1, lse_p1)]
        d_of = [ref[1:2, :] for ref in (lse_n2, lse_n1, lse, lse, lse_n2, lse_p2, lse_n1, lse_p1)]
        q_kind = [q_of, q_of, d_of, q_of, d_of, q_of, d_of, q_of]
        for slot in range(8):
            taken = pos_col == lane if slot == 2 else None
            put(coef_q, slot, q_tiles[slot], q_col, q_kind[slot][slot], taken)
        d_rows = [
            lse[1:2, :],
            lse[0:1, :],
            lse_n2[1:2, :],
            lse_p2[0:1, :],
            lse_n1[1:2, :],
            lse_p1[0:1, :],
            lse_p2[1:2, :],
            lse_p1[1:2, :],
        ]
        for slot in range(8):
            taken = pos[...] == sublane if slot == 1 else None
            put(coef_d, slot, d_tiles[slot], d_col, d_rows[slot], taken)

    pltpu.make_async_copy(rows.at[step], rows.at[step], arrived.at[step]).wait()
    depth = coef_q.shape[1]
    grad_q[...] = factor * jnp.dot(
        coef_q[...], rows[step, 0:depth, :], preferred_element_type=jnp.float32
    )
    grad_d[...] = factor * jnp.dot(
        coef_d[...], rows[step, 2 * size :, :], preferred_element_type=jnp.float32
    )


def per_device(queries, documents, positives):
    size, width = queries.shape
    count = lax.axis_size(AXES)
    scale = 2.0 / math.sqrt(width)
    factor = scale / (2.0 * size * count)
    own_block = lax.axis_index("dp") * lax.axis_size("inner") + lax.axis_index("inner")
    half = count // 2
    within = own_block % half
    first, last = within < 2, within >= half - 2
    place = jnp.stack(
        [own_block % 2 == 0, first, last, (within == 0) | (within == half - 1)]
    ).astype(jnp.int32)
    pos = (positives - own_block * size).reshape(1, size)
    index = jnp.arange(size)
    same_row = index[:, None] == index[None, :]
    down, up = down_hop(half), up_hop(half)

    q_down = sent(queries, down)
    d_up = sent(documents, up)
    d_p2 = sent(documents, lambda i: i + 2)
    d_n2 = sent(documents, lambda i: i - 2)
    q_edge = sent(
        queries,
        lambda i: i - 1 if i % half == 0 else i + 1,
        [0, half - 1, half, count - 1],
    )
    q_down, d_up = lax.optimization_barrier((q_down, d_up))
    q_pair = sent(q_down, down)
    d_pair = sent(d_up, up)
    q_own, d_p2, d_n2, q_edge, q_down, d_up = lax.optimization_barrier(
        (queries, d_p2, d_n2, q_edge, q_down, d_up)
    )
    q_p2 = sent(q_own, within_half(half, 2))
    q_n2 = sent(q_own, within_half(half, -2))
    d_turn = jnp.where(own_block % 2 == 0, d_n2, d_p2)
    q_diag = sent(q_pair, lambda i: within_half(half, -2 if i % 2 else 2)(i))
    d_turn, d_pair = lax.optimization_barrier((d_turn, d_pair))
    d_low = sent(d_turn[: size // 2], up)
    d_high = sent(d_turn[size // 2 :], down)
    d_low, d_high, q_n2, q_p2 = lax.optimization_barrier((d_low, d_high, q_n2, q_p2))
    d_low = sent(d_low, up)
    d_high = sent(d_high, down)
    q_swap = sent(
        jnp.where(last, q_n2, q_p2),
        lambda i: i + half,
        [i for i in range(count) if i % half < 2 or i % half >= half - 2],
    )

    def tile(left, right):
        return scale * contract(left, right)

    def masked(tile):
        return jnp.where(same_row, NEGATIVE, tile)

    tiles = [
        masked(tile(queries, queries)),
        tile(queries, documents),
        tile(documents, queries),
        masked(tile(documents, documents)),
        tile(queries, q_n2),
        tile(queries, d_n2),
        tile(documents, d_n2),
        tile(documents, q_p2),
        tile(documents, d_p2),
        tile(queries, q_p2),
        tile(queries, q_pair),
        tile(documents, q_pair),
        tile(queries, d_pair),
        tile(documents, d_pair),
        tile(queries, q_edge),
        tile(documents, q_edge),
        tile(queries, d_low),
        tile(documents, d_low),
        tile(queries, d_high),
        tile(documents, d_high),
        tile(queries, q_diag),
        tile(documents, q_diag),
        tile(queries, q_swap),
        tile(documents, q_swap),
    ]
    in_vmem = pl.BlockSpec(memory_space=pltpu.VMEM)
    in_smem = pl.BlockSpec(memory_space=pltpu.SMEM)
    anywhere = pl.BlockSpec(memory_space=pl.ANY)
    lse, row_terms = pl.pallas_call(
        lse_kernel,
        out_shape=(
            jax.ShapeDtypeStruct((2, size), jnp.float32),
            jax.ShapeDtypeStruct((1, size), jnp.float32),
        ),
        in_specs=[in_smem] + [in_vmem] * (1 + TILES),
        out_specs=(in_vmem, in_vmem),
        compiler_params=pltpu.CompilerParams(vmem_limit_bytes=VMEM_LIMIT),
        cost_estimate=pl.CostEstimate(
            flops=0, bytes_accessed=18 * size * size * 4, transcendentals=16 * size * size
        ),
    )(place, pos, *tiles)
    lse_n1 = sent(lse, lambda i: i - 1)
    lse_p1 = sent(lse, lambda i: i + 1)
    lse_n2 = sent(lse, lambda i: i - 2)
    lse_p2 = sent(lse, lambda i: i + 2)
    sources = [queries, documents, q_n2, d_n2, q_p2, d_p2, q_pair, d_pair]
    sources += [q_edge, d_low, d_high, q_diag, q_swap]
    parts = width // CHUNK

    def kernel(*refs):
        grad_kernel(factor, *refs)

    grad_block = pl.BlockSpec((size, CHUNK), lambda step: (0, step))
    grad_q, grad_d = pl.pallas_call(
        kernel,
        grid=(parts,),
        out_shape=(jax.ShapeDtypeStruct((size, width), jnp.float32),) * 2,
        in_specs=[in_smem] + [in_vmem] * (6 + TILES) + [anywhere] * len(sources),
        out_specs=(grad_block, grad_block),
        scratch_shapes=[
            pltpu.VMEM((size, 8 * size), jnp.bfloat16),
            pltpu.VMEM((size, 8 * size), jnp.bfloat16),
            pltpu.VMEM((parts, 10 * size, CHUNK), jnp.bfloat16),
            pltpu.SemaphoreType.DMA((parts,)),
        ],
        compiler_params=pltpu.CompilerParams(vmem_limit_bytes=VMEM_LIMIT),
        cost_estimate=pl.CostEstimate(
            flops=2 * 16 * size * size * width,
            bytes_accessed=(20 + 8) * size * width,
            transcendentals=32 * size * size,
        ),
    )(place, pos, *tiles, lse, lse_n1, lse_p1, lse_n2, lse_p2, *sources)
    return (row_terms.reshape(size), grad_q, grad_d)


def solution(mesh):
    placed = (P(AXES, None), P(AXES, None), P(AXES))
    return jax.shard_map(
        per_device,
        mesh=mesh,
        in_specs=placed,
        out_specs=(P(AXES), P(AXES, None), P(AXES, None)),
        check_vma=False,
    )
```

time: 594 us -> 234 us (0.39)
  the two profiles are of different devices: /device:TPU:1 before, /device:TPU:0 now
where the time goes in v1:
time: 234 us; the launch traced here: 233 us
  waiting for transfers between devices  124 us (53%)
  starting transfers between devices  43.9 us (19%)
  matrix products  37.6 us (16%)
  Pallas kernels  22.8 us (10%)
    ppermute x19, waiting for transfers between devices, sent(): return lax.ppermute(value, AXES, [(i, target(i) % count) for i in senders])  124 us
    ppermute x19, starting transfers between devices, sent(): return lax.ppermute(value, AXES, [(i, target(i) % count) for i in senders])  43.9 us
    dot_general x24, matrix products, contract(): lax.dot_general(left_rows, right_rows, (((1,), (1,)), ((), ())), preferre...  37.6 us
    pallas_call x1, Pallas kernels, per_device(): pl.pallas_call(kernel, grid=(parts,), out_shape=(jax.ShapeDtypeStruct((si...  19.7 us
  transfers between devices with their start and end apart: 19, of which 9 were waited for; matrix products, arithmetic and copies ran while one was open for 16% of the time, Pallas kernels for 0%

profile of v1, /device:TPU:0, one launch (start us, length us, event | category | flops | bytes accessed | tf_op | source)
XLA Modules:
  0.0 232.7 jit_solution(5585151603829827969)
XLA Ops:
  2.7 10.8 %collective-permute-start.2 = (bf16[256,4096]{1,0:T(8,128)(2,1)}, bf16[256,4096]{1,0:T(8,128)(2,1)}, u32[]{:S(2)}, u32[]{:S(2)}) collective-permute-start(bf16[256,4096]{1,0:T(8,128)(2,1)} %refs_31_.1), channel_id=1, source_target_pairs={{0,255},{127,128},{128,127},{255,0}} | collective-permute-start | bytes 6291464 | tf_op jit(solution)/shard_map/ppermute | solution.py:25
  15.6 3.1 %convolution_multiply_fusion.17 = f32[256,256]{0,1:T(8,128)S(1)} fusion(bf16[256,4096]{1,0:T(8,128)(2,1)} %refs_32_.1, bf16[256,4096]{1,0:T(8,128)(2,1)} %refs_31_.1), kind=kOutput, calls=%fused_computation.36 | convolution fusion | flops 536936448 | bytes 4456448 | tf_op jit(solution)/shard_map/dot_general | solution.py:17
  18.9 2.3 %convolution_multiply_fusion.18 = f32[256,256]{0,1:T(8,128)S(1)} fusion(bf16[256,4096]{1,0:T(8,128)(2,1)S(1)} %copy-done, bf16[256,4096]{1,0:T(8,128)(2,1)} %refs_32_.1), kind=kOutput, calls=%fused_computation.37 | convolution fusion | flops 536936448 | bytes 4456448 | tf_op jit(solution)/shard_map/dot_general | solution.py:17
  22.2 3.0 %fusion.16 = f32[256,256]{0,1:T(8,128)S(1)} fusion(bf16[256,4096]{1,0:T(8,128)(2,1)} %refs_32_.1), kind=kOutput, calls=%fused_computation.35 | convolution fusion | flops 537067520 | bytes 2359296 | tf_op jit(solution)/shard_map/dot_general | solution.py:17
  25.4 43.5 %collective-permute-done.3 = bf16[256,4096]{1,0:T(8,128)(2,1)} collective-permute-done((bf16[256,4096]{1,0:T(8,128)(2,1)}, bf16[256,4096]{1,0:T(8,128)(2,1)}, u32[]{:S(2)}, u32[]{:S(2)}) %collective-permute-start.3) | collective-permute-done | bytes 2097184 | tf_op jit(solution)/shard_map/ppermute | solution.py:25
  69.0 4.1 %collective-permute-done.4 = bf16[256,4096]{1,0:T(8,128)(2,1)} collective-permute-done((bf16[256,4096]{1,0:T(8,128)(2,1)}, bf16[256,4096]{1,0:T(8,128)(2,1)}, u32[]{:S(2)}, u32[]{:S(2)}) %collective-permute-start.4) | collective-permute-done | bytes 2097184 | tf_op jit(solution)/shard_map/ppermute | solution.py:25
  73.1 2.0 collective-permute-start.5
  75.1 3.7 %fusion.4.refs_15_.refs_17_ = f32[256,256]{1,0:T(8,128)} fusion(bf16[256,4096]{1,0:T(8,128)(2,1)} %collective-permute-done.2.refs_39_, bf16[256,4096]{1,0:T(8,128)(2,1)} %refs_32_.1), kind=kOutput, calls=%fused_computation.11 | convolution fusion | flops 536936448 | bytes 4456448 | tf_op jit(solution)/shard_map/dot_general | solution.py:17
  78.8 3.2 %fusion.5.refs_14_.refs_16_ = f32[256,256]{1,0:T(8,128)} fusion(bf16[256,4096]{1,0:T(8,128)(2,1)} %collective-permute-done.2.refs_39_, bf16[256,4096]{1,0:T(8,128)(2,1)S(1)} %copy-done), kind=kOutput, calls=%fused_computation.13 | convolution fusion | flops 536936448 | bytes 4456448 | tf_op jit(solution)/shard_map/dot_general | solution.py:17
  82.0 5.1 %collective-permute-start.8 = (bf16[256,4096]{1,0:T(8,128)(2,1)S(1)}, bf16[256,4096]{1,0:T(8,128)(2,1)S(1)}, u32[]{:S(2)}, u32[]{:S(2)}) collective-permute-start(bf16[256,4096]{1,0:T(8,128)(2,1)S(1)} %copy-done), channel_id=1, source_target_pairs={{0,126},{1,127},{2,0},{3,1},{4,2},{5,3},{6,4},{7,5},{8,6},{9,7},{1... | collective-permute-start | bytes 6291464 | tf_op jit(solution)/shard_map/ppermute | solution.py:25
  87.0 2.3 %fusion.13.refs_6_.refs_8_ = f32[256,256]{1,0:T(8,128)S(1)} fusion(bf16[256,4096]{1,0:T(8,128)(2,1)} %collective-permute-done.1.refs_34_, bf16[256,4096]{1,0:T(8,128)(2,1)S(1)} %copy-done.1), kind=kOutput, calls=%fused_computation.29 | convolution fusion | flops 536936448 | bytes 4456448 | tf_op jit(solution)/shard_map/dot_general | solution.py:17
  89.4 2.3 %fusion.14.refs_5_.refs_7_ = f32[256,256]{1,0:T(8,128)S(1)} fusion(bf16[256,4096]{1,0:T(8,128)(2,1)} %collective-permute-done.1.refs_34_, bf16[256,4096]{1,0:T(8,128)(2,1)S(1)} %copy-done), kind=kOutput, calls=%fused_computation.31 | convolution fusion | flops 536936448 | bytes 4456448 | tf_op jit(solution)/shard_map/dot_general | solution.py:17
  91.7 2.3 %fusion.11.refs_8_.refs_10_ = f32[256,256]{1,0:T(8,128)S(1)} fusion(bf16[256,4096]{1,0:T(8,128)(2,1)} %collective-permute-done.refs_36_, bf16[256,4096]{1,0:T(8,128)(2,1)S(1)} %copy-done.1), kind=kOutput, calls=%fused_computation.25 | convolution fusion | flops 536936448 | bytes 4456448 | tf_op jit(solution)/shard_map/dot_general | solution.py:17
  95.9 24.8 %collective-permute-done.5.refs_38_ = bf16[256,4096]{1,0:T(8,128)(2,1)S(1)} collective-permute-done((bf16[256,4096]{1,0:T(8,128)(2,1)}, bf16[256,4096]{1,0:T(8,128)(2,1)S(1)}, u32[]{:S(2)}, u32[]{:S(2)}) %collective-permute-start.5) | collective-permute-done | bytes 2097184 | tf_op jit(solution)/shard_map/ppermute | solution.py:25
  128.1 15.6 %collective-permute-done.7 = bf16[128,4096]{1,0:T(8,128)(2,1)S(1)} collective-permute-done((bf16[128,4096]{1,0:T(8,128)(2,1)S(1)}, bf16[128,4096]{1,0:T(8,128)(2,1)S(1)}, u32[]{:S(2)}, u32[]{:S(2)}) %collective-permute-start.7) | collective-permute-done | bytes 1048608 | tf_op jit(solution)/shard_map/ppermute | solution.py:25
  147.9 2.2 collective-permute-start.12
  150.0 2.1 collective-permute-start.14
  152.9 17.4 %collective-permute-done.13.refs_42_ = bf16[256,4096]{1,0:T(8,128)(2,1)S(1)} collective-permute-done((bf16[256,4096]{1,0:T(8,128)(2,1)S(1)}, bf16[256,4096]{1,0:T(8,128)(2,1)S(1)}, u32[]{:S(2)}, u32[]{:S(2)}) %collective-permute-start.13) | collective-permute-done | bytes 2097184 | tf_op jit(solution)/shard_map/ppermute | solution.py:25
  176.2 14.9 %collective-permute-done.14.refs_43_ = bf16[256,4096]{1,0:T(8,128)(2,1)S(1)} collective-permute-done((bf16[256,4096]{1,0:T(8,128)(2,1)S(1)}, bf16[256,4096]{1,0:T(8,128)(2,1)S(1)}, u32[]{:S(2)}, u32[]{:S(2)}) %collective-permute-start.14) | collective-permute-done | bytes 2097184 | tf_op jit(solution)/shard_map/ppermute | solution.py:25
  194.1 3.1 %shard_map.58 = (f32[2,256]{1,0:T(2,128)S(1)}, f32[1,256]{1,0:T(1,128)}) custom-call(s32[4]{0:T(128)S(1)} %add_convert_fusion.place.refs_0_, s32[1,256]{1,0:T(1,128)S(1)} %bitcast.94, f32[256,256]{1,0:T(8,128)S(1)} %copy.30.refs_0_.refs_2_, f32[256,256]{1,0:T(8,128)S(1)} %copy.31.refs_1_.refs_3_, f32[256,256]{1,0:T(8,128)S(1)} %copy.32.refs_2_.refs_4_, ...), custom_call_target="tpu_custom_call" | custom-call | bytes 4718592 | tf_op jit(solution)/shard_map/pallas_call | solution.py:279
  197.2 7.1 %collective-permute-start.17 = (f32[2,256]{1,0:T(2,128)S(1)}, f32[2,256]{1,0:T(2,128)S(1)}, u32[]{:S(2)}, u32[]{:S(2)}) collective-permute-start(f32[2,256]{1,0:T(2,128)S(1)} %get-tuple-element.32.refs_26_), channel_id=1, source_target_pairs={{0,254},{1,255},{2,0},{3,1},{4,2},{5,3},{6,4},{7,5},{8,6},{9,7},{1... | collective-permute-start | bytes 6152 | tf_op jit(solution)/shard_map/ppermute | solution.py:25
  204.3 2.7 %collective-permute-start.16 = (f32[2,256]{1,0:T(2,128)S(1)}, f32[2,256]{1,0:T(2,128)S(1)}, u32[]{:S(2)}, u32[]{:S(2)}) collective-permute-start(f32[2,256]{1,0:T(2,128)S(1)} %get-tuple-element.32.refs_26_), channel_id=1, source_target_pairs={{0,1},{1,2},{2,3},{3,4},{4,5},{5,6},{6,7},{7,8},{8,9},{9,10},{10,1... | collective-permute-start | bytes 6152 | tf_op jit(solution)/shard_map/ppermute | solution.py:25
  207.0 4.5 %collective-permute-start.15 = (f32[2,256]{1,0:T(2,128)S(1)}, f32[2,256]{1,0:T(2,128)S(1)}, u32[]{:S(2)}, u32[]{:S(2)}) collective-permute-start(f32[2,256]{1,0:T(2,128)S(1)} %get-tuple-element.32.refs_26_), channel_id=1, source_target_pairs={{0,255},{1,0},{2,1},{3,2},{4,3},{5,4},{6,5},{7,6},{8,7},{9,8},{10,... | collective-permute-start | bytes 6152 | tf_op jit(solution)/shard_map/ppermute | solution.py:25
  212.8 19.7 %shard_map.59 = (f32[256,4096]{1,0:T(8,128)}, f32[256,4096]{1,0:T(8,128)}) custom-call(s32[4]{0:T(128)S(1)} %add_convert_fusion.place.refs_0_, s32[1,256]{1,0:T(1,128)S(1)} %bitcast.95, f32[256,256]{1,0:T(8,128)S(1)} %copy.30.refs_0_.refs_2_, f32[256,256]{1,0:T(8,128)S(1)} %copy.31.refs_1_.refs_3_, f32[256,256]{1,0:T(8,128)S(1)} %copy.32.refs_2_.refs_4_, ...), custom_call_target="tpu_custom_call" | custom-call | flops 8589934592 | bytes 29360128 | tf_op jit(solution)/shard_map/pallas_call | solution.py:304
  (71 shorter events, 29.6 us)
Async XLA Ops:
  0.6 68.3 %collective-permute-start.3 = (bf16[256,4096]{1,0:T(8,128)(2,1)}, bf16[256,4096]{1,0:T(8,128)(2,1)}, u32[]{:S(2)}, u32[]{:S(2)}) collective-permute-start(bf16[256,4096]{1,0:T(8,128)(2,1)} %refs_31_.1), channel_id=1, source_target_pairs={{0,129},{1,128},{2,131},{3,130},{4,133},{5,132},{6,135},{7,134},{8... | collective-permute-start | bytes 6291464 | tf_op jit(solution)/shard_map/ppermute | solution.py:25
  2.0 71.1 %collective-permute-start.4 = (bf16[256,4096]{1,0:T(8,128)(2,1)}, bf16[256,4096]{1,0:T(8,128)(2,1)}, u32[]{:S(2)}, u32[]{:S(2)}) collective-permute-start(bf16[256,4096]{1,0:T(8,128)(2,1)} %refs_32_.1), channel_id=1, source_target_pairs={{0,128},{1,129},{2,130},{3,131},{4,132},{5,133},{6,134},{7,135},{8... | collective-permute-start | bytes 6291464 | tf_op jit(solution)/shard_map/ppermute | solution.py:25
  2.7 72.4 %collective-permute-start.2 = (bf16[256,4096]{1,0:T(8,128)(2,1)}, bf16[256,4096]{1,0:T(8,128)(2,1)}, u32[]{:S(2)}, u32[]{:S(2)}) collective-permute-start(bf16[256,4096]{1,0:T(8,128)(2,1)} %refs_31_.1), channel_id=1, source_target_pairs={{0,255},{127,128},{128,127},{255,0}} | collective-permute-start | bytes 6291464 | tf_op jit(solution)/shard_map/ppermute | solution.py:25
  13.5 61.6 %collective-permute-start.1 = (bf16[256,4096]{1,0:T(8,128)(2,1)}, bf16[256,4096]{1,0:T(8,128)(2,1)}, u32[]{:S(2)}, u32[]{:S(2)}) collective-permute-start(bf16[256,4096]{1,0:T(8,128)(2,1)} %refs_32_.1), channel_id=1, source_target_pairs={{0,254},{1,255},{2,0},{3,1},{4,2},{5,3},{6,4},{7,5},{8,6},{9,7},{1... | collective-permute-start | bytes 6291464 | tf_op jit(solution)/shard_map/ppermute | solution.py:25
  13.6 61.5 %collective-permute-start = (bf16[256,4096]{1,0:T(8,128)(2,1)}, bf16[256,4096]{1,0:T(8,128)(2,1)}, u32[]{:S(2)}, u32[]{:S(2)}) collective-permute-start(bf16[256,4096]{1,0:T(8,128)(2,1)} %refs_32_.1), channel_id=1, source_target_pairs={{0,2},{1,3},{2,4},{3,5},{4,6},{5,7},{6,8},{7,9},{8,10},{9,11},{10,... | collective-permute-start | bytes 6291464 | tf_op jit(solution)/shard_map/ppermute | solution.py:25
  15.6 3.3 %copy-start = (bf16[256,4096]{1,0:T(8,128)(2,1)S(1)}, bf16[256,4096]{1,0:T(8,128)(2,1)}, u32[]{:S(2)}) copy-start(bf16[256,4096]{1,0:T(8,128)(2,1)} %refs_31_.1) | copy-start | bytes 6291460
  73.1 51.3 %collective-permute-start.10 = (bf16[256,4096]{1,0:T(8,128)(2,1)}, bf16[256,4096]{1,0:T(8,128)(2,1)S(1)}, u32[]{:S(2)}, u32[]{:S(2)}) collective-permute-start(bf16[256,4096]{1,0:T(8,128)(2,1)} %collective-permute-done.3), channel_id=1, source_target_pairs={{0,129},{1,128},{2,131},{3,130},{4,133},{5,132},{6,135},{7,134},{8... | collective-permute-start | bytes 6291464 | tf_op jit(solution)/shard_map/ppermute | solution.py:25
  73.1 47.6 %collective-permute-start.5 = (bf16[256,4096]{1,0:T(8,128)(2,1)}, bf16[256,4096]{1,0:T(8,128)(2,1)S(1)}, u32[]{:S(2)}, u32[]{:S(2)}) collective-permute-start(bf16[256,4096]{1,0:T(8,128)(2,1)} %collective-permute-done.4), channel_id=1, source_target_pairs={{0,128},{1,129},{2,130},{3,131},{4,132},{5,133},{6,134},{7,135},{8... | collective-permute-start | bytes 6291464 | tf_op jit(solution)/shard_map/ppermute | solution.py:25
  78.8 8.3 %copy-start.1 = (bf16[256,4096]{1,0:T(8,128)(2,1)S(1)}, bf16[256,4096]{1,0:T(8,128)(2,1)}, u32[]{:S(2)}) copy-start(bf16[256,4096]{1,0:T(8,128)(2,1)} %refs_32_.1) | copy-start | bytes 6291460
  82.0 46.1 %collective-permute-start.9 = (bf16[256,4096]{1,0:T(8,128)(2,1)S(1)}, bf16[256,4096]{1,0:T(8,128)(2,1)S(1)}, u32[]{:S(2)}, u32[]{:S(2)}) collective-permute-start(bf16[256,4096]{1,0:T(8,128)(2,1)S(1)} %copy-done), channel_id=1, source_target_pairs={{0,2},{1,3},{2,4},{3,5},{4,6},{5,7},{6,8},{7,9},{8,10},{9,11},{10,... | collective-permute-start | bytes 6291464 | tf_op jit(solution)/shard_map/ppermute | solution.py:25
  82.0 46.1 %collective-permute-start.8 = (bf16[256,4096]{1,0:T(8,128)(2,1)S(1)}, bf16[256,4096]{1,0:T(8,128)(2,1)S(1)}, u32[]{:S(2)}, u32[]{:S(2)}) collective-permute-start(bf16[256,4096]{1,0:T(8,128)(2,1)S(1)} %copy-done), channel_id=1, source_target_pairs={{0,126},{1,127},{2,0},{3,1},{4,2},{5,3},{6,4},{7,5},{8,6},{9,7},{1... | collective-permute-start | bytes 6291464 | tf_op jit(solution)/shard_map/ppermute | solution.py:25
  120.7 3.7 %copy-start.8 = (bf16[256,4096]{1,0:T(8,128)(2,1)}, bf16[256,4096]{1,0:T(8,128)(2,1)S(1)}, u32[]{:S(2)}) copy-start(bf16[256,4096]{1,0:T(8,128)(2,1)S(1)} %collective-permute-done.5.refs_38_) | copy-start | bytes 6291460
  120.8 22.9 %collective-permute-start.7 = (bf16[128,4096]{1,0:T(8,128)(2,1)S(1)}, bf16[128,4096]{1,0:T(8,128)(2,1)S(1)}, u32[]{:S(2)}, u32[]{:S(2)}) collective-permute-start(bf16[128,4096]{1,0:T(8,128)(2,1)S(1)} %get-tuple-element.35), channel_id=1, source_target_pairs={{0,129},{1,128},{2,131},{3,130},{4,133},{5,132},{6,135},{7,134},{8... | collective-permute-start | bytes 3145736 | tf_op jit(solution)/shard_map/ppermute | solution.py:25
  120.9 24.1 %collective-permute-start.6 = (bf16[128,4096]{1,0:T(8,128)(2,1)S(1)}, bf16[128,4096]{1,0:T(8,128)(2,1)S(1)}, u32[]{:S(2)}, u32[]{:S(2)}) collective-permute-start(bf16[128,4096]{1,0:T(8,128)(2,1)S(1)} %get-tuple-element.36), channel_id=1, source_target_pairs={{0,128},{1,129},{2,130},{3,131},{4,132},{5,133},{6,134},{7,135},{8... | collective-permute-start | bytes 3145736 | tf_op jit(solution)/shard_map/ppermute | solution.py:25
  124.4 45.9 %collective-permute-start.13 = (bf16[256,4096]{1,0:T(8,128)(2,1)S(1)}, bf16[256,4096]{1,0:T(8,128)(2,1)S(1)}, u32[]{:S(2)}, u32[]{:S(2)}) collective-permute-start(bf16[256,4096]{1,0:T(8,128)(2,1)S(1)} %collective-permute-done.10.refs_37_), channel_id=1, source_target_pairs={{0,2},{1,127},{2,4},{3,1},{4,6},{5,3},{6,8},{7,5},{8,10},{9,7},{10... | collective-permute-start | bytes 6291464 | tf_op jit(solution)/shard_map/ppermute | solution.py:25
  128.1 24.1 %copy-start.4 = (bf16[256,4096]{1,0:T(8,128)(2,1)}, bf16[256,4096]{1,0:T(8,128)(2,1)S(1)}, u32[]{:S(2)}) copy-start(bf16[256,4096]{1,0:T(8,128)(2,1)S(1)} %collective-permute-done.9.refs_35_) | copy-start | bytes 6291460
  128.1 18.8 %copy-start.5 = (bf16[256,4096]{1,0:T(8,128)(2,1)}, bf16[256,4096]{1,0:T(8,128)(2,1)S(1)}, u32[]{:S(2)}) copy-start(bf16[256,4096]{1,0:T(8,128)(2,1)S(1)} %collective-permute-done.8.refs_33_) | copy-start | bytes 6291460
  145.0 28.3 %collective-permute-start.11 = (bf16[128,4096]{1,0:T(8,128)(2,1)S(1)}, bf16[128,4096]{1,0:T(8,128)(2,1)S(1)}, u32[]{:S(2)}, u32[]{:S(2)}) collective-permute-start(bf16[128,4096]{1,0:T(8,128)(2,1)S(1)} %collective-permute-done.6), channel_id=1, source_target_pairs={{0,128},{1,129},{2,130},{3,131},{4,132},{5,133},{6,134},{7,135},{8... | collective-permute-start | bytes 3145736 | tf_op jit(solution)/shard_map/ppermute | solution.py:25
  147.9 26.9 %collective-permute-start.12 = (bf16[128,4096]{1,0:T(8,128)(2,1)S(1)}, bf16[128,4096]{1,0:T(8,128)(2,1)S(1)}, u32[]{:S(2)}, u32[]{:S(2)}) collective-permute-start(bf16[128,4096]{1,0:T(8,128)(2,1)S(1)} %collective-permute-done.7), channel_id=1, source_target_pairs={{0,129},{1,128},{2,131},{3,130},{4,133},{5,132},{6,135},{7,134},{8... | collective-permute-start | bytes 3145736 | tf_op jit(solution)/shard_map/ppermute | solution.py:25
  150.0 41.1 %collective-permute-start.14 = (bf16[256,4096]{1,0:T(8,128)(2,1)S(1)}, bf16[256,4096]{1,0:T(8,128)(2,1)S(1)}, u32[]{:S(2)}, u32[]{:S(2)}) collective-permute-start(bf16[256,4096]{1,0:T(8,128)(2,1)S(1)} %broadcast_select_fusion), channel_id=1, source_target_pairs={{0,128},{1,129},{126,254},{127,255},{128,0},{129,1},{254,126},{255... | collective-permute-start | bytes 6291464 | tf_op jit(solution)/shard_map/ppermute | solution.py:25
  197.2 14.3 %collective-permute-start.18 = (f32[2,256]{1,0:T(2,128)S(1)}, f32[2,256]{1,0:T(2,128)S(1)}, u32[]{:S(2)}, u32[]{:S(2)}) collective-permute-start(f32[2,256]{1,0:T(2,128)S(1)} %get-tuple-element.32.refs_26_), channel_id=1, source_target_pairs={{0,2},{1,3},{2,4},{3,5},{4,6},{5,7},{6,8},{7,9},{8,10},{9,11},{10,... | collective-permute-start | bytes 6152 | tf_op jit(solution)/shard_map/ppermute | solution.py:25
  197.2 14.3 %collective-permute-start.17 = (f32[2,256]{1,0:T(2,128)S(1)}, f32[2,256]{1,0:T(2,128)S(1)}, u32[]{:S(2)}, u32[]{:S(2)}) collective-permute-start(f32[2,256]{1,0:T(2,128)S(1)} %get-tuple-element.32.refs_26_), channel_id=1, source_target_pairs={{0,254},{1,255},{2,0},{3,1},{4,2},{5,3},{6,4},{7,5},{8,6},{9,7},{1... | collective-permute-start | bytes 6152 | tf_op jit(solution)/shard_map/ppermute | solution.py:25
  204.3 8.4 %collective-permute-start.16 = (f32[2,256]{1,0:T(2,128)S(1)}, f32[2,256]{1,0:T(2,128)S(1)}, u32[]{:S(2)}, u32[]{:S(2)}) collective-permute-start(f32[2,256]{1,0:T(2,128)S(1)} %get-tuple-element.32.refs_26_), channel_id=1, source_target_pairs={{0,1},{1,2},{2,3},{3,4},{4,5},{5,6},{6,7},{7,8},{8,9},{9,10},{10,1... | collective-permute-start | bytes 6152 | tf_op jit(solution)/shard_map/ppermute | solution.py:25
  207.0 5.8 %collective-permute-start.15 = (f32[2,256]{1,0:T(2,128)S(1)}, f32[2,256]{1,0:T(2,128)S(1)}, u32[]{:S(2)}, u32[]{:S(2)}) collective-permute-start(f32[2,256]{1,0:T(2,128)S(1)} %get-tuple-element.32.refs_26_), channel_id=1, source_target_pairs={{0,255},{1,0},{2,1},{3,2},{4,3},{5,4},{6,5},{7,6},{8,7},{9,8},{10,... | collective-permute-start | bytes 6152 | tf_op jit(solution)/shard_map/ppermute | solution.py:25
  (6 other events, 10.6 us)

commit v2 on v1

v2 whole, which is shorter than its diff:
```python
import math

import jax
import jax.numpy as jnp
from jax import lax
from jax.experimental import pallas as pl
from jax.experimental.pallas import tpu as pltpu
from jax.sharding import PartitionSpec as P

AXES = ("dp", "inner")
NEGATIVE = -1e30
CHUNK = 1024
VMEM_LIMIT = 46 * 1024 * 1024
SMALL_LIMIT = 16 * 1024 * 1024


def contract(left_rows, right_rows):
    return lax.dot_general(
        left_rows, right_rows, (((1,), (1,)), ((), ())), preferred_element_type=jnp.float32
    )


def sent(value, target, senders=None):
    count = lax.axis_size(AXES)
    senders = range(count) if senders is None else senders
    return lax.ppermute(value, AXES, [(i, target(i) % count) for i in senders])


def down_hop(half):
    return lambda i: i - half if i >= half else (i ^ 1) + half


def up_hop(half):
    return lambda i: (i - half) ^ 1 if i >= half else i + half


def as_columns(row):
    size = row.shape[1]
    return jnp.broadcast_to(row, (size, size)).T


def peak_and_sum(tiles):
    largest = tiles[0]
    for tile in tiles[1:]:
        largest = jnp.maximum(largest, tile)
    largest = jnp.max(largest, axis=1, keepdims=True)
    total = jnp.exp(tiles[0] - largest)
    for tile in tiles[1:]:
        total = total + jnp.exp(tile - largest)
    return largest, jnp.sum(total, axis=1, keepdims=True)


def early_kernel(scale, place, pos, *refs):
    qq, qd, dq, dd, qd_n2, dd_n2, dd_p2 = refs[:7]
    own_q, own_d, q_n2, q_p2, q_pair, d_pair = refs[7:13]
    qq_n2, dq_p2, qq_p2, qq_pair, cross_pair, dd_pair = refs[13:19]
    q_max, q_sum, d_max, d_sum, positive = refs[19:]
    even, first, last = [place[k] == 1 for k in range(3)]
    qq_pair[...] = scale * contract(own_q[...], q_pair[...])
    dd_pair[...] = scale * contract(own_d[...], d_pair[...])
    qq_n2[...] = scale * contract(own_q[...], q_n2[...])
    qq_p2[...] = scale * contract(own_q[...], q_p2[...])
    dq_p2[...] = scale * contract(own_d[...], q_p2[...])

    @pl.when(even)
    def _():
        cross_pair[...] = scale * contract(own_q[...], d_pair[...])

    @pl.when(jnp.logical_not(even))
    def _():
        cross_pair[...] = scale * contract(own_d[...], q_pair[...])

    cross = cross_pair[...]
    q_tiles = [
        qd[...],
        qq[...],
        qd_n2[...],
        qq_pair[...],
        jnp.where(last, NEGATIVE, qq_n2[...]),
        jnp.where(first, NEGATIVE, qq_p2[...]),
        jnp.where(even, cross, NEGATIVE),
    ]
    d_tiles = [
        dd[...],
        dq[...],
        dd_n2[...],
        dd_p2[...],
        dd_pair[...],
        jnp.where(first, NEGATIVE, dq_p2[...]),
        jnp.where(even, NEGATIVE, cross),
    ]
    for tiles, out_max, out_sum in ((q_tiles, q_max, q_sum), (d_tiles, d_max, d_sum)):
        largest, total = peak_and_sum(tiles)
        out_max[...] = jnp.broadcast_to(largest, out_max.shape)
        out_sum[...] = jnp.broadcast_to(total, out_sum.shape)
    doc = lax.broadcasted_iota(jnp.int32, dq.shape, 0)
    positive[...] = jnp.sum(jnp.where(doc == pos[...], dq[...], 0.0), axis=0, keepdims=True)


def lse_kernel(scale, place, qq_edge, dq_edge, q_max, q_sum, d_max, d_sum, positive, *refs):
    own_q, own_d, q_diag, d_low, d_high, q_swap = refs[:6]
    qq_diag, cross_diag, dd_diag, qq_swap, dq_swap, lse, row_terms = refs[6:]
    even, first, last, edge = [place[k] == 1 for k in range(4)]
    half = d_low.shape[1]

    def with_documents(own):
        return scale * (contract(own[:, :half], d_low[...]) + contract(own[:, half:], d_high[...]))

    qq_diag[...] = jnp.where(edge, qq_edge[...], scale * contract(own_q[...], q_diag[...]))
    dd_diag[...] = with_documents(own_d)

    @pl.when(even)
    def _():
        cross_diag[...] = jnp.where(edge, dq_edge[...], scale * contract(own_d[...], q_diag[...]))

    @pl.when(jnp.logical_not(even))
    def _():
        cross_diag[...] = with_documents(own_q)

    @pl.when(first | last)
    def _():
        qq_swap[...] = scale * contract(own_q[...], q_swap[...])
        dq_swap[...] = scale * contract(own_d[...], q_swap[...])

    @pl.when(jnp.logical_not(first | last))
    def _():
        qq_swap[...] = jnp.full(qq_swap.shape, NEGATIVE, jnp.float32)
        dq_swap[...] = jnp.full(dq_swap.shape, NEGATIVE, jnp.float32)

    def finished(early_max, early_sum, tiles):
        largest = early_max[:, :1]
        for tile in tiles:
            largest = jnp.maximum(largest, jnp.max(tile, axis=1, keepdims=True))
        total = jnp.exp(tiles[0] - largest)
        for tile in tiles[1:]:
            total = total + jnp.exp(tile - largest)
        total = jnp.sum(total, axis=1, keepdims=True)
        total = total + early_sum[:, :1] * jnp.exp(early_max[:, :1] - largest)
        return jnp.broadcast_to(largest + jnp.log(total), tiles[0].shape).T[:1]

    cross = cross_diag[...]
    q_late = [qq_diag[...], qq_swap[...], jnp.where(even, NEGATIVE, cross)]
    d_late = [dd_diag[...], jnp.where(first, dq_swap[...], NEGATIVE), jnp.where(even, cross, NEGATIVE)]
    q_row = finished(q_max, q_sum, q_late)
    d_row = finished(d_max, d_sum, d_late)
    lse[0:1, :] = q_row
    lse[1:2, :] = d_row
    row_terms[...] = q_row + d_row - 2.0 * positive[...]


TILES = 18


def grad_kernel(factor, place, pos, *refs):
    tiles, refs = refs[:TILES], refs[TILES:]
    lse, lse_n1, lse_p1, lse_n2, lse_p2 = refs[:5]
    own_q, own_d, q_n2, d_n2, q_p2, d_p2, q_pair, d_pair = refs[5:13]
    q_edge, d_low, d_high, q_diag, q_swap = refs[13:18]
    grad_q, grad_d, coef_q, coef_d, rows, arrived = refs[18:]
    step = pl.program_id(0)
    size = grad_q.shape[0]
    width = own_q.shape[1]
    chunk = rows.shape[2]
    parts = width // chunk
    even, first, last, edge = [place[k] == 1 for k in range(4)]

    def bring(part):
        def one(source, slot, column=part * chunk):
            start = slot * size if isinstance(slot, int) else pl.multiple_of(slot * size, size)
            pltpu.make_async_copy(
                source.at[:, pl.ds(column, chunk)],
                rows.at[part, pl.ds(start, size), :],
                arrived.at[part],
            ).start()

        def either(taken, yes, no, slot):
            pl.when(taken)(lambda: one(yes, slot))
            pl.when(jnp.logical_not(taken))(lambda: one(no, slot))

        one(own_d, 2)
        one(own_q, 3)
        one(d_n2, 4)
        one(d_p2, 8)
        one(q_pair, jnp.where(even, 1, 7))
        one(d_pair, jnp.where(even, 6, 9))
        source = d_low if part < parts // 2 else d_high
        one(source, jnp.where(even, 9, 6), part % (parts // 2) * chunk)
        either(edge, q_edge, q_diag, jnp.where(even, 7, 1))
        either(last, q_swap, q_n2, 0)
        either(first, q_swap, q_p2, 5)

    @pl.when(step == 0)
    def _():
        bring(0)
        bring(1)
        qq, qd, dq, dd, qd_n2, dd_n2, dd_p2 = tiles[:7]
        qq_n2, dq_p2, qq_p2, qq_pair, cross_pair, dd_pair = tiles[7:13]
        qq_diag, cross_diag, dd_diag, qq_swap, dq_swap = tiles[13:]
        q_col = as_columns(lse[0:1, :])
        d_col = as_columns(lse[1:2, :])
        lane = lax.broadcasted_iota(jnp.int32, (size, size), 1)
        sublane = lax.broadcasted_iota(jnp.int32, (size, size), 0)
        pos_col = as_columns(pos[...])

        def put(target, slot, tile, column, row, taken=None):
            value = jnp.exp(tile - column) + jnp.exp(tile - row)
            if taken is not None:
                value = value - jnp.where(taken, 2.0, 0.0)
            target[:, slot * size : (slot + 1) * size] = value.astype(jnp.bfloat16)

        def q_of(ref):
            return ref[0:1, :]

        def d_of(ref):
            return ref[1:2, :]

        def pick(taken, yes, no):
            return jnp.where(taken, yes[...], no[...])

        put(coef_q, 0, pick(last, qq_swap, qq_n2), q_col, q_of(lse_n2))
        put(coef_q, 1, pick(even, qq_pair, qq_diag), q_col, q_of(lse_n1))
        put(coef_q, 2, qd[...], q_col, d_of(lse), pos_col == lane)
        put(coef_q, 3, qq[...], q_col, q_of(lse))
        put(coef_q, 4, qd_n2[...], q_col, d_of(lse_n2))
        put(coef_q, 5, pick(first, qq_swap, qq_p2), q_col, q_of(lse_p2))
        put(coef_q, 6, pick(even, cross_pair, cross_diag), q_col, d_of(lse_n1))
        put(coef_q, 7, pick(even, qq_diag, qq_pair), q_col, q_of(lse_p1))
        put(coef_d, 0, dd[...], d_col, d_of(lse))
        put(coef_d, 1, dq[...], d_col, q_of(lse), pos[...] == sublane)
        put(coef_d, 2, dd_n2[...], d_col, d_of(lse_n2))
        put(coef_d, 3, pick(first, dq_swap, dq_p2), d_col, q_of(lse_p2))
        put(coef_d, 4, pick(even, dd_pair, dd_diag), d_col, d_of(lse_n1))
        put(coef_d, 5, pick(even, cross_diag, cross_pair), d_col, q_of(lse_p1))
        put(coef_d, 6, dd_p2[...], d_col, d_of(lse_p2))
        put(coef_d, 7, pick(even, dd_diag, dd_pair), d_col, d_of(lse_p1))
        for part in range(2, parts):
            bring(part)

    pltpu.make_async_copy(rows.at[step], rows.at[step], arrived.at[step]).wait()
    depth = coef_q.shape[1]
    grad_q[...] = factor * jnp.dot(
        coef_q[...], rows[step, 0:depth, :], preferred_element_type=jnp.float32
    )
    grad_d[...] = factor * jnp.dot(
        coef_d[...], rows[step, 2 * size :, :], preferred_element_type=jnp.float32
    )


def per_device(queries, documents, positives):
    size, width = queries.shape
    count = lax.axis_size(AXES)
    scale = 2.0 / math.sqrt(width)
    factor = scale / (2.0 * size * count)
    own_block = lax.axis_index("dp") * lax.axis_size("inner") + lax.axis_index("inner")
    half, inner = count // 2, lax.axis_size("inner")
    within = own_block % half
    is_even = own_block % 2 == 0
    first, last = within < 2, within >= half - 2
    place = jnp.stack(
        [is_even, first, last, (within == 0) | (within == half - 1)]
    ).astype(jnp.int32)
    pos = (positives - own_block * size).reshape(1, size)
    index = jnp.arange(size)
    same_row = index[:, None] == index[None, :]
    down, up = down_hop(half), up_hop(half)
    barrier = lax.optimization_barrier

    def tile(left, right):
        return scale * contract(left, right)

    def masked(tile):
        return jnp.where(same_row, NEGATIVE, tile)

    q_down = sent(queries, down)
    d_up = sent(documents, up)
    d_p2 = sent(documents, lambda i: i + 2)
    d_n2 = sent(documents, lambda i: i - 2)
    q_edge = sent(
        queries,
        lambda i: i - 1 if i % half == 0 else i + 1,
        [0, half - 1, half, count - 1],
    )
    own_tiles = [
        masked(tile(queries, queries)),
        tile(queries, documents),
        tile(documents, queries),
        masked(tile(documents, documents)),
    ]
    q_down, d_up, own_tiles = barrier((q_down, d_up, own_tiles))
    q_pair = sent(q_down, down)
    d_pair = sent(d_up, up)
    q_own, d_p2, d_n2, q_edge, q_down, d_up = barrier((queries, d_p2, d_n2, q_edge, q_down, d_up))
    crossing = [i for i in range(count) if i % half < 2 or i % half >= half - 2]
    q_swap = sent(
        q_own, lambda i: i + half + (inner - 2 if i % half < 2 else 2 - inner), crossing
    )
    q_p2 = sent(q_own, lambda i: i + 2, [i for i in range(count) if i % half < half - 2])
    q_n2 = sent(q_own, lambda i: i - 2, [i for i in range(count) if i % half >= 2])
    far_tiles = [
        tile(queries, d_n2),
        tile(documents, d_n2),
        tile(documents, d_p2),
        tile(queries, q_edge),
        tile(documents, q_edge),
    ]
    cut = width // 2
    d_low = jnp.where(is_even, d_n2[:, :cut], d_p2[:, :cut])
    d_high = jnp.where(is_even, d_n2[:, cut:], d_p2[:, cut:])
    d_low, d_high, q_pair, d_pair, far_tiles = barrier((d_low, d_high, q_pair, d_pair, far_tiles))
    d_low = sent(d_low, up)
    d_high = sent(d_high, down)
    q_diag = sent(
        q_pair,
        lambda i: i - 2 if i % 2 else i + 2,
        [i for i in range(count) if i % half != 1 and i % half != half - 2],
    )
    d_low, d_high, q_swap, q_pair, d_pair, q_p2, q_n2 = barrier(
        (d_low, d_high, q_swap, q_pair, d_pair, q_p2, q_n2)
    )
    d_low = sent(d_low, up)
    d_high = sent(d_high, down)
    q_swap = sent(
        q_swap,
        lambda i: i + half - inner if i % half < inner else i - half + inner,
        [i for i in range(count) if i % half in (inner - 2, inner - 1, half - inner, half - inner + 1)],
    )

    in_vmem = pl.BlockSpec(memory_space=pltpu.VMEM)
    in_smem = pl.BlockSpec(memory_space=pltpu.SMEM)
    anywhere = pl.BlockSpec(memory_space=pl.ANY)
    column = jax.ShapeDtypeStruct((size, 128), jnp.float32)
    row = jax.ShapeDtypeStruct((1, size), jnp.float32)
    square = jax.ShapeDtypeStruct((size, size), jnp.float32)

    def early_tiles(*refs):
        early_kernel(scale, *refs)

    *early, q_max, q_sum, d_max, d_sum, positive = pl.pallas_call(
        early_tiles,
        out_shape=(square,) * 6 + (column,) * 4 + (row,),
        in_specs=[in_smem] + [in_vmem] * 14,
        out_specs=(in_vmem,) * 11,
        compiler_params=pltpu.CompilerParams(vmem_limit_bytes=SMALL_LIMIT),
        cost_estimate=pl.CostEstimate(
            flops=12 * size * size * width,
            bytes_accessed=12 * size * width,
            transcendentals=14 * size * size,
        ),
    )(
        place,
        pos,
        *own_tiles,
        *far_tiles[:3],
        queries,
        documents,
        q_n2,
        q_p2,
        q_pair,
        d_pair,
    )

    def last_tiles(*refs):
        lse_kernel(scale, *refs)

    *late, lse, row_terms = pl.pallas_call(
        last_tiles,
        out_shape=(square,) * 5 + (jax.ShapeDtypeStruct((2, size), jnp.float32), row),
        in_specs=[in_smem] + [in_vmem] * 13,
        out_specs=(in_vmem,) * 7,
        compiler_params=pltpu.CompilerParams(vmem_limit_bytes=SMALL_LIMIT),
        cost_estimate=pl.CostEstimate(
            flops=6 * size * size * width,
            bytes_accessed=8 * size * width,
            transcendentals=6 * size * size,
        ),
    )(
        place,
        far_tiles[3],
        far_tiles[4],
        q_max,
        q_sum,
        d_max,
        d_sum,
        positive,
        queries,
        documents,
        q_diag,
        d_low,
        d_high,
        q_swap,
    )
    tiles = [*own_tiles, *far_tiles[:3], *early, *late]
    lse_n1 = sent(lse, lambda i: i - 1)
    lse_p1 = sent(lse, lambda i: i + 1)
    lse_n2 = sent(lse, lambda i: i - 2)
    lse_p2 = sent(lse, lambda i: i + 2)
    sources = [queries, documents, q_n2, d_n2, q_p2, d_p2, q_pair, d_pair]
    sources += [q_edge, d_low, d_high, q_diag, q_swap]
    parts = width // CHUNK

    def kernel(*refs):
        grad_kernel(factor, *refs)

    grad_block = pl.BlockSpec((size, CHUNK), lambda step: (0, step))
    grad_q, grad_d = pl.pallas_call(
        kernel,
        grid=(parts,),
        out_shape=(jax.ShapeDtypeStruct((size, width), jnp.float32),) * 2,
        in_specs=[in_smem] + [in_vmem] * (6 + TILES) + [anywhere] * len(sources),
        out_specs=(grad_block, grad_block),
        scratch_shapes=[
            pltpu.VMEM((size, 8 * size), jnp.bfloat16),
            pltpu.VMEM((size, 8 * size), jnp.bfloat16),
            pltpu.VMEM((parts, 10 * size, CHUNK), jnp.bfloat16),
            pltpu.SemaphoreType.DMA((parts,)),
        ],
        compiler_params=pltpu.CompilerParams(vmem_limit_bytes=VMEM_LIMIT),
        cost_estimate=pl.CostEstimate(
            flops=2 * 16 * size * size * width,
            bytes_accessed=(20 + 8) * size * width,
            transcendentals=32 * size * size,
        ),
    )(place, pos, *tiles, lse, lse_n1, lse_p1, lse_n2, lse_p2, *sources)
    return (row_terms.reshape(size), grad_q, grad_d)


def solution(mesh):
    placed = (P(AXES, None), P(AXES, None), P(AXES))
    return jax.shard_map(
        per_device,
        mesh=mesh,
        in_specs=placed,
        out_specs=(P(AXES), P(AXES, None), P(AXES, None)),
        check_vma=False,
    )
```

time: 234 us -> 225 us (0.962)
  waiting for transfers between devices: 124 us -> 106 us
  matrix products: 37.6 us -> 20.5 us
  local copies, waits for them, and re-layouts: 0.69 us -> 14.2 us
  starting transfers between devices: 43.9 us -> 52 us
  Pallas kernels: 22.8 us -> 28.6 us
    ppermute x19 -> x20, waiting for transfers between devices: 124 us -> 106 us  [sent(): return lax.ppermute(value, AXES, [(i, target(i) % count) for i in senders])]
    dot_general x24 -> x9, matrix products: 37.6 us -> 20.5 us  [contract(): lax.dot_general(left_rows, right_rows, (((1,), (1,)), ((), ())), preferre...]
    unnamed x22 -> x34, local copies, waits for them, and re-layouts: 0.04 us -> 12.7 us
    pallas_call x1 -> x2, Pallas kernels: 3.1 us -> 13.9 us  [the longest x1 7.72 us: per_device(): pl.pallas_call(last_tiles, out_shape=(square,) * 5 + (jax.ShapeDtypeStruc...]
    ppermute x19 -> x20, starting transfers between devices: 43.9 us -> 52 us  [sent(): return lax.ppermute(value, AXES, [(i, target(i) % count) for i in senders])]
    pallas_call x1, Pallas kernels: 19.7 us -> 14.7 us  [per_device(): pl.pallas_call(kernel, grid=(parts,), out_shape=(jax.ShapeDtypeStruct((si...]
  transfers between devices with their start and end apart: 19 -> 20, of which waited for: 9 -> 9; matrix products, arithmetic and copies ran while one was open for 16% -> 11% of each run, Pallas kernels for 0% -> 3%
where the time goes in v2:
time: 225 us; the launch traced here: 224 us
  waiting for transfers between devices  106 us (47%)
  starting transfers between devices  52 us (23%)
  Pallas kernels  28.6 us (13%)
  matrix products  20.5 us (9%)
  local copies, waits for them, and re-layouts  14.2 us (6%)
  other arithmetic  2.47 us (1%)
    ppermute x20, waiting for transfers between devices, sent(): return lax.ppermute(value, AXES, [(i, target(i) % count) for i in senders])  106 us
    ppermute x20, starting transfers between devices, sent(): return lax.ppermute(value, AXES, [(i, target(i) % count) for i in senders])  52 us
    dot_general x9, matrix products, contract(): lax.dot_general(left_rows, right_rows, (((1,), (1,)), ((), ())), preferre...  20.5 us
    pallas_call x1, Pallas kernels, per_device(): pl.pallas_call(kernel, grid=(parts,), out_shape=(jax.ShapeDtypeStruct((si...  14.7 us
    unnamed x34, local copies, waits for them, and re-layouts  12.7 us
    pallas_call x1, Pallas kernels, per_device(): pl.pallas_call(last_tiles, out_shape=(square,) * 5 + (jax.ShapeDtypeStruc...  7.72 us
    pallas_call x1, Pallas kernels, per_device(): pl.pallas_call(early_tiles, out_shape=(square,) * 6 + (column,) * 4 + (ro...  6.19 us
  transfers between devices with their start and end apart: 20, of which 9 were waited for; matrix products, arithmetic and copies ran while one was open for 11% of the time, Pallas kernels for 3%

profile of v2, /device:TPU:0, one launch (start us, length us, event | category | flops | bytes accessed | tf_op | source)
XLA Modules:
  0.0 224.5 jit_solution(17069225381886254971)
XLA Ops:
  2.7 10.8 %collective-permute-start.2 = (bf16[256,4096]{1,0:T(8,128)(2,1)}, bf16[256,4096]{1,0:T(8,128)(2,1)}, u32[]{:S(2)}, u32[]{:S(2)}) collective-permute-start(bf16[256,4096]{1,0:T(8,128)(2,1)} %refs_25_.1), channel_id=1, source_target_pairs={{0,255},{127,128},{128,127},{255,0}} | collective-permute-start | bytes 6291464 | tf_op jit(solution)/shard_map/ppermute | solution.py:26
  15.6 3.1 %convolution_multiply_fusion.6 = f32[256,256]{0,1:T(8,128)S(1)} fusion(bf16[256,4096]{1,0:T(8,128)(2,1)} %refs_26_.1, bf16[256,4096]{1,0:T(8,128)(2,1)} %refs_25_.1), kind=kOutput, calls=%fused_computation.12 | convolution fusion | flops 536936448 | bytes 4456448 | tf_op jit(solution)/shard_map/dot_general | solution.py:18
  22.0 46.9 %collective-permute-done.3 = bf16[256,4096]{1,0:T(8,128)(2,1)} collective-permute-done((bf16[256,4096]{1,0:T(8,128)(2,1)}, bf16[256,4096]{1,0:T(8,128)(2,1)}, u32[]{:S(2)}, u32[]{:S(2)}) %collective-permute-start.3) | collective-permute-done | bytes 2097184 | tf_op jit(solution)/shard_map/ppermute | solution.py:26
  69.0 4.1 %collective-permute-done.4 = bf16[256,4096]{1,0:T(8,128)(2,1)} collective-permute-done((bf16[256,4096]{1,0:T(8,128)(2,1)}, bf16[256,4096]{1,0:T(8,128)(2,1)}, u32[]{:S(2)}, u32[]{:S(2)}) %collective-permute-start.4) | collective-permute-done | bytes 2097184 | tf_op jit(solution)/shard_map/ppermute | solution.py:26
  76.4 4.7 %collective-permute-start.10 = (bf16[256,4096]{1,0:T(8,128)(2,1)S(1)}, bf16[256,4096]{1,0:T(8,128)(2,1)S(1)}, u32[]{:S(2)}, u32[]{:S(2)}) collective-permute-start(bf16[256,4096]{1,0:T(8,128)(2,1)S(1)} %copy-done), channel_id=1, source_target_pairs={{0,2},{1,3},{2,4},{3,5},{4,6},{5,7},{6,8},{7,9},{8,10},{9,11},{10,... | collective-permute-start | bytes 6291464 | tf_op jit(solution)/shard_map/ppermute | solution.py:26
  81.1 2.7 %collective-permute-start.9 = (bf16[256,4096]{1,0:T(8,128)(2,1)S(1)}, bf16[256,4096]{1,0:T(8,128)(2,1)}, u32[]{:S(2)}, u32[]{:S(2)}) collective-permute-start(bf16[256,4096]{1,0:T(8,128)(2,1)S(1)} %copy-done), channel_id=1, source_target_pairs={{0,134},{1,135},{126,248},{127,249},{128,6},{129,7},{254,120},{255... | collective-permute-start | bytes 6291464 | tf_op jit(solution)/shard_map/ppermute | solution.py:26
  83.8 3.0 %fusion.refs_2_ = f32[256,256]{1,0:T(8,128)} fusion(bf16[256,4096]{1,0:T(8,128)(2,1)} %collective-permute-done.2.refs_33_, bf16[256,4096]{1,0:T(8,128)(2,1)S(1)} %copy-done.1), kind=kOutput, calls=%fused_computation.1 | convolution fusion | flops 536936448 | bytes 4456448 | tf_op jit(solution)/shard_map/dot_general | solution.py:18
  86.8 3.0 %fusion.1.refs_1_ = f32[256,256]{1,0:T(8,128)} fusion(bf16[256,4096]{1,0:T(8,128)(2,1)} %collective-permute-done.2.refs_33_, bf16[256,4096]{1,0:T(8,128)(2,1)S(1)} %copy-done), kind=kOutput, calls=%fused_computation.3 | convolution fusion | flops 536936448 | bytes 4456448 | tf_op jit(solution)/shard_map/dot_general | solution.py:18
  89.8 2.3 %fusion.3.refs_7_ = f32[256,256]{1,0:T(8,128)S(1)} fusion(bf16[256,4096]{1,0:T(8,128)(2,1)} %collective-permute-done.1.refs_28_, bf16[256,4096]{1,0:T(8,128)(2,1)S(1)} %copy-done.1), kind=kOutput, calls=%fused_computation.7 | convolution fusion | flops 536936448 | bytes 4456448 | tf_op jit(solution)/shard_map/dot_general | solution.py:18
  92.2 3.1 %fusion.4.refs_6_ = f32[256,256]{1,0:T(8,128)} fusion(bf16[256,4096]{1,0:T(8,128)(2,1)} %collective-permute-done.1.refs_28_, bf16[256,4096]{1,0:T(8,128)(2,1)S(1)} %copy-done), kind=kOutput, calls=%fused_computation.9 | convolution fusion | flops 536936448 | bytes 4456448 | tf_op jit(solution)/shard_map/dot_general | solution.py:18
  95.2 3.0 %fusion.2.refs_8_ = f32[256,256]{1,0:T(8,128)} fusion(bf16[256,4096]{1,0:T(8,128)(2,1)} %collective-permute-done.refs_30_, bf16[256,4096]{1,0:T(8,128)(2,1)S(1)} %copy-done.1), kind=kOutput, calls=%fused_computation.5 | convolution fusion | flops 536936448 | bytes 4456448 | tf_op jit(solution)/shard_map/dot_general | solution.py:18
  98.3 2.4 %slice_select_fusion = (bf16[256,2048]{1,0:T(8,128)(2,1)S(1)}, bf16[256,2048]{1,0:T(8,128)(2,1)S(1)}) fusion(bf16[256,4096]{1,0:T(8,128)(2,1)} %collective-permute-done.refs_30_, bf16[256,4096]{1,0:T(8,128)(2,1)} %collective-permute-done.1.refs_28_, pred[]{:T(512)} %eq.31), kind=kLoop, calls=%fused_computation.16 | loop fusion | flops 1048576 | bytes 6291457 | tf_op jit(solution)/shard_map/jit(_where)/select_n | solution.py:308
  100.7 18.9 %collective-permute-done.5.refs_13_.refs_31_ = bf16[256,4096]{1,0:T(8,128)(2,1)} collective-permute-done((bf16[256,4096]{1,0:T(8,128)(2,1)}, bf16[256,4096]{1,0:T(8,128)(2,1)}, u32[]{:S(2)}, u32[]{:S(2)}) %collective-permute-start.5) | collective-permute-done | bytes 2097184 | tf_op jit(solution)/shard_map/ppermute | solution.py:26
  122.6 2.7 %collective-permute-start.8 = (bf16[256,2048]{1,0:T(8,128)(2,1)S(1)}, bf16[256,2048]{1,0:T(8,128)(2,1)}, u32[]{:S(2)}, u32[]{:S(2)}) collective-permute-start(bf16[256,2048]{1,0:T(8,128)(2,1)S(1)} %get-tuple-element.64), channel_id=1, source_target_pairs={{0,129},{1,128},{2,131},{3,130},{4,133},{5,132},{6,135},{7,134},{8... | collective-permute-start | bytes 3145736 | tf_op jit(solution)/shard_map/ppermute | solution.py:26
  126.7 2.6 %collective-permute-start.12 = (bf16[256,4096]{1,0:T(8,128)(2,1)}, bf16[256,4096]{1,0:T(8,128)(2,1)}, u32[]{:S(2)}, u32[]{:S(2)}) collective-permute-start(bf16[256,4096]{1,0:T(8,128)(2,1)} %collective-permute-done.5.refs_13_.refs_31_), channel_id=1, source_target_pairs={{0,2},{2,4},{3,1},{4,6},{5,3},{6,8},{7,5},{8,10},{9,7},{10,12},{11... | collective-permute-start | bytes 6291464 | tf_op jit(solution)/shard_map/ppermute | solution.py:26
  130.6 15.6 %collective-permute-done.7 = bf16[256,2048]{1,0:T(8,128)(2,1)} collective-permute-done((bf16[256,2048]{1,0:T(8,128)(2,1)S(1)}, bf16[256,2048]{1,0:T(8,128)(2,1)}, u32[]{:S(2)}, u32[]{:S(2)}) %collective-permute-start.7) | collective-permute-done | bytes 1048608 | tf_op jit(solution)/shard_map/ppermute | solution.py:26
  147.5 6.0 %collective-permute-start.14 = (bf16[256,2048]{1,0:T(8,128)(2,1)}, bf16[256,2048]{1,0:T(8,128)(2,1)}, u32[]{:S(2)}, u32[]{:S(2)}) collective-permute-start(bf16[256,2048]{1,0:T(8,128)(2,1)} %collective-permute-done.8), channel_id=1, source_target_pairs={{0,129},{1,128},{2,131},{3,130},{4,133},{5,132},{6,135},{7,134},{8... | collective-permute-start | bytes 3145736 | tf_op jit(solution)/shard_map/ppermute | solution.py:26
  163.4 6.2 %shard_map.58 = (f32[256,256]{1,0:T(8,128)S(1)}, f32[256,256]{1,0:T(8,128)S(1)}, f32[256,256]{1,0:T(8,128)S(1)}, f32[256,256]{1,0:T(8,128)S(1)}, f32[256,256]{1,...) custom-call(s32[4]{0:T(128)S(1)} %add_convert_fusion.refs_0_, ...), custom_call_target="tpu_custom_call" | custom-call | flops 3221225472 | bytes 12582912 | tf_op jit(solution)/shard_map/pallas_call | solution.py:338
  171.4 4.1 %collective-permute-done.13.refs_11_.refs_34_ = bf16[256,2048]{1,0:T(8,128)(2,1)} collective-permute-done((bf16[256,2048]{1,0:T(8,128)(2,1)}, bf16[256,2048]{1,0:T(8,128)(2,1)}, u32[]{:S(2)}, u32[]{:S(2)}) %collective-permute-start.13) | collective-permute-done | bytes 1048608 | tf_op jit(solution)/shard_map/ppermute | solution.py:26
  175.5 11.9 %collective-permute-done.15.refs_13_.refs_37_ = bf16[256,4096]{1,0:T(8,128)(2,1)} collective-permute-done((bf16[256,4096]{1,0:T(8,128)(2,1)}, bf16[256,4096]{1,0:T(8,128)(2,1)}, u32[]{:S(2)}, u32[]{:S(2)}) %collective-permute-start.15) | collective-permute-done | bytes 2097184 | tf_op jit(solution)/shard_map/ppermute | solution.py:26
  187.4 7.7 %shard_map.59 = (f32[256,256]{1,0:T(8,128)S(1)}, f32[256,256]{1,0:T(8,128)S(1)}, f32[256,256]{1,0:T(8,128)S(1)}, f32[256,256]{1,0:T(8,128)S(1)}, f32[256,256]{1,...) custom-call(s32[4]{0:T(128)S(1)} %add_convert_fusion.refs_0_, f32[256,256]{1,0:T(8,128)S(1)} %copy-done.15, ...), custom_call_target="tpu_custom_call" | custom-call | flops 1610612736 | bytes 8388608 | tf_op jit(solution)/shard_map/pallas_call | solution.py:365
  195.2 6.0 %collective-permute-start.18 = (f32[2,256]{1,0:T(2,128)S(1)}, f32[2,256]{1,0:T(2,128)S(1)}, u32[]{:S(2)}, u32[]{:S(2)}) collective-permute-start(f32[2,256]{1,0:T(2,128)S(1)} %get-tuple-element.92.refs_20_), channel_id=1, source_target_pairs={{0,254},{1,255},{2,0},{3,1},{4,2},{5,3},{6,4},{7,5},{8,6},{9,7},{1... | collective-permute-start | bytes 6152 | tf_op jit(solution)/shard_map/ppermute | solution.py:26
  201.1 7.2 %collective-permute-start.16 = (f32[2,256]{1,0:T(2,128)S(1)}, f32[2,256]{1,0:T(2,128)S(1)}, u32[]{:S(2)}, u32[]{:S(2)}) collective-permute-start(f32[2,256]{1,0:T(2,128)S(1)} %get-tuple-element.92.refs_20_), channel_id=1, source_target_pairs={{0,255},{1,0},{2,1},{3,2},{4,3},{5,4},{6,5},{7,6},{8,7},{9,8},{10,... | collective-permute-start | bytes 6152 | tf_op jit(solution)/shard_map/ppermute | solution.py:26
  209.6 14.7 %shard_map.60 = (f32[256,4096]{1,0:T(8,128)}, f32[256,4096]{1,0:T(8,128)}) custom-call(s32[4]{0:T(128)S(1)} %add_convert_fusion.refs_0_, s32[1,256]{1,0:T(1,128)S(1)} %bitcast.35, f32[256,256]{1,0:T(8,128)S(1)} %copy.15.refs_2_, f32[256,256]{1,0:T(8,128)S(1)} %copy.16.refs_3_, f32[256,256]{1,0:T(8,128)S(1)} %copy.17.refs_4_, f32[256,256]{1,0:T(8,128)S(1)} %copy.18.refs_5_, ...), custom_call_target="tpu_custom_call" | custom-call | flops 8589934592 | bytes 29360128 | tf_op jit(solution)/shard_map/pallas_call | solution.py:405
  (69 shorter events, 30.8 us)
Async XLA Ops:
  0.6 68.3 %collective-permute-start.3 = (bf16[256,4096]{1,0:T(8,128)(2,1)}, bf16[256,4096]{1,0:T(8,128)(2,1)}, u32[]{:S(2)}, u32[]{:S(2)}) collective-permute-start(bf16[256,4096]{1,0:T(8,128)(2,1)} %refs_25_.1), channel_id=1, source_target_pairs={{0,129},{1,128},{2,131},{3,130},{4,133},{5,132},{6,135},{7,134},{8... | collective-permute-start | bytes 6291464 | tf_op jit(solution)/shard_map/ppermute | solution.py:26
  2.0 71.1 %collective-permute-start.4 = (bf16[256,4096]{1,0:T(8,128)(2,1)}, bf16[256,4096]{1,0:T(8,128)(2,1)}, u32[]{:S(2)}, u32[]{:S(2)}) collective-permute-start(bf16[256,4096]{1,0:T(8,128)(2,1)} %refs_26_.1), channel_id=1, source_target_pairs={{0,128},{1,129},{2,130},{3,131},{4,132},{5,133},{6,134},{7,135},{8... | collective-permute-start | bytes 6291464 | tf_op jit(solution)/shard_map/ppermute | solution.py:26
  2.7 72.4 %collective-permute-start.2 = (bf16[256,4096]{1,0:T(8,128)(2,1)}, bf16[256,4096]{1,0:T(8,128)(2,1)}, u32[]{:S(2)}, u32[]{:S(2)}) collective-permute-start(bf16[256,4096]{1,0:T(8,128)(2,1)} %refs_25_.1), channel_id=1, source_target_pairs={{0,255},{127,128},{128,127},{255,0}} | collective-permute-start | bytes 6291464 | tf_op jit(solution)/shard_map/ppermute | solution.py:26
  13.5 61.6 %collective-permute-start.1 = (bf16[256,4096]{1,0:T(8,128)(2,1)}, bf16[256,4096]{1,0:T(8,128)(2,1)}, u32[]{:S(2)}, u32[]{:S(2)}) collective-permute-start(bf16[256,4096]{1,0:T(8,128)(2,1)} %refs_26_.1), channel_id=1, source_target_pairs={{0,254},{1,255},{2,0},{3,1},{4,2},{5,3},{6,4},{7,5},{8,6},{9,7},{1... | collective-permute-start | bytes 6291464 | tf_op jit(solution)/shard_map/ppermute | solution.py:26
  13.6 61.5 %collective-permute-start = (bf16[256,4096]{1,0:T(8,128)(2,1)}, bf16[256,4096]{1,0:T(8,128)(2,1)}, u32[]{:S(2)}, u32[]{:S(2)}) collective-permute-start(bf16[256,4096]{1,0:T(8,128)(2,1)} %refs_26_.1), channel_id=1, source_target_pairs={{0,2},{1,3},{2,4},{3,5},{4,6},{5,7},{6,8},{7,9},{8,10},{9,11},{10,... | collective-permute-start | bytes 6291464 | tf_op jit(solution)/shard_map/ppermute | solution.py:26
  73.1 46.5 %collective-permute-start.5 = (bf16[256,4096]{1,0:T(8,128)(2,1)}, bf16[256,4096]{1,0:T(8,128)(2,1)}, u32[]{:S(2)}, u32[]{:S(2)}) collective-permute-start(bf16[256,4096]{1,0:T(8,128)(2,1)} %collective-permute-done.3), channel_id=1, source_target_pairs={{0,129},{1,128},{2,131},{3,130},{4,133},{5,132},{6,135},{7,134},{8... | collective-permute-start | bytes 6291464 | tf_op jit(solution)/shard_map/ppermute | solution.py:26
  73.1 47.6 %collective-permute-start.6 = (bf16[256,4096]{1,0:T(8,128)(2,1)}, bf16[256,4096]{1,0:T(8,128)(2,1)S(1)}, u32[]{:S(2)}, u32[]{:S(2)}) collective-permute-start(bf16[256,4096]{1,0:T(8,128)(2,1)} %collective-permute-done.4), channel_id=1, source_target_pairs={{0,128},{1,129},{2,130},{3,131},{4,132},{5,133},{6,134},{7,135},{8... | collective-permute-start | bytes 6291464 | tf_op jit(solution)/shard_map/ppermute | solution.py:26
  75.1 50.2 %collective-permute-start.11 = (bf16[256,4096]{1,0:T(8,128)(2,1)S(1)}, bf16[256,4096]{1,0:T(8,128)(2,1)S(1)}, u32[]{:S(2)}, u32[]{:S(2)}) collective-permute-start(bf16[256,4096]{1,0:T(8,128)(2,1)S(1)} %copy-done), channel_id=1, source_target_pairs={{2,0},{3,1},{4,2},{5,3},{6,4},{7,5},{8,6},{9,7},{10,8},{11,9},{12,... | collective-permute-start | bytes 6291464 | tf_op jit(solution)/shard_map/ppermute | solution.py:26
  76.4 52.9 %collective-permute-start.10 = (bf16[256,4096]{1,0:T(8,128)(2,1)S(1)}, bf16[256,4096]{1,0:T(8,128)(2,1)S(1)}, u32[]{:S(2)}, u32[]{:S(2)}) collective-permute-start(bf16[256,4096]{1,0:T(8,128)(2,1)S(1)} %copy-done), channel_id=1, source_target_pairs={{0,2},{1,3},{2,4},{3,5},{4,6},{5,7},{6,8},{7,9},{8,10},{9,11},{10,... | collective-permute-start | bytes 6291464 | tf_op jit(solution)/shard_map/ppermute | solution.py:26
  81.1 49.5 %collective-permute-start.9 = (bf16[256,4096]{1,0:T(8,128)(2,1)S(1)}, bf16[256,4096]{1,0:T(8,128)(2,1)}, u32[]{:S(2)}, u32[]{:S(2)}) collective-permute-start(bf16[256,4096]{1,0:T(8,128)(2,1)S(1)} %copy-done), channel_id=1, source_target_pairs={{0,134},{1,135},{126,248},{127,249},{128,6},{129,7},{254,120},{255... | collective-permute-start | bytes 6291464 | tf_op jit(solution)/shard_map/ppermute | solution.py:26
  98.3 55.3 %copy-start.16 = (s32[256]{0:T(256)S(1)}, s32[256]{0:T(256)}, u32[]{:S(2)}) copy-start(s32[256]{0:T(256)} %param.5) | copy-start | bytes 3076
  122.1 24.1 %collective-permute-start.7 = (bf16[256,2048]{1,0:T(8,128)(2,1)S(1)}, bf16[256,2048]{1,0:T(8,128)(2,1)}, u32[]{:S(2)}, u32[]{:S(2)}) collective-permute-start(bf16[256,2048]{1,0:T(8,128)(2,1)S(1)} %get-tuple-element.63), channel_id=1, source_target_pairs={{0,128},{1,129},{2,130},{3,131},{4,132},{5,133},{6,134},{7,135},{8... | collective-permute-start | bytes 3145736 | tf_op jit(solution)/shard_map/ppermute | solution.py:26
  122.6 23.6 %collective-permute-start.8 = (bf16[256,2048]{1,0:T(8,128)(2,1)S(1)}, bf16[256,2048]{1,0:T(8,128)(2,1)}, u32[]{:S(2)}, u32[]{:S(2)}) collective-permute-start(bf16[256,2048]{1,0:T(8,128)(2,1)S(1)} %get-tuple-element.64), channel_id=1, source_target_pairs={{0,129},{1,128},{2,131},{3,130},{4,133},{5,132},{6,135},{7,134},{8... | collective-permute-start | bytes 3145736 | tf_op jit(solution)/shard_map/ppermute | solution.py:26
  126.7 44.7 %collective-permute-start.12 = (bf16[256,4096]{1,0:T(8,128)(2,1)}, bf16[256,4096]{1,0:T(8,128)(2,1)}, u32[]{:S(2)}, u32[]{:S(2)}) collective-permute-start(bf16[256,4096]{1,0:T(8,128)(2,1)} %collective-permute-done.5.refs_13_.refs_31_), channel_id=1, source_target_pairs={{0,2},{2,4},{3,1},{4,6},{5,3},{6,8},{7,5},{8,10},{9,7},{10,12},{11... | collective-permute-start | bytes 6291464 | tf_op jit(solution)/shard_map/ppermute | solution.py:26
  146.2 41.2 %collective-permute-start.15 = (bf16[256,4096]{1,0:T(8,128)(2,1)}, bf16[256,4096]{1,0:T(8,128)(2,1)}, u32[]{:S(2)}, u32[]{:S(2)}) collective-permute-start(bf16[256,4096]{1,0:T(8,128)(2,1)} %collective-permute-done.9), channel_id=1, source_target_pairs={{6,126},{7,127},{120,0},{121,1},{134,254},{135,255},{248,128},{249... | collective-permute-start | bytes 6291464 | tf_op jit(solution)/shard_map/ppermute | solution.py:26
  147.4 28.0 %collective-permute-start.13 = (bf16[256,2048]{1,0:T(8,128)(2,1)}, bf16[256,2048]{1,0:T(8,128)(2,1)}, u32[]{:S(2)}, u32[]{:S(2)}) collective-permute-start(bf16[256,2048]{1,0:T(8,128)(2,1)} %collective-permute-done.7), channel_id=1, source_target_pairs={{0,128},{1,129},{2,130},{3,131},{4,132},{5,133},{6,134},{7,135},{8... | collective-permute-start | bytes 3145736 | tf_op jit(solution)/shard_map/ppermute | solution.py:26
  147.5 27.9 %collective-permute-start.14 = (bf16[256,2048]{1,0:T(8,128)(2,1)}, bf16[256,2048]{1,0:T(8,128)(2,1)}, u32[]{:S(2)}, u32[]{:S(2)}) collective-permute-start(bf16[256,2048]{1,0:T(8,128)(2,1)} %collective-permute-done.8), channel_id=1, source_target_pairs={{0,129},{1,128},{2,131},{3,130},{4,133},{5,132},{6,135},{7,134},{8... | collective-permute-start | bytes 3145736 | tf_op jit(solution)/shard_map/ppermute | solution.py:26
  163.4 24.0 %copy-start.3 = (bf16[256,4096]{1,0:T(8,128)(2,1)S(1)}, bf16[256,4096]{1,0:T(8,128)(2,1)}, u32[]{:S(2)}) copy-start(bf16[256,4096]{1,0:T(8,128)(2,1)} %refs_26_.1) | copy-start | bytes 6291460
  163.4 24.0 %copy-start.14 = (f32[256,256]{1,0:T(8,128)S(1)}, f32[256,256]{1,0:T(8,128)}, u32[]{:S(2)}) copy-start(f32[256,256]{1,0:T(8,128)} %fusion.refs_2_) | copy-start | bytes 786436
  163.4 24.0 %copy-start.15 = (f32[256,256]{1,0:T(8,128)S(1)}, f32[256,256]{1,0:T(8,128)}, u32[]{:S(2)}) copy-start(f32[256,256]{1,0:T(8,128)} %fusion.1.refs_1_) | copy-start | bytes 786436
  195.2 13.1 %collective-permute-start.19 = (f32[2,256]{1,0:T(2,128)S(1)}, f32[2,256]{1,0:T(2,128)S(1)}, u32[]{:S(2)}, u32[]{:S(2)}) collective-permute-start(f32[2,256]{1,0:T(2,128)S(1)} %get-tuple-element.92.refs_20_), channel_id=1, source_target_pairs={{0,2},{1,3},{2,4},{3,5},{4,6},{5,7},{6,8},{7,9},{8,10},{9,11},{10,... | collective-permute-start | bytes 6152 | tf_op jit(solution)/shard_map/ppermute | solution.py:26
  195.2 13.1 %collective-permute-start.18 = (f32[2,256]{1,0:T(2,128)S(1)}, f32[2,256]{1,0:T(2,128)S(1)}, u32[]{:S(2)}, u32[]{:S(2)}) collective-permute-start(f32[2,256]{1,0:T(2,128)S(1)} %get-tuple-element.92.refs_20_), channel_id=1, source_target_pairs={{0,254},{1,255},{2,0},{3,1},{4,2},{5,3},{6,4},{7,5},{8,6},{9,7},{1... | collective-permute-start | bytes 6152 | tf_op jit(solution)/shard_map/ppermute | solution.py:26
  201.1 8.4 %collective-permute-start.17 = (f32[2,256]{1,0:T(2,128)S(1)}, f32[2,256]{1,0:T(2,128)S(1)}, u32[]{:S(2)}, u32[]{:S(2)}) collective-permute-start(f32[2,256]{1,0:T(2,128)S(1)} %get-tuple-element.92.refs_20_), channel_id=1, source_target_pairs={{0,1},{1,2},{2,3},{3,4},{4,5},{5,6},{6,7},{7,8},{8,9},{9,10},{10,1... | collective-permute-start | bytes 6152 | tf_op jit(solution)/shard_map/ppermute | solution.py:26
  201.1 8.5 %collective-permute-start.16 = (f32[2,256]{1,0:T(2,128)S(1)}, f32[2,256]{1,0:T(2,128)S(1)}, u32[]{:S(2)}, u32[]{:S(2)}) collective-permute-start(f32[2,256]{1,0:T(2,128)S(1)} %get-tuple-element.92.refs_20_), channel_id=1, source_target_pairs={{0,255},{1,0},{2,1},{3,2},{4,3},{5,4},{6,5},{7,6},{8,7},{9,8},{10,... | collective-permute-start | bytes 6152 | tf_op jit(solution)/shard_map/ppermute | solution.py:26
  (13 other events, 63.3 us)

commit v3 on v2

--- a/solution.py
+++ b/solution.py
@@ -9,9 +9,10 @@
 
 AXES = ("dp", "inner")
 NEGATIVE = -1e30
-CHUNK = 1024
-VMEM_LIMIT = 46 * 1024 * 1024
-SMALL_LIMIT = 16 * 1024 * 1024
+CHUNK = 512
+SLOTS = 4
+VMEM_LIMIT = 20 * 1024 * 1024
+SMALL_LIMIT = 14 * 1024 * 1024
 
 
 def contract(left_rows, right_rows):
@@ -165,12 +166,15 @@
     even, first, last, edge = [place[k] == 1 for k in range(4)]
 
     def bring(part):
-        def one(source, slot, column=part * chunk):
+        held = part % SLOTS
+        column = part * chunk if isinstance(part, int) else pl.multiple_of(part * chunk, chunk)
+
+        def one(source, slot, column=column):
             start = slot * size if isinstance(slot, int) else pl.multiple_of(slot * size, size)
             pltpu.make_async_copy(
                 source.at[:, pl.ds(column, chunk)],
-                rows.at[part, pl.ds(start, size), :],
-                arrived.at[part],
+                rows.at[held, pl.ds(start, size), :],
+                arrived.at[held],
             ).start()
 
         def either(taken, yes, no, slot):
@@ -183,16 +187,22 @@
         one(d_p2, 8)
         one(q_pair, jnp.where(even, 1, 7))
         one(d_pair, jnp.where(even, 6, 9))
-        source = d_low if part < parts // 2 else d_high
-        one(source, jnp.where(even, 9, 6), part % (parts // 2) * chunk)
+        d_slot = jnp.where(even, 9, 6)
+        if isinstance(part, int):
+            source = d_low if part < parts // 2 else d_high
+            one(source, d_slot, part % (parts // 2) * chunk)
+        else:
+            inside = pl.multiple_of(part % (parts // 2) * chunk, chunk)
+            pl.when(part < parts // 2)(lambda: one(d_low, d_slot, inside))
+            pl.when(part >= parts // 2)(lambda: one(d_high, d_slot, inside))
         either(edge, q_edge, q_diag, jnp.where(even, 7, 1))
         either(last, q_swap, q_n2, 0)
         either(first, q_swap, q_p2, 5)
 
     @pl.when(step == 0)
     def _():
-        bring(0)
-        bring(1)
+        for part in range(SLOTS - 1):
+            bring(part)
         qq, qd, dq, dd, qd_n2, dd_n2, dd_p2 = tiles[:7]
         qq_n2, dq_p2, qq_p2, qq_pair, cross_pair, dd_pair = tiles[7:13]
         qq_diag, cross_diag, dd_diag, qq_swap, dq_swap = tiles[13:]
@@ -233,16 +243,19 @@
         put(coef_d, 5, pick(even, cross_diag, cross_pair), d_col, q_of(lse_p1))
         put(coef_d, 6, dd_p2[...], d_col, d_of(lse_p2))
         put(coef_d, 7, pick(even, dd_diag, dd_pair), d_col, d_of(lse_p1))
-        for part in range(2, parts):
-            bring(part)
-
-    pltpu.make_async_copy(rows.at[step], rows.at[step], arrived.at[step]).wait()
+
+    @pl.when(step + SLOTS - 1 < parts)
+    def _():
+        bring(step + SLOTS - 1)
+
+    held = step % SLOTS
+    pltpu.make_async_copy(rows.at[held], rows.at[held], arrived.at[held]).wait()
     depth = coef_q.shape[1]
     grad_q[...] = factor * jnp.dot(
-        coef_q[...], rows[step, 0:depth, :], preferred_element_type=jnp.float32
+        coef_q[...], rows[held, 0:depth, :], preferred_element_type=jnp.float32
     )
     grad_d[...] = factor * jnp.dot(
-        coef_d[...], rows[step, 2 * size :, :], preferred_element_type=jnp.float32
+        coef_d[...], rows[held, 2 * size :, :], preferred_element_type=jnp.float32
     )
 
 
@@ -289,13 +302,15 @@
     q_down, d_up, own_tiles = barrier((q_down, d_up, own_tiles))
     q_pair = sent(q_down, down)
     d_pair = sent(d_up, up)
-    q_own, d_p2, d_n2, q_edge, q_down, d_up = barrier((queries, d_p2, d_n2, q_edge, q_down, d_up))
+    q_own, q_edge = barrier((queries, q_edge))
+    q_p2 = sent(q_own, lambda i: i + 2, [i for i in range(count) if i % half < half - 2])
+    q_own, d_n2 = barrier((queries, d_n2))
+    q_n2 = sent(q_own, lambda i: i - 2, [i for i in range(count) if i % half >= 2])
+    q_own, d_p2, d_n2, q_down, d_up = barrier((queries, d_p2, d_n2, q_down, d_up))
     crossing = [i for i in range(count) if i % half < 2 or i % half >= half - 2]
     q_swap = sent(
         q_own, lambda i: i + half + (inner - 2 if i % half < 2 else 2 - inner), crossing
     )
-    q_p2 = sent(q_own, lambda i: i + 2, [i for i in range(count) if i % half < half - 2])
-    q_n2 = sent(q_own, lambda i: i - 2, [i for i in range(count) if i % half >= 2])
     far_tiles = [
         tile(queries, d_n2),
         tile(documents, d_n2),
@@ -306,14 +321,12 @@
     cut = width // 2
     d_low = jnp.where(is_even, d_n2[:, :cut], d_p2[:, :cut])
     d_high = jnp.where(is_even, d_n2[:, cut:], d_p2[:, cut:])
-    d_low, d_high, q_pair, d_pair, far_tiles = barrier((d_low, d_high, q_pair, d_pair, far_tiles))
+    d_low, d_high, q_pair, d_pair, q_p2, q_n2, far_tiles = barrier(
+        (d_low, d_high, q_pair, d_pair, q_p2, q_n2, far_tiles)
+    )
+    q_diag = sent(q_pair, lambda i: i - i % half + (i + (-2 if i % 2 else 2)) % half)
     d_low = sent(d_low, up)
     d_high = sent(d_high, down)
-    q_diag = sent(
-        q_pair,
-        lambda i: i - 2 if i % 2 else i + 2,
-        [i for i in range(count) if i % half != 1 and i % half != half - 2],
-    )
     d_low, d_high, q_swap, q_pair, d_pair, q_p2, q_n2 = barrier(
         (d_low, d_high, q_swap, q_pair, d_pair, q_p2, q_n2)
     )
@@ -411,8 +424,8 @@
         scratch_shapes=[
             pltpu.VMEM((size, 8 * size), jnp.bfloat16),
             pltpu.VMEM((size, 8 * size), jnp.bfloat16),
-            pltpu.VMEM((parts, 10 * size, CHUNK), jnp.bfloat16),
-            pltpu.SemaphoreType.DMA((parts,)),
+            pltpu.VMEM((SLOTS, 10 * size, CHUNK), jnp.bfloat16),
+            pltpu.SemaphoreType.DMA((SLOTS,)),
         ],
         compiler_params=pltpu.CompilerParams(vmem_limit_bytes=VMEM_LIMIT),
         cost_estimate=pl.CostEstimate(

time: 225 us -> 240 us (1.067)
  waiting for transfers between devices: 106 us -> 132 us
  starting transfers between devices: 52 us -> 42.4 us
    ppermute x20, waiting for transfers between devices: 106 us -> 132 us  [sent(): return lax.ppermute(value, AXES, [(i, target(i) % count) for i in senders])]
    ppermute x20, starting transfers between devices: 52 us -> 42.4 us  [sent(): return lax.ppermute(value, AXES, [(i, target(i) % count) for i in senders])]
    unnamed x34 -> x40, local copies, waits for them, and re-layouts: 12.7 us -> 12.2 us
  transfers between devices with their start and end apart: 20 -> 20, of which waited for: 9 -> 10; matrix products, arithmetic and copies ran while one was open for 11% -> 10% of each run, Pallas kernels for 3% -> 3%
where the time goes in v3:
time: 240 us
  waiting for transfers between devices  132 us (55%)
  starting transfers between devices  42.4 us (18%)
  Pallas kernels  27.9 us (12%)
  matrix products  20.5 us (9%)
  local copies, waits for them, and re-layouts  13.7 us (6%)
  other arithmetic  2.47 us (1%)
    ppermute x20, waiting for transfers between devices, sent(): return lax.ppermute(value, AXES, [(i, target(i) % count) for i in senders])  132 us
    ppermute x20, starting transfers between devices, sent(): return lax.ppermute(value, AXES, [(i, target(i) % count) for i in senders])  42.4 us
    dot_general x9, matrix products, contract(): lax.dot_general(left_rows, right_rows, (((1,), (1,)), ((), ())), preferre...  20.5 us
    pallas_call x1, Pallas kernels, per_device(): pl.pallas_call(kernel, grid=(parts,), out_shape=(jax.ShapeDtypeStruct((si...  13.9 us
    unnamed x40, local copies, waits for them, and re-layouts  12.2 us
    pallas_call x1, Pallas kernels, per_device(): pl.pallas_call(last_tiles, out_shape=(square,) * 5 + (jax.ShapeDtypeStruc...  7.77 us
    pallas_call x1, Pallas kernels, per_device(): pl.pallas_call(early_tiles, out_shape=(square,) * 6 + (column,) * 4 + (ro...  6.25 us
  transfers between devices with their start and end apart: 20, of which 10 were waited for; matrix products, arithmetic and copies ran while one was open for 10% of the time, Pallas kernels for 3%

profile of v3, /device:TPU:0, one launch (start us, length us, event | category | flops | bytes accessed | tf_op | source)
XLA Modules:
  0.0 239.8 jit_solution(10181766170201109583)
XLA Ops:
  0.6 6.9 %collective-permute-start.1 = (bf16[256,4096]{1,0:T(8,128)(2,1)}, bf16[256,4096]{1,0:T(8,128)(2,1)}, u32[]{:S(2)}, u32[]{:S(2)}) collective-permute-start(bf16[256,4096]{1,0:T(8,128)(2,1)} %refs_26_.1), channel_id=1, source_target_pairs={{0,254},{1,255},{2,0},{3,1},{4,2},{5,3},{6,4},{7,5},{8,6},{9,7},{1... | collective-permute-start | bytes 6291464 | tf_op jit(solution)/shard_map/ppermute | solution.py:27
  7.5 3.9 %collective-permute-start.6 = (bf16[256,4096]{1,0:T(8,128)(2,1)}, bf16[256,4096]{1,0:T(8,128)(2,1)}, u32[]{:S(2)}, u32[]{:S(2)}) collective-permute-start(bf16[256,4096]{1,0:T(8,128)(2,1)} %refs_25_.1), channel_id=1, source_target_pairs={{0,255},{127,128},{128,127},{255,0}} | collective-permute-start | bytes 6291464 | tf_op jit(solution)/shard_map/ppermute | solution.py:27
  11.6 3.1 %collective-permute-start.2 = (bf16[256,4096]{1,0:T(8,128)(2,1)}, bf16[256,4096]{1,0:T(8,128)(2,1)}, u32[]{:S(2)}, u32[]{:S(2)}) collective-permute-start(bf16[256,4096]{1,0:T(8,128)(2,1)} %refs_25_.1), channel_id=1, source_target_pairs={{0,129},{1,128},{2,131},{3,130},{4,133},{5,132},{6,135},{7,134},{8... | collective-permute-start | bytes 6291464 | tf_op jit(solution)/shard_map/ppermute | solution.py:27
  14.7 3.8 %fusion.5 = f32[256,256]{0,1:T(8,128)} fusion(bf16[256,4096]{1,0:T(8,128)(2,1)} %refs_26_.1), kind=kOutput, calls=%fused_computation.11 | convolution fusion | flops 537067520 | bytes 2359296 | tf_op jit(solution)/shard_map/dot_general | solution.py:19
  20.8 25.7 %collective-permute-done.1.refs_28_ = bf16[256,4096]{1,0:T(8,128)(2,1)} collective-permute-done((bf16[256,4096]{1,0:T(8,128)(2,1)}, bf16[256,4096]{1,0:T(8,128)(2,1)}, u32[]{:S(2)}, u32[]{:S(2)}) %collective-permute-start.1) | collective-permute-done | bytes 2097184 | tf_op jit(solution)/shard_map/ppermute | solution.py:27
  47.7 6.2 %collective-permute-done.6.refs_33_ = bf16[256,4096]{1,0:T(8,128)(2,1)} collective-permute-done((bf16[256,4096]{1,0:T(8,128)(2,1)}, bf16[256,4096]{1,0:T(8,128)(2,1)}, u32[]{:S(2)}, u32[]{:S(2)}) %collective-permute-start.6) | collective-permute-done | bytes 2097184 | tf_op jit(solution)/shard_map/ppermute | solution.py:27
  55.3 20.2 %collective-permute-done.3 = bf16[256,4096]{1,0:T(8,128)(2,1)} collective-permute-done((bf16[256,4096]{1,0:T(8,128)(2,1)}, bf16[256,4096]{1,0:T(8,128)(2,1)}, u32[]{:S(2)}, u32[]{:S(2)}) %collective-permute-start.3) | collective-permute-done | bytes 2097184 | tf_op jit(solution)/shard_map/ppermute | solution.py:27
  75.5 3.7 %collective-permute-done.2 = bf16[256,4096]{1,0:T(8,128)(2,1)} collective-permute-done((bf16[256,4096]{1,0:T(8,128)(2,1)}, bf16[256,4096]{1,0:T(8,128)(2,1)}, u32[]{:S(2)}, u32[]{:S(2)}) %collective-permute-start.2) | collective-permute-done | bytes 2097184 | tf_op jit(solution)/shard_map/ppermute | solution.py:27
  81.2 2.7 %collective-permute-start.11 = (bf16[256,4096]{1,0:T(8,128)(2,1)S(1)}, bf16[256,4096]{1,0:T(8,128)(2,1)}, u32[]{:S(2)}, u32[]{:S(2)}) collective-permute-start(bf16[256,4096]{1,0:T(8,128)(2,1)S(1)} %copy-done), channel_id=1, source_target_pairs={{0,134},{1,135},{126,248},{127,249},{128,6},{129,7},{254,120},{255... | collective-permute-start | bytes 6291464 | tf_op jit(solution)/shard_map/ppermute | solution.py:27
  83.9 3.0 %fusion.refs_2_ = f32[256,256]{1,0:T(8,128)} fusion(bf16[256,4096]{1,0:T(8,128)(2,1)} %collective-permute-done.6.refs_33_, bf16[256,4096]{1,0:T(8,128)(2,1)S(1)} %copy-done.1), kind=kOutput, calls=%fused_computation.1 | convolution fusion | flops 536936448 | bytes 4456448 | tf_op jit(solution)/shard_map/dot_general | solution.py:19
  87.0 3.0 %fusion.1.refs_1_ = f32[256,256]{1,0:T(8,128)} fusion(bf16[256,4096]{1,0:T(8,128)(2,1)} %collective-permute-done.6.refs_33_, bf16[256,4096]{1,0:T(8,128)(2,1)S(1)} %copy-done), kind=kOutput, calls=%fused_computation.3 | convolution fusion | flops 536936448 | bytes 4456448 | tf_op jit(solution)/shard_map/dot_general | solution.py:19
  90.0 2.3 fusion.3.refs_7_
  92.3 3.0 %fusion.4.refs_6_ = f32[256,256]{1,0:T(8,128)} fusion(bf16[256,4096]{1,0:T(8,128)(2,1)} %collective-permute-done.1.refs_28_, bf16[256,4096]{1,0:T(8,128)(2,1)S(1)} %copy-done), kind=kOutput, calls=%fused_computation.9 | convolution fusion | flops 536936448 | bytes 4456448 | tf_op jit(solution)/shard_map/dot_general | solution.py:19
  95.4 3.0 %fusion.2.refs_8_ = f32[256,256]{1,0:T(8,128)} fusion(bf16[256,4096]{1,0:T(8,128)(2,1)} %collective-permute-done.refs_30_, bf16[256,4096]{1,0:T(8,128)(2,1)S(1)} %copy-done.1), kind=kOutput, calls=%fused_computation.5 | convolution fusion | flops 536936448 | bytes 4456448 | tf_op jit(solution)/shard_map/dot_general | solution.py:19
  98.4 2.4 slice_select_fusion
  103.5 19.0 %collective-permute-done.4.refs_13_.refs_31_ = bf16[256,4096]{1,0:T(8,128)(2,1)} collective-permute-done((bf16[256,4096]{1,0:T(8,128)(2,1)}, bf16[256,4096]{1,0:T(8,128)(2,1)}, u32[]{:S(2)}, u32[]{:S(2)}) %collective-permute-start.4) | collective-permute-done | bytes 2097184 | tf_op jit(solution)/shard_map/ppermute | solution.py:27
  123.8 2.2 collective-permute-start.9
  127.1 17.9 %collective-permute-done.9 = bf16[256,2048]{1,0:T(8,128)(2,1)} collective-permute-done((bf16[256,2048]{1,0:T(8,128)(2,1)S(1)}, bf16[256,2048]{1,0:T(8,128)(2,1)}, u32[]{:S(2)}, u32[]{:S(2)}) %collective-permute-start.9) | collective-permute-done | bytes 1048608 | tf_op jit(solution)/shard_map/ppermute | solution.py:27
  160.2 6.2 %shard_map.58 = (f32[256,256]{1,0:T(8,128)S(1)}, f32[256,256]{1,0:T(8,128)S(1)}, f32[256,256]{1,0:T(8,128)S(1)}, f32[256,256]{1,0:T(8,128)S(1)}, f32[256,256]{1,...) custom-call(s32[4]{0:T(128)S(1)} %add_convert_fusion.refs_0_, ...), custom_call_target="tpu_custom_call" | custom-call | flops 3221225472 | bytes 12582912 | tf_op jit(solution)/shard_map/pallas_call | solution.py:351
  166.5 37.0 %collective-permute-done.15.refs_13_.refs_37_ = bf16[256,4096]{1,0:T(8,128)(2,1)} collective-permute-done((bf16[256,4096]{1,0:T(8,128)(2,1)}, bf16[256,4096]{1,0:T(8,128)(2,1)}, u32[]{:S(2)}, u32[]{:S(2)}) %collective-permute-start.15) | collective-permute-done | bytes 2097184 | tf_op jit(solution)/shard_map/ppermute | solution.py:27
  203.6 7.8 %shard_map.59 = (f32[256,256]{1,0:T(8,128)S(1)}, f32[256,256]{1,0:T(8,128)S(1)}, f32[256,256]{1,0:T(8,128)S(1)}, f32[256,256]{1,0:T(8,128)S(1)}, f32[256,256]{1,...) custom-call(s32[4]{0:T(128)S(1)} %add_convert_fusion.refs_0_, f32[256,256]{1,0:T(8,128)S(1)} %copy-done.18, ...), custom_call_target="tpu_custom_call" | custom-call | flops 1610612736 | bytes 8388608 | tf_op jit(solution)/shard_map/pallas_call | solution.py:378
  211.3 6.0 %collective-permute-start.18 = (f32[2,256]{1,0:T(2,128)S(1)}, f32[2,256]{1,0:T(2,128)S(1)}, u32[]{:S(2)}, u32[]{:S(2)}) collective-permute-start(f32[2,256]{1,0:T(2,128)S(1)} %get-tuple-element.102.refs_20_), channel_id=1, source_target_pairs={{0,254},{1,255},{2,0},{3,1},{4,2},{5,3},{6,4},{7,5},{8,6},{9,7},{1... | collective-permute-start | bytes 6152 | tf_op jit(solution)/shard_map/ppermute | solution.py:27
  219.0 5.4 %collective-permute-start.16 = (f32[2,256]{1,0:T(2,128)S(1)}, f32[2,256]{1,0:T(2,128)S(1)}, u32[]{:S(2)}, u32[]{:S(2)}) collective-permute-start(f32[2,256]{1,0:T(2,128)S(1)} %get-tuple-element.102.refs_20_), channel_id=1, source_target_pairs={{0,255},{1,0},{2,1},{3,2},{4,3},{5,4},{6,5},{7,6},{8,7},{9,8},{10,... | collective-permute-start | bytes 6152 | tf_op jit(solution)/shard_map/ppermute | solution.py:27
  225.8 13.9 %shard_map.60 = (f32[256,4096]{1,0:T(8,128)}, f32[256,4096]{1,0:T(8,128)}) custom-call(s32[4]{0:T(128)S(1)} %add_convert_fusion.refs_0_, s32[1,256]{1,0:T(1,128)S(1)} %bitcast.35, f32[256,256]{1,0:T(8,128)S(1)} %copy.15.refs_2_, f32[256,256]{1,0:T(8,128)S(1)} %copy.16.refs_3_, f32[256,256]{1,0:T(8,128)S(1)} %copy.17.refs_4_, f32[256,256]{1,0:T(8,128)S(1)} %copy.18.refs_5_, ...), custom_call_target="tpu_custom_call" | custom-call | flops 8589934592 | bytes 29360128 | tf_op jit(solution)/shard_map/pallas_call | solution.py:418
  (75 shorter events, 30.5 us)
Async XLA Ops:
  0.6 45.8 %collective-permute-start.1 = (bf16[256,4096]{1,0:T(8,128)(2,1)}, bf16[256,4096]{1,0:T(8,128)(2,1)}, u32[]{:S(2)}, u32[]{:S(2)}) collective-permute-start(bf16[256,4096]{1,0:T(8,128)(2,1)} %refs_26_.1), channel_id=1, source_target_pairs={{0,254},{1,255},{2,0},{3,1},{4,2},{5,3},{6,4},{7,5},{8,6},{9,7},{1... | collective-permute-start | bytes 6291464 | tf_op jit(solution)/shard_map/ppermute | solution.py:27
  7.5 46.4 %collective-permute-start.6 = (bf16[256,4096]{1,0:T(8,128)(2,1)}, bf16[256,4096]{1,0:T(8,128)(2,1)}, u32[]{:S(2)}, u32[]{:S(2)}) collective-permute-start(bf16[256,4096]{1,0:T(8,128)(2,1)} %refs_25_.1), channel_id=1, source_target_pairs={{0,255},{127,128},{128,127},{255,0}} | collective-permute-start | bytes 6291464 | tf_op jit(solution)/shard_map/ppermute | solution.py:27
  11.4 64.2 %collective-permute-start.3 = (bf16[256,4096]{1,0:T(8,128)(2,1)}, bf16[256,4096]{1,0:T(8,128)(2,1)}, u32[]{:S(2)}, u32[]{:S(2)}) collective-permute-start(bf16[256,4096]{1,0:T(8,128)(2,1)} %refs_26_.1), channel_id=1, source_target_pairs={{0,128},{1,129},{2,130},{3,131},{4,132},{5,133},{6,134},{7,135},{8... | collective-permute-start | bytes 6291464 | tf_op jit(solution)/shard_map/ppermute | solution.py:27
  11.6 67.6 %collective-permute-start.2 = (bf16[256,4096]{1,0:T(8,128)(2,1)}, bf16[256,4096]{1,0:T(8,128)(2,1)}, u32[]{:S(2)}, u32[]{:S(2)}) collective-permute-start(bf16[256,4096]{1,0:T(8,128)(2,1)} %refs_25_.1), channel_id=1, source_target_pairs={{0,129},{1,128},{2,131},{3,130},{4,133},{5,132},{6,135},{7,134},{8... | collective-permute-start | bytes 6291464 | tf_op jit(solution)/shard_map/ppermute | solution.py:27
  14.7 66.6 %collective-permute-start = (bf16[256,4096]{1,0:T(8,128)(2,1)}, bf16[256,4096]{1,0:T(8,128)(2,1)}, u32[]{:S(2)}, u32[]{:S(2)}) collective-permute-start(bf16[256,4096]{1,0:T(8,128)(2,1)} %refs_26_.1), channel_id=1, source_target_pairs={{0,2},{1,3},{2,4},{3,5},{4,6},{5,7},{6,8},{7,9},{8,10},{9,11},{10,... | collective-permute-start | bytes 6291464 | tf_op jit(solution)/shard_map/ppermute | solution.py:27
  46.4 54.4 %collective-permute-start.8 = (bf16[256,4096]{1,0:T(8,128)(2,1)S(1)}, bf16[256,4096]{1,0:T(8,128)(2,1)S(1)}, u32[]{:S(2)}, u32[]{:S(2)}) collective-permute-start(bf16[256,4096]{1,0:T(8,128)(2,1)S(1)} %copy-done), channel_id=1, source_target_pairs={{2,0},{3,1},{4,2},{5,3},{6,4},{7,5},{8,6},{9,7},{10,8},{11,9},{12,... | collective-permute-start | bytes 6291464 | tf_op jit(solution)/shard_map/ppermute | solution.py:27
  53.9 48.2 %collective-permute-start.7 = (bf16[256,4096]{1,0:T(8,128)(2,1)S(1)}, bf16[256,4096]{1,0:T(8,128)(2,1)S(1)}, u32[]{:S(2)}, u32[]{:S(2)}) collective-permute-start(bf16[256,4096]{1,0:T(8,128)(2,1)S(1)} %copy-done), channel_id=1, source_target_pairs={{0,2},{1,3},{2,4},{3,5},{4,6},{5,7},{6,8},{7,9},{8,10},{9,11},{10,... | collective-permute-start | bytes 6291464 | tf_op jit(solution)/shard_map/ppermute | solution.py:27
  79.2 43.2 %collective-permute-start.4 = (bf16[256,4096]{1,0:T(8,128)(2,1)}, bf16[256,4096]{1,0:T(8,128)(2,1)}, u32[]{:S(2)}, u32[]{:S(2)}) collective-permute-start(bf16[256,4096]{1,0:T(8,128)(2,1)} %collective-permute-done.2), channel_id=1, source_target_pairs={{0,129},{1,128},{2,131},{3,130},{4,133},{5,132},{6,135},{7,134},{8... | collective-permute-start | bytes 6291464 | tf_op jit(solution)/shard_map/ppermute | solution.py:27
  80.5 42.1 %collective-permute-start.5 = (bf16[256,4096]{1,0:T(8,128)(2,1)}, bf16[256,4096]{1,0:T(8,128)(2,1)S(1)}, u32[]{:S(2)}, u32[]{:S(2)}) collective-permute-start(bf16[256,4096]{1,0:T(8,128)(2,1)} %collective-permute-done.3), channel_id=1, source_target_pairs={{0,128},{1,129},{2,130},{3,131},{4,132},{5,133},{6,134},{7,135},{8... | collective-permute-start | bytes 6291464 | tf_op jit(solution)/shard_map/ppermute | solution.py:27
  81.2 45.8 %collective-permute-start.11 = (bf16[256,4096]{1,0:T(8,128)(2,1)S(1)}, bf16[256,4096]{1,0:T(8,128)(2,1)}, u32[]{:S(2)}, u32[]{:S(2)}) collective-permute-start(bf16[256,4096]{1,0:T(8,128)(2,1)S(1)} %copy-done), channel_id=1, source_target_pairs={{0,134},{1,135},{126,248},{127,249},{128,6},{129,7},{254,120},{255... | collective-permute-start | bytes 6291464 | tf_op jit(solution)/shard_map/ppermute | solution.py:27
  98.4 52.0 %copy-start.19 = (s32[256]{0:T(256)S(1)}, s32[256]{0:T(256)}, u32[]{:S(2)}) copy-start(s32[256]{0:T(256)} %param.5) | copy-start | bytes 3076
  123.8 21.1 %collective-permute-start.9 = (bf16[256,2048]{1,0:T(8,128)(2,1)S(1)}, bf16[256,2048]{1,0:T(8,128)(2,1)}, u32[]{:S(2)}, u32[]{:S(2)}) collective-permute-start(bf16[256,2048]{1,0:T(8,128)(2,1)S(1)} %get-tuple-element.71), channel_id=1, source_target_pairs={{0,128},{1,129},{2,130},{3,131},{4,132},{5,133},{6,134},{7,135},{8... | collective-permute-start | bytes 3145736 | tf_op jit(solution)/shard_map/ppermute | solution.py:27
  126.1 19.7 %collective-permute-start.10 = (bf16[256,2048]{1,0:T(8,128)(2,1)S(1)}, bf16[256,2048]{1,0:T(8,128)(2,1)}, u32[]{:S(2)}, u32[]{:S(2)}) collective-permute-start(bf16[256,2048]{1,0:T(8,128)(2,1)S(1)} %get-tuple-element.72), channel_id=1, source_target_pairs={{0,129},{1,128},{2,131},{3,130},{4,133},{5,132},{6,135},{7,134},{8... | collective-permute-start | bytes 3145736 | tf_op jit(solution)/shard_map/ppermute | solution.py:27
  127.1 39.4 %collective-permute-start.12 = (bf16[256,4096]{1,0:T(8,128)(2,1)}, bf16[256,4096]{1,0:T(8,128)(2,1)}, u32[]{:S(2)}, u32[]{:S(2)}) collective-permute-start(bf16[256,4096]{1,0:T(8,128)(2,1)} %collective-permute-done.4.refs_13_.refs_31_), channel_id=1, source_target_pairs={{0,2},{1,127},{2,4},{3,1},{4,6},{5,3},{6,8},{7,5},{8,10},{9,7},{10... | collective-permute-start | bytes 6291464 | tf_op jit(solution)/shard_map/ppermute | solution.py:27
  145.8 57.7 %collective-permute-start.15 = (bf16[256,4096]{1,0:T(8,128)(2,1)}, bf16[256,4096]{1,0:T(8,128)(2,1)}, u32[]{:S(2)}, u32[]{:S(2)}) collective-permute-start(bf16[256,4096]{1,0:T(8,128)(2,1)} %collective-permute-done.11), channel_id=1, source_target_pairs={{6,126},{7,127},{120,0},{121,1},{134,254},{135,255},{248,128},{249... | collective-permute-start | bytes 6291464 | tf_op jit(solution)/shard_map/ppermute | solution.py:27
  147.1 19.4 %collective-permute-start.13 = (bf16[256,2048]{1,0:T(8,128)(2,1)}, bf16[256,2048]{1,0:T(8,128)(2,1)}, u32[]{:S(2)}, u32[]{:S(2)}) collective-permute-start(bf16[256,2048]{1,0:T(8,128)(2,1)} %collective-permute-done.9), channel_id=1, source_target_pairs={{0,128},{1,129},{2,130},{3,131},{4,132},{5,133},{6,134},{7,135},{8... | collective-permute-start | bytes 3145736 | tf_op jit(solution)/shard_map/ppermute | solution.py:27
  148.5 17.9 %collective-permute-start.14 = (bf16[256,2048]{1,0:T(8,128)(2,1)}, bf16[256,2048]{1,0:T(8,128)(2,1)}, u32[]{:S(2)}, u32[]{:S(2)}) collective-permute-start(bf16[256,2048]{1,0:T(8,128)(2,1)} %collective-permute-done.10), channel_id=1, source_target_pairs={{0,129},{1,128},{2,131},{3,130},{4,133},{5,132},{6,135},{7,134},{8... | collective-permute-start | bytes 3145736 | tf_op jit(solution)/shard_map/ppermute | solution.py:27
  160.2 43.3 %copy-start.3 = (bf16[256,4096]{1,0:T(8,128)(2,1)S(1)}, bf16[256,4096]{1,0:T(8,128)(2,1)}, u32[]{:S(2)}) copy-start(bf16[256,4096]{1,0:T(8,128)(2,1)} %refs_26_.1) | copy-start | bytes 6291460
  160.2 43.3 %copy-start.17 = (f32[256,256]{1,0:T(8,128)S(1)}, f32[256,256]{1,0:T(8,128)}, u32[]{:S(2)}) copy-start(f32[256,256]{1,0:T(8,128)} %fusion.refs_2_) | copy-start | bytes 786436
  160.2 43.3 %copy-start.18 = (f32[256,256]{1,0:T(8,128)S(1)}, f32[256,256]{1,0:T(8,128)}, u32[]{:S(2)}) copy-start(f32[256,256]{1,0:T(8,128)} %fusion.1.refs_1_) | copy-start | bytes 786436
  211.3 13.1 %collective-permute-start.19 = (f32[2,256]{1,0:T(2,128)S(1)}, f32[2,256]{1,0:T(2,128)S(1)}, u32[]{:S(2)}, u32[]{:S(2)}) collective-permute-start(f32[2,256]{1,0:T(2,128)S(1)} %get-tuple-element.102.refs_20_), channel_id=1, source_target_pairs={{0,2},{1,3},{2,4},{3,5},{4,6},{5,7},{6,8},{7,9},{8,10},{9,11},{10,... | collective-permute-start | bytes 6152 | tf_op jit(solution)/shard_map/ppermute | solution.py:27
  211.3 13.1 %collective-permute-start.18 = (f32[2,256]{1,0:T(2,128)S(1)}, f32[2,256]{1,0:T(2,128)S(1)}, u32[]{:S(2)}, u32[]{:S(2)}) collective-permute-start(f32[2,256]{1,0:T(2,128)S(1)} %get-tuple-element.102.refs_20_), channel_id=1, source_target_pairs={{0,254},{1,255},{2,0},{3,1},{4,2},{5,3},{6,4},{7,5},{8,6},{9,7},{1... | collective-permute-start | bytes 6152 | tf_op jit(solution)/shard_map/ppermute | solution.py:27
  217.3 8.4 %collective-permute-start.17 = (f32[2,256]{1,0:T(2,128)S(1)}, f32[2,256]{1,0:T(2,128)S(1)}, u32[]{:S(2)}, u32[]{:S(2)}) collective-permute-start(f32[2,256]{1,0:T(2,128)S(1)} %get-tuple-element.102.refs_20_), channel_id=1, source_target_pairs={{0,1},{1,2},{2,3},{3,4},{4,5},{5,6},{6,7},{7,8},{8,9},{9,10},{10,1... | collective-permute-start | bytes 6152 | tf_op jit(solution)/shard_map/ppermute | solution.py:27
  219.0 6.8 %collective-permute-start.16 = (f32[2,256]{1,0:T(2,128)S(1)}, f32[2,256]{1,0:T(2,128)S(1)}, u32[]{:S(2)}, u32[]{:S(2)}) collective-permute-start(f32[2,256]{1,0:T(2,128)S(1)} %get-tuple-element.102.refs_20_), channel_id=1, source_target_pairs={{0,255},{1,0},{2,1},{3,2},{4,3},{5,4},{6,5},{7,6},{8,7},{9,8},{10,... | collective-permute-start | bytes 6152 | tf_op jit(solution)/shard_map/ppermute | solution.py:27
  (16 other events, 131.2 us)

commit v4 on v3

--- a/solution.py
+++ b/solution.py
@@ -11,8 +11,7 @@
 NEGATIVE = -1e30
 CHUNK = 512
 SLOTS = 4
-VMEM_LIMIT = 20 * 1024 * 1024
-SMALL_LIMIT = 14 * 1024 * 1024
+VMEM_LIMIT = 50 * 1024 * 1024
 
 
 def contract(left_rows, right_rows):
@@ -52,24 +51,46 @@
 
 
 def early_kernel(scale, place, pos, *refs):
-    qq, qd, dq, dd, qd_n2, dd_n2, dd_p2 = refs[:7]
-    own_q, own_d, q_n2, q_p2, q_pair, d_pair = refs[7:13]
-    qq_n2, dq_p2, qq_p2, qq_pair, cross_pair, dd_pair = refs[13:19]
-    q_max, q_sum, d_max, d_sum, positive = refs[19:]
+    qq, qd, dq, dd = refs[:4]
+    sources = refs[4:12]
+    qd_n2, dd_n2, dd_p2, qq_n2, dq_p2, qq_p2, qq_pair, cross_pair, dd_pair = refs[12:21]
+    q_max, q_sum, d_max, d_sum, positive = refs[21:26]
+    held, arrived = refs[26:]
     even, first, last = [place[k] == 1 for k in range(3)]
-    qq_pair[...] = scale * contract(own_q[...], q_pair[...])
-    dd_pair[...] = scale * contract(own_d[...], d_pair[...])
-    qq_n2[...] = scale * contract(own_q[...], q_n2[...])
-    qq_p2[...] = scale * contract(own_q[...], q_p2[...])
-    dq_p2[...] = scale * contract(own_d[...], q_p2[...])
+    copies = [
+        pltpu.make_async_copy(source, held.at[k], arrived.at[k])
+        for k, source in enumerate(sources)
+    ]
+    for copy in copies:
+        copy.start()
+    own_q, own_d, d_n2, d_p2, q_n2, q_p2, q_pair, d_pair = range(8)
+
+    def product(left, right):
+        return scale * contract(held[left], held[right])
+
+    for k in (own_q, own_d, d_n2):
+        copies[k].wait()
+    qd_n2[...] = product(own_q, d_n2)
+    dd_n2[...] = product(own_d, d_n2)
+    copies[d_p2].wait()
+    dd_p2[...] = product(own_d, d_p2)
+    copies[q_n2].wait()
+    qq_n2[...] = product(own_q, q_n2)
+    copies[q_p2].wait()
+    qq_p2[...] = product(own_q, q_p2)
+    dq_p2[...] = product(own_d, q_p2)
+    copies[q_pair].wait()
+    qq_pair[...] = product(own_q, q_pair)
+    copies[d_pair].wait()
+    dd_pair[...] = product(own_d, d_pair)
 
     @pl.when(even)
     def _():
-        cross_pair[...] = scale * contract(own_q[...], d_pair[...])
+        cross_pair[...] = product(own_q, d_pair)
 
     @pl.when(jnp.logical_not(even))
     def _():
-        cross_pair[...] = scale * contract(own_d[...], q_pair[...])
+        cross_pair[...] = product(own_d, q_pair)
 
     cross = cross_pair[...]
     q_tiles = [
@@ -98,32 +119,51 @@
     positive[...] = jnp.sum(jnp.where(doc == pos[...], dq[...], 0.0), axis=0, keepdims=True)
 
 
-def lse_kernel(scale, place, qq_edge, dq_edge, q_max, q_sum, d_max, d_sum, positive, *refs):
-    own_q, own_d, q_diag, d_low, d_high, q_swap = refs[:6]
-    qq_diag, cross_diag, dd_diag, qq_swap, dq_swap, lse, row_terms = refs[6:]
+def lse_kernel(scale, place, q_max, q_sum, d_max, d_sum, positive, *refs):
+    own_q, own_d, q_diag, q_edge, d_low, d_high, q_swap = refs[:7]
+    qq_diag, cross_diag, dd_diag, qq_swap, dq_swap, lse, row_terms = refs[7:14]
+    held, arrived = refs[14:]
     even, first, last, edge = [place[k] == 1 for k in range(4)]
     half = d_low.shape[1]
-
-    def with_documents(own):
-        return scale * (contract(own[:, :half], d_low[...]) + contract(own[:, half:], d_high[...]))
-
-    qq_diag[...] = jnp.where(edge, qq_edge[...], scale * contract(own_q[...], q_diag[...]))
-    dd_diag[...] = with_documents(own_d)
+    crossed = first | last
+
+    def copy(source, k, columns=slice(None)):
+        return pltpu.make_async_copy(source, held.at[k, :, columns], arrived.at[k])
+
+    low, high = slice(0, half), slice(half, 2 * half)
+    copy(own_d, 0).start()
+    copy(d_low, 1, low).start()
+    copy(d_high, 1, high).start()
+    copy(own_q, 2).start()
+    pl.when(edge)(lambda: copy(q_edge, 3).start())
+    pl.when(jnp.logical_not(edge))(lambda: copy(q_diag, 3).start())
+    pl.when(crossed)(lambda: copy(q_swap, 4).start())
+
+    def product(left, right):
+        return scale * contract(held[left], held[right])
+
+    copy(own_d, 0).wait()
+    copy(own_d, 1).wait()
+    dd_diag[...] = product(0, 1)
+    copy(own_q, 2).wait()
+    copy(q_diag, 3).wait()
+    qq_diag[...] = product(2, 3)
 
     @pl.when(even)
     def _():
-        cross_diag[...] = jnp.where(edge, dq_edge[...], scale * contract(own_d[...], q_diag[...]))
+        cross_diag[...] = product(0, 3)
 
     @pl.when(jnp.logical_not(even))
     def _():
-        cross_diag[...] = with_documents(own_q)
-
-    @pl.when(first | last)
-    def _():
-        qq_swap[...] = scale * contract(own_q[...], q_swap[...])
-        dq_swap[...] = scale * contract(own_d[...], q_swap[...])
-
-    @pl.when(jnp.logical_not(first | last))
+        cross_diag[...] = product(2, 1)
+
+    @pl.when(crossed)
+    def _():
+        copy(q_swap, 4).wait()
+        qq_swap[...] = product(2, 4)
+        dq_swap[...] = product(0, 4)
+
+    @pl.when(jnp.logical_not(crossed))
     def _():
         qq_swap[...] = jnp.full(qq_swap.shape, NEGATIVE, jnp.float32)
         dq_swap[...] = jnp.full(dq_swap.shape, NEGATIVE, jnp.float32)
@@ -286,12 +326,12 @@
 
     q_down = sent(queries, down)
     d_up = sent(documents, up)
-    d_p2 = sent(documents, lambda i: i + 2)
-    d_n2 = sent(documents, lambda i: i - 2)
-    q_edge = sent(
+    q_p2 = sent(queries, lambda i: i + 2, [i for i in range(count) if i % half < half - 2])
+    q_n2 = sent(queries, lambda i: i - 2, [i for i in range(count) if i % half >= 2])
+    q_swap = sent(
         queries,
-        lambda i: i - 1 if i % half == 0 else i + 1,
-        [0, half - 1, half, count - 1],
+        lambda i: i + half + (inner - 2 if i % half < 2 else 2 - inner),
+        [i for i in range(count) if i % half < 2 or i % half >= half - 2],
     )
     own_tiles = [
         masked(tile(queries, queries)),
@@ -302,29 +342,22 @@
     q_down, d_up, own_tiles = barrier((q_down, d_up, own_tiles))
     q_pair = sent(q_down, down)
     d_pair = sent(d_up, up)
-    q_own, q_edge = barrier((queries, q_edge))
-    q_p2 = sent(q_own, lambda i: i + 2, [i for i in range(count) if i % half < half - 2])
-    q_own, d_n2 = barrier((queries, d_n2))
-    q_n2 = sent(q_own, lambda i: i - 2, [i for i in range(count) if i % half >= 2])
-    q_own, d_p2, d_n2, q_down, d_up = barrier((queries, d_p2, d_n2, q_down, d_up))
-    crossing = [i for i in range(count) if i % half < 2 or i % half >= half - 2]
-    q_swap = sent(
-        q_own, lambda i: i + half + (inner - 2 if i % half < 2 else 2 - inner), crossing
-    )
-    far_tiles = [
-        tile(queries, d_n2),
-        tile(documents, d_n2),
-        tile(documents, d_p2),
-        tile(queries, q_edge),
-        tile(documents, q_edge),
-    ]
+    d_own, q_p2, q_n2, q_down, d_up = barrier((documents, q_p2, q_n2, q_down, d_up))
+    d_p2 = sent(d_own, lambda i: i + 2)
+    d_n2 = sent(d_own, lambda i: i - 2)
+    q_own, q_swap, q_p2, q_n2 = barrier((queries, q_swap, q_p2, q_n2))
+    q_edge = sent(
+        q_own,
+        lambda i: i - 1 if i % half == 0 else i + 1,
+        [0, half - 1, half, count - 1],
+    )
+    q_pair, d_pair = barrier((q_pair, d_pair))
+    q_diag = sent(q_pair, lambda i: i - i % half + (i + (-2 if i % 2 else 2)) % half)
+    d_p2, d_n2, q_pair, d_pair = barrier((d_p2, d_n2, q_pair, d_pair))
     cut = width // 2
     d_low = jnp.where(is_even, d_n2[:, :cut], d_p2[:, :cut])
     d_high = jnp.where(is_even, d_n2[:, cut:], d_p2[:, cut:])
-    d_low, d_high, q_pair, d_pair, q_p2, q_n2, far_tiles = barrier(
-        (d_low, d_high, q_pair, d_pair, q_p2, q_n2, far_tiles)
-    )
-    q_diag = sent(q_pair, lambda i: i - i % half + (i + (-2 if i % 2 else 2)) % half)
+    d_low, d_high, q_edge = barrier((d_low, d_high, q_edge))
     d_low = sent(d_low, up)
     d_high = sent(d_high, down)
     d_low, d_high, q_swap, q_pair, d_pair, q_p2, q_n2 = barrier(
@@ -350,27 +383,20 @@
 
     *early, q_max, q_sum, d_max, d_sum, positive = pl.pallas_call(
         early_tiles,
-        out_shape=(square,) * 6 + (column,) * 4 + (row,),
-        in_specs=[in_smem] + [in_vmem] * 14,
-        out_specs=(in_vmem,) * 11,
-        compiler_params=pltpu.CompilerParams(vmem_limit_bytes=SMALL_LIMIT),
+        out_shape=(square,) * 9 + (column,) * 4 + (row,),
+        in_specs=[in_smem] + [in_vmem] * 5 + [anywhere] * 8,
+        out_specs=(in_vmem,) * 14,
+        scratch_shapes=[
+            pltpu.VMEM((8, size, width), jnp.bfloat16),
+            pltpu.SemaphoreType.DMA((8,)),
+        ],
+        compiler_params=pltpu.CompilerParams(vmem_limit_bytes=VMEM_LIMIT),
         cost_estimate=pl.CostEstimate(
-            flops=12 * size * size * width,
-            bytes_accessed=12 * size * width,
+            flops=18 * size * size * width,
+            bytes_accessed=16 * size * width,
             transcendentals=14 * size * size,
         ),
-    )(
-        place,
-        pos,
-        *own_tiles,
-        *far_tiles[:3],
-        queries,
-        documents,
-        q_n2,
-        q_p2,
-        q_pair,
-        d_pair,
-    )
+    )(place, pos, *own_tiles, queries, documents, d_n2, d_p2, q_n2, q_p2, q_pair, d_pair)
 
     def last_tiles(*refs):
         lse_kernel(scale, *refs)
@@ -378,9 +404,13 @@
     *late, lse, row_terms = pl.pallas_call(
         last_tiles,
         out_shape=(square,) * 5 + (jax.ShapeDtypeStruct((2, size), jnp.float32), row),
-        in_specs=[in_smem] + [in_vmem] * 13,
+        in_specs=[in_smem] + [in_vmem] * 5 + [anywhere] * 7,
         out_specs=(in_vmem,) * 7,
-        compiler_params=pltpu.CompilerParams(vmem_limit_bytes=SMALL_LIMIT),
+        scratch_shapes=[
+            pltpu.VMEM((5, size, width), jnp.bfloat16),
+            pltpu.SemaphoreType.DMA((5,)),
+        ],
+        compiler_params=pltpu.CompilerParams(vmem_limit_bytes=VMEM_LIMIT),
         cost_estimate=pl.CostEstimate(
             flops=6 * size * size * width,
             bytes_accessed=8 * size * width,
@@ -388,8 +418,6 @@
         ),
     )(
         place,
-        far_tiles[3],
-        far_tiles[4],
         q_max,
         q_sum,
         d_max,
@@ -398,11 +426,12 @@
         queries,
         documents,
         q_diag,
+        q_edge,
         d_low,
         d_high,
         q_swap,
     )
-    tiles = [*own_tiles, *far_tiles[:3], *early, *late]
+    tiles = [*own_tiles, *early, *late]
     lse_n1 = sent(lse, lambda i: i - 1)
     lse_p1 = sent(lse, lambda i: i + 1)
     lse_n2 = sent(lse, lambda i: i - 2)

time: 240 us -> 243 us (1.012)
  starting transfers between devices: 42.4 us -> 56.5 us
  local copies, waits for them, and re-layouts: 13.7 us -> 4.84 us
  matrix products: 20.5 us -> 11.9 us
  Pallas kernels: 27.9 us -> 36.1 us
  waiting for transfers between devices: 132 us -> 129 us
    ppermute x20, starting transfers between devices: 42.4 us -> 56.5 us  [sent(): return lax.ppermute(value, AXES, [(i, target(i) % count) for i in senders])]
    dot_general x9 -> x4, matrix products: 20.5 us -> 11.9 us  [contract(): lax.dot_general(left_rows, right_rows, (((1,), (1,)), ((), ())), preferre...]
    unnamed x40 -> x18, local copies, waits for them, and re-layouts: 12.2 us -> 4.84 us
    pallas_call x1, Pallas kernels: 6.25 us -> 12.7 us  [per_device(): pl.pallas_call(early_tiles, out_shape=(square,) * 9 + (column,) * 4 + (ro...]
    ppermute x20, waiting for transfers between devices: 132 us -> 129 us  [sent(): return lax.ppermute(value, AXES, [(i, target(i) % count) for i in senders])]
  transfers between devices with their start and end apart: 20 -> 20, of which waited for: 10 -> 10; matrix products, arithmetic and copies ran while one was open for 10% -> 6% of each run, Pallas kernels for 3% -> 5%
where the time goes in v4:
time: 243 us; the launch traced here: 242 us
  waiting for transfers between devices  129 us (53%)
  starting transfers between devices  56.5 us (23%)
  Pallas kernels  36.1 us (15%)
  matrix products  11.9 us (5%)
  local copies, waits for them, and re-layouts  4.84 us (2%)
  other arithmetic  2.59 us (1%)
    ppermute x20, waiting for transfers between devices, sent(): return lax.ppermute(value, AXES, [(i, target(i) % count) for i in senders])  129 us
    ppermute x20, starting transfers between devices, sent(): return lax.ppermute(value, AXES, [(i, target(i) % count) for i in senders])  56.5 us
    pallas_call x1, Pallas kernels, per_device(): pl.pallas_call(kernel, grid=(parts,), out_shape=(jax.ShapeDtypeStruct((si...  15.2 us
    pallas_call x1, Pallas kernels, per_device(): pl.pallas_call(early_tiles, out_shape=(square,) * 9 + (column,) * 4 + (ro...  12.7 us
    dot_general x4, matrix products, contract(): lax.dot_general(left_rows, right_rows, (((1,), (1,)), ((), ())), preferre...  11.9 us
    pallas_call x1, Pallas kernels, per_device(): pl.pallas_call(last_tiles, out_shape=(square,) * 5 + (jax.ShapeDtypeStruc...  8.24 us
  transfers between devices with their start and end apart: 20, of which 10 were waited for; matrix products, arithmetic and copies ran while one was open for 6% of the time, Pallas kernels for 5%

profile of v4, /device:TPU:0, one launch (start us, length us, event | category | flops | bytes accessed | tf_op | source)
XLA Modules:
  0.0 242.0 jit_solution(2305745905945291661)
XLA Ops:
  0.7 3.2 %collective-permute-start = (bf16[256,4096]{1,0:T(8,128)(2,1)}, bf16[256,4096]{1,0:T(8,128)(2,1)}, u32[]{:S(2)}, u32[]{:S(2)}) collective-permute-start(bf16[256,4096]{1,0:T(8,128)(2,1)} %refs_25_.1), channel_id=1, source_target_pairs={{0,129},{1,128},{2,131},{3,130},{4,133},{5,132},{6,135},{7,134},{8... | collective-permute-start | bytes 6291464 | tf_op jit(solution)/shard_map/ppermute | solution.py:26
  5.2 4.7 %collective-permute-start.2 = (bf16[256,4096]{1,0:T(8,128)(2,1)}, bf16[256,4096]{1,0:T(8,128)(2,1)S(1)}, u32[]{:S(2)}, u32[]{:S(2)}) collective-permute-start(bf16[256,4096]{1,0:T(8,128)(2,1)} %refs_25_.1), channel_id=1, source_target_pairs={{0,2},{1,3},{2,4},{3,5},{4,6},{5,7},{6,8},{7,9},{8,10},{9,11},{10,... | collective-permute-start | bytes 6291464 | tf_op jit(solution)/shard_map/ppermute | solution.py:26
  9.9 4.9 %collective-permute-start.8 = (bf16[256,4096]{1,0:T(8,128)(2,1)}, bf16[256,4096]{1,0:T(8,128)(2,1)}, u32[]{:S(2)}, u32[]{:S(2)}) collective-permute-start(bf16[256,4096]{1,0:T(8,128)(2,1)} %refs_25_.1), channel_id=1, source_target_pairs={{0,134},{1,135},{126,248},{127,249},{128,6},{129,7},{254,120},{255... | collective-permute-start | bytes 6291464 | tf_op jit(solution)/shard_map/ppermute | solution.py:26
  14.8 3.0 %fusion.refs_5_ = f32[256,256]{1,0:T(8,128)S(1)} fusion(bf16[256,4096]{1,0:T(8,128)(2,1)} %refs_26_.1), kind=kOutput, calls=%fused_computation.1 | convolution fusion | flops 537067520 | bytes 2359296 | tf_op jit(solution)/shard_map/dot_general | solution.py:18
  17.8 3.0 %convolution_multiply_fusion.1.refs_4_ = f32[256,256]{1,0:T(8,128)S(1)} fusion(bf16[256,4096]{1,0:T(8,128)(2,1)} %refs_26_.1, bf16[256,4096]{1,0:T(8,128)(2,1)} %refs_25_.1), kind=kOutput, calls=%fused_computation.2 | convolution fusion | flops 536936448 | bytes 4456448 | tf_op jit(solution)/shard_map/dot_general | solution.py:18
  20.7 3.0 %convolution_multiply_fusion.2.refs_3_ = f32[256,256]{1,0:T(8,128)S(1)} fusion(bf16[256,4096]{1,0:T(8,128)(2,1)} %refs_25_.1, bf16[256,4096]{1,0:T(8,128)(2,1)} %refs_26_.1), kind=kOutput, calls=%fused_computation.3 | convolution fusion | flops 536936448 | bytes 4456448 | tf_op jit(solution)/shard_map/dot_general | solution.py:18
  23.7 3.0 %fusion.1.refs_2_ = f32[256,256]{1,0:T(8,128)S(1)} fusion(bf16[256,4096]{1,0:T(8,128)(2,1)} %refs_25_.1), kind=kOutput, calls=%fused_computation.5 | convolution fusion | flops 537067520 | bytes 2359296 | tf_op jit(solution)/shard_map/dot_general | solution.py:18
  26.7 21.3 %collective-permute-done.1 = bf16[256,4096]{1,0:T(8,128)(2,1)} collective-permute-done((bf16[256,4096]{1,0:T(8,128)(2,1)}, bf16[256,4096]{1,0:T(8,128)(2,1)}, u32[]{:S(2)}, u32[]{:S(2)}) %collective-permute-start.1) | collective-permute-done | bytes 2097184 | tf_op jit(solution)/shard_map/ppermute | solution.py:26
  48.0 3.0 %collective-permute-start.6 = (bf16[256,4096]{1,0:T(8,128)(2,1)}, bf16[256,4096]{1,0:T(8,128)(2,1)}, u32[]{:S(2)}, u32[]{:S(2)}) collective-permute-start(bf16[256,4096]{1,0:T(8,128)(2,1)} %collective-permute-done), channel_id=1, source_target_pairs={{0,129},{1,128},{2,131},{3,130},{4,133},{5,132},{6,135},{7,134},{8... | collective-permute-start | bytes 6291464 | tf_op jit(solution)/shard_map/ppermute | solution.py:26
  55.9 4.8 %collective-permute-start.5 = (bf16[256,4096]{1,0:T(8,128)(2,1)}, bf16[256,4096]{1,0:T(8,128)(2,1)S(1)}, u32[]{:S(2)}, u32[]{:S(2)}) collective-permute-start(bf16[256,4096]{1,0:T(8,128)(2,1)} %refs_26_.1), channel_id=1, source_target_pairs={{0,254},{1,255},{2,0},{3,1},{4,2},{5,3},{6,4},{7,5},{8,6},{9,7},{1... | collective-permute-start | bytes 6291464 | tf_op jit(solution)/shard_map/ppermute | solution.py:26
  60.7 36.8 %collective-permute-done.8 = bf16[256,4096]{1,0:T(8,128)(2,1)} collective-permute-done((bf16[256,4096]{1,0:T(8,128)(2,1)}, bf16[256,4096]{1,0:T(8,128)(2,1)}, u32[]{:S(2)}, u32[]{:S(2)}) %collective-permute-start.8) | collective-permute-done | bytes 2097184 | tf_op jit(solution)/shard_map/ppermute | solution.py:26
  97.6 13.5 %collective-permute-start.9 = (bf16[256,4096]{1,0:T(8,128)(2,1)}, bf16[256,4096]{1,0:T(8,128)(2,1)}, u32[]{:S(2)}, u32[]{:S(2)}) collective-permute-start(bf16[256,4096]{1,0:T(8,128)(2,1)} %refs_25_.1), channel_id=1, source_target_pairs={{0,255},{127,128},{128,127},{255,0}} | collective-permute-start | bytes 6291464 | tf_op jit(solution)/shard_map/ppermute | solution.py:26
  111.1 5.6 %collective-permute-done.6.refs_12_.refs_31_ = bf16[256,4096]{1,0:T(8,128)(2,1)} collective-permute-done((bf16[256,4096]{1,0:T(8,128)(2,1)}, bf16[256,4096]{1,0:T(8,128)(2,1)}, u32[]{:S(2)}, u32[]{:S(2)}) %collective-permute-start.6) | collective-permute-done | bytes 2097184 | tf_op jit(solution)/shard_map/ppermute | solution.py:26
  119.3 15.9 %collective-permute-done.9.refs_9_.refs_33_ = bf16[256,4096]{1,0:T(8,128)(2,1)} collective-permute-done((bf16[256,4096]{1,0:T(8,128)(2,1)}, bf16[256,4096]{1,0:T(8,128)(2,1)}, u32[]{:S(2)}, u32[]{:S(2)}) %collective-permute-start.9) | collective-permute-done | bytes 2097184 | tf_op jit(solution)/shard_map/ppermute | solution.py:26
  135.4 3.1 %collective-permute-start.11 = (bf16[256,2048]{1,0:T(8,128)(2,1)S(1)}, bf16[256,2048]{1,0:T(8,128)(2,1)}, u32[]{:S(2)}, u32[]{:S(2)}) collective-permute-start(bf16[256,2048]{1,0:T(8,128)(2,1)S(1)} %get-tuple-element.70), channel_id=1, source_target_pairs={{0,129},{1,128},{2,131},{3,130},{4,133},{5,132},{6,135},{7,134},{8... | collective-permute-start | bytes 3145736 | tf_op jit(solution)/shard_map/ppermute | solution.py:26
  138.5 17.0 %collective-permute-done.10 = bf16[256,2048]{1,0:T(8,128)(2,1)} collective-permute-done((bf16[256,2048]{1,0:T(8,128)(2,1)S(1)}, bf16[256,2048]{1,0:T(8,128)(2,1)}, u32[]{:S(2)}, u32[]{:S(2)}) %collective-permute-start.10) | collective-permute-done | bytes 1048608 | tf_op jit(solution)/shard_map/ppermute | solution.py:26
  156.8 2.7 %collective-permute-start.13 = (bf16[256,2048]{1,0:T(8,128)(2,1)}, bf16[256,2048]{1,0:T(8,128)(2,1)S(1)}, u32[]{:S(2)}, u32[]{:S(2)}) collective-permute-start(bf16[256,2048]{1,0:T(8,128)(2,1)} %collective-permute-done.10), channel_id=1, source_target_pairs={{0,128},{1,129},{2,130},{3,131},{4,132},{5,133},{6,134},{7,135},{8... | collective-permute-start | bytes 3145736 | tf_op jit(solution)/shard_map/ppermute | solution.py:26
  160.2 12.7 %shard_map.58 = (f32[256,256]{1,0:T(8,128)S(1)}, f32[256,256]{1,0:T(8,128)S(1)}, f32[256,256]{1,0:T(8,128)S(1)}, f32[256,256]{1,0:T(8,128)S(1)}, f32[256,256]{1,...) custom-call(s32[4]{0:T(128)S(1)} %add_convert_fusion.refs_0_, ...), custom_call_target="tpu_custom_call" | custom-call | flops 4831838208 | bytes 16777216 | tf_op jit(solution)/shard_map/pallas_call | solution.py:384
  172.9 7.0 %collective-permute-done.13.refs_10_.refs_34_ = bf16[256,2048]{1,0:T(8,128)(2,1)S(1)} collective-permute-done((bf16[256,2048]{1,0:T(8,128)(2,1)}, bf16[256,2048]{1,0:T(8,128)(2,1)S(1)}, u32[]{:S(2)}, u32[]{:S(2)}) %collective-permute-start.13) | collective-permute-done | bytes 1048608 | tf_op jit(solution)/shard_map/ppermute | solution.py:26
  179.9 21.9 %collective-permute-done.15.refs_12_.refs_37_ = bf16[256,4096]{1,0:T(8,128)(2,1)} collective-permute-done((bf16[256,4096]{1,0:T(8,128)(2,1)}, bf16[256,4096]{1,0:T(8,128)(2,1)}, u32[]{:S(2)}, u32[]{:S(2)}) %collective-permute-start.15) | collective-permute-done | bytes 2097184 | tf_op jit(solution)/shard_map/ppermute | solution.py:26
  201.8 8.2 %shard_map.59 = (f32[256,256]{1,0:T(8,128)S(1)}, f32[256,256]{1,0:T(8,128)S(1)}, f32[256,256]{1,0:T(8,128)S(1)}, f32[256,256]{1,0:T(8,128)S(1)}, f32[256,256]{1,...) custom-call(s32[4]{0:T(128)S(1)} %add_convert_fusion.refs_0_, f32[256,128]{1,0:T(8,128)S(1)} %get-tuple-element.80.refs_1_, ...), custom_call_target="tpu_custom_call" | custom-call | flops 1610612736 | bytes 8388608 | tf_op jit(solution)/shard_map/pallas_call | solution.py:404
  212.2 6.0 %collective-permute-start.18 = (f32[2,256]{1,0:T(2,128)S(1)}, f32[2,256]{1,0:T(2,128)S(1)}, u32[]{:S(2)}, u32[]{:S(2)}) collective-permute-start(f32[2,256]{1,0:T(2,128)S(1)} %get-tuple-element.104.refs_20_), channel_id=1, source_target_pairs={{0,254},{1,255},{2,0},{3,1},{4,2},{5,3},{6,4},{7,5},{8,6},{9,7},{1... | collective-permute-start | bytes 6152 | tf_op jit(solution)/shard_map/ppermute | solution.py:26
  219.7 5.7 %collective-permute-start.16 = (f32[2,256]{1,0:T(2,128)S(1)}, f32[2,256]{1,0:T(2,128)S(1)}, u32[]{:S(2)}, u32[]{:S(2)}) collective-permute-start(f32[2,256]{1,0:T(2,128)S(1)} %get-tuple-element.104.refs_20_), channel_id=1, source_target_pairs={{0,255},{1,0},{2,1},{3,2},{4,3},{5,4},{6,5},{7,6},{8,7},{9,8},{10,... | collective-permute-start | bytes 6152 | tf_op jit(solution)/shard_map/ppermute | solution.py:26
  226.7 15.2 %shard_map.60 = (f32[256,4096]{1,0:T(8,128)}, f32[256,4096]{1,0:T(8,128)}) custom-call(s32[4]{0:T(128)S(1)} %add_convert_fusion.refs_0_, s32[1,256]{1,0:T(1,128)S(1)} %bitcast.15, f32[256,256]{1,0:T(8,128)S(1)} %fusion.1.refs_2_, f32[256,256]{1,0:T(8,128)S(1)} %convolution_multiply_fusion.2.refs_3_, f32[256,256]{1,0:T(8,128)S(1)} %convolution_multiply_fusion.1.refs_4_, ...), custom_call_target="tpu_custom_call" | custom-call | flops 8589934592 | bytes 29360128 | tf_op jit(solution)/shard_map/pallas_call | solution.py:447
  (44 shorter events, 15.9 us)
Async XLA Ops:
  0.6 47.3 %collective-permute-start.1 = (bf16[256,4096]{1,0:T(8,128)(2,1)}, bf16[256,4096]{1,0:T(8,128)(2,1)}, u32[]{:S(2)}, u32[]{:S(2)}) collective-permute-start(bf16[256,4096]{1,0:T(8,128)(2,1)} %refs_26_.1), channel_id=1, source_target_pairs={{0,128},{1,129},{2,130},{3,131},{4,132},{5,133},{6,134},{7,135},{8... | collective-permute-start | bytes 6291464 | tf_op jit(solution)/shard_map/ppermute | solution.py:26
  0.7 47.2 %collective-permute-start = (bf16[256,4096]{1,0:T(8,128)(2,1)}, bf16[256,4096]{1,0:T(8,128)(2,1)}, u32[]{:S(2)}, u32[]{:S(2)}) collective-permute-start(bf16[256,4096]{1,0:T(8,128)(2,1)} %refs_25_.1), channel_id=1, source_target_pairs={{0,129},{1,128},{2,131},{3,130},{4,133},{5,132},{6,135},{7,134},{8... | collective-permute-start | bytes 6291464 | tf_op jit(solution)/shard_map/ppermute | solution.py:26
  3.9 47.3 %collective-permute-start.3 = (bf16[256,4096]{1,0:T(8,128)(2,1)}, bf16[256,4096]{1,0:T(8,128)(2,1)S(1)}, u32[]{:S(2)}, u32[]{:S(2)}) collective-permute-start(bf16[256,4096]{1,0:T(8,128)(2,1)} %refs_25_.1), channel_id=1, source_target_pairs={{2,0},{3,1},{4,2},{5,3},{6,4},{7,5},{8,6},{9,7},{10,8},{11,9},{12,... | collective-permute-start | bytes 6291464 | tf_op jit(solution)/shard_map/ppermute | solution.py:26
  5.2 49.3 %collective-permute-start.2 = (bf16[256,4096]{1,0:T(8,128)(2,1)}, bf16[256,4096]{1,0:T(8,128)(2,1)S(1)}, u32[]{:S(2)}, u32[]{:S(2)}) collective-permute-start(bf16[256,4096]{1,0:T(8,128)(2,1)} %refs_25_.1), channel_id=1, source_target_pairs={{0,2},{1,3},{2,4},{3,5},{4,6},{5,7},{6,8},{7,9},{8,10},{9,11},{10,... | collective-permute-start | bytes 6291464 | tf_op jit(solution)/shard_map/ppermute | solution.py:26
  9.9 87.6 %collective-permute-start.8 = (bf16[256,4096]{1,0:T(8,128)(2,1)}, bf16[256,4096]{1,0:T(8,128)(2,1)}, u32[]{:S(2)}, u32[]{:S(2)}) collective-permute-start(bf16[256,4096]{1,0:T(8,128)(2,1)} %refs_25_.1), channel_id=1, source_target_pairs={{0,134},{1,135},{126,248},{127,249},{128,6},{129,7},{254,120},{255... | collective-permute-start | bytes 6291464 | tf_op jit(solution)/shard_map/ppermute | solution.py:26
  48.0 68.8 %collective-permute-start.6 = (bf16[256,4096]{1,0:T(8,128)(2,1)}, bf16[256,4096]{1,0:T(8,128)(2,1)}, u32[]{:S(2)}, u32[]{:S(2)}) collective-permute-start(bf16[256,4096]{1,0:T(8,128)(2,1)} %collective-permute-done), channel_id=1, source_target_pairs={{0,129},{1,128},{2,131},{3,130},{4,133},{5,132},{6,135},{7,134},{8... | collective-permute-start | bytes 6291464 | tf_op jit(solution)/shard_map/ppermute | solution.py:26
  51.0 65.8 %collective-permute-start.7 = (bf16[256,4096]{1,0:T(8,128)(2,1)}, bf16[256,4096]{1,0:T(8,128)(2,1)}, u32[]{:S(2)}, u32[]{:S(2)}) collective-permute-start(bf16[256,4096]{1,0:T(8,128)(2,1)} %collective-permute-done.1), channel_id=1, source_target_pairs={{0,128},{1,129},{2,130},{3,131},{4,132},{5,133},{6,134},{7,135},{8... | collective-permute-start | bytes 6291464 | tf_op jit(solution)/shard_map/ppermute | solution.py:26
  55.9 60.8 %collective-permute-start.5 = (bf16[256,4096]{1,0:T(8,128)(2,1)}, bf16[256,4096]{1,0:T(8,128)(2,1)S(1)}, u32[]{:S(2)}, u32[]{:S(2)}) collective-permute-start(bf16[256,4096]{1,0:T(8,128)(2,1)} %refs_26_.1), channel_id=1, source_target_pairs={{0,254},{1,255},{2,0},{3,1},{4,2},{5,3},{6,4},{7,5},{8,6},{9,7},{1... | collective-permute-start | bytes 6291464 | tf_op jit(solution)/shard_map/ppermute | solution.py:26
  60.7 56.0 %collective-permute-start.4 = (bf16[256,4096]{1,0:T(8,128)(2,1)}, bf16[256,4096]{1,0:T(8,128)(2,1)}, u32[]{:S(2)}, u32[]{:S(2)}) collective-permute-start(bf16[256,4096]{1,0:T(8,128)(2,1)} %refs_26_.1), channel_id=1, source_target_pairs={{0,2},{1,3},{2,4},{3,5},{4,6},{5,7},{6,8},{7,9},{8,10},{9,11},{10,... | collective-permute-start | bytes 6291464 | tf_op jit(solution)/shard_map/ppermute | solution.py:26
  97.6 37.7 %collective-permute-start.9 = (bf16[256,4096]{1,0:T(8,128)(2,1)}, bf16[256,4096]{1,0:T(8,128)(2,1)}, u32[]{:S(2)}, u32[]{:S(2)}) collective-permute-start(bf16[256,4096]{1,0:T(8,128)(2,1)} %refs_25_.1), channel_id=1, source_target_pairs={{0,255},{127,128},{128,127},{255,0}} | collective-permute-start | bytes 6291464 | tf_op jit(solution)/shard_map/ppermute | solution.py:26
  111.1 49.1 %copy-start.6 = (s32[256]{0:T(256)S(1)}, s32[256]{0:T(256)}, u32[]{:S(2)}) copy-start(s32[256]{0:T(256)} %param.5) | copy-start | bytes 3076
  116.8 2.5 %copy-start.5 = (bf16[256,4096]{1,0:T(8,128)(2,1)}, bf16[256,4096]{1,0:T(8,128)(2,1)S(1)}, u32[]{:S(2)}) copy-start(bf16[256,4096]{1,0:T(8,128)(2,1)S(1)} %collective-permute-done.5.refs_8_.refs_28_) | copy-start | bytes 6291460
  135.2 20.3 %collective-permute-start.10 = (bf16[256,2048]{1,0:T(8,128)(2,1)S(1)}, bf16[256,2048]{1,0:T(8,128)(2,1)}, u32[]{:S(2)}, u32[]{:S(2)}) collective-permute-start(bf16[256,2048]{1,0:T(8,128)(2,1)S(1)} %get-tuple-element.69), channel_id=1, source_target_pairs={{0,128},{1,129},{2,130},{3,131},{4,132},{5,133},{6,134},{7,135},{8... | collective-permute-start | bytes 3145736 | tf_op jit(solution)/shard_map/ppermute | solution.py:26
  135.4 20.1 %collective-permute-start.11 = (bf16[256,2048]{1,0:T(8,128)(2,1)S(1)}, bf16[256,2048]{1,0:T(8,128)(2,1)}, u32[]{:S(2)}, u32[]{:S(2)}) collective-permute-start(bf16[256,2048]{1,0:T(8,128)(2,1)S(1)} %get-tuple-element.70), channel_id=1, source_target_pairs={{0,129},{1,128},{2,131},{3,130},{4,133},{5,132},{6,135},{7,134},{8... | collective-permute-start | bytes 3145736 | tf_op jit(solution)/shard_map/ppermute | solution.py:26
  138.5 34.4 %collective-permute-start.12 = (bf16[256,4096]{1,0:T(8,128)(2,1)}, bf16[256,4096]{1,0:T(8,128)(2,1)}, u32[]{:S(2)}, u32[]{:S(2)}) collective-permute-start(bf16[256,4096]{1,0:T(8,128)(2,1)} %collective-permute-done.6.refs_12_.refs_31_), channel_id=1, source_target_pairs={{0,2},{1,127},{2,4},{3,1},{4,6},{5,3},{6,8},{7,5},{8,10},{9,7},{10... | collective-permute-start | bytes 6291464 | tf_op jit(solution)/shard_map/ppermute | solution.py:26
  155.5 46.3 %collective-permute-start.15 = (bf16[256,4096]{1,0:T(8,128)(2,1)}, bf16[256,4096]{1,0:T(8,128)(2,1)}, u32[]{:S(2)}, u32[]{:S(2)}) collective-permute-start(bf16[256,4096]{1,0:T(8,128)(2,1)} %collective-permute-done.8), channel_id=1, source_target_pairs={{6,126},{7,127},{120,0},{121,1},{134,254},{135,255},{248,128},{249... | collective-permute-start | bytes 6291464 | tf_op jit(solution)/shard_map/ppermute | solution.py:26
  156.8 23.1 %collective-permute-start.13 = (bf16[256,2048]{1,0:T(8,128)(2,1)}, bf16[256,2048]{1,0:T(8,128)(2,1)S(1)}, u32[]{:S(2)}, u32[]{:S(2)}) collective-permute-start(bf16[256,2048]{1,0:T(8,128)(2,1)} %collective-permute-done.10), channel_id=1, source_target_pairs={{0,128},{1,129},{2,130},{3,131},{4,132},{5,133},{6,134},{7,135},{8... | collective-permute-start | bytes 3145736 | tf_op jit(solution)/shard_map/ppermute | solution.py:26
  159.5 20.4 %collective-permute-start.14 = (bf16[256,2048]{1,0:T(8,128)(2,1)}, bf16[256,2048]{1,0:T(8,128)(2,1)S(1)}, u32[]{:S(2)}, u32[]{:S(2)}) collective-permute-start(bf16[256,2048]{1,0:T(8,128)(2,1)} %collective-permute-done.11), channel_id=1, source_target_pairs={{0,129},{1,128},{2,131},{3,130},{4,133},{5,132},{6,135},{7,134},{8... | collective-permute-start | bytes 3145736 | tf_op jit(solution)/shard_map/ppermute | solution.py:26
  179.9 30.2 %copy-start = (bf16[256,2048]{1,0:T(8,128)(2,1)}, bf16[256,2048]{1,0:T(8,128)(2,1)S(1)}, u32[]{:S(2)}) copy-start(bf16[256,2048]{1,0:T(8,128)(2,1)S(1)} %collective-permute-done.13.refs_10_.refs_34_) | copy-start | bytes 3145732
  179.9 30.2 %copy-start.1 = (bf16[256,2048]{1,0:T(8,128)(2,1)}, bf16[256,2048]{1,0:T(8,128)(2,1)S(1)}, u32[]{:S(2)}) copy-start(bf16[256,2048]{1,0:T(8,128)(2,1)S(1)} %collective-permute-done.14.refs_11_.refs_35_) | copy-start | bytes 3145732
  212.2 13.1 %collective-permute-start.19 = (f32[2,256]{1,0:T(2,128)S(1)}, f32[2,256]{1,0:T(2,128)S(1)}, u32[]{:S(2)}, u32[]{:S(2)}) collective-permute-start(f32[2,256]{1,0:T(2,128)S(1)} %get-tuple-element.104.refs_20_), channel_id=1, source_target_pairs={{0,2},{1,3},{2,4},{3,5},{4,6},{5,7},{6,8},{7,9},{8,10},{9,11},{10,... | collective-permute-start | bytes 6152 | tf_op jit(solution)/shard_map/ppermute | solution.py:26
  212.2 13.1 %collective-permute-start.18 = (f32[2,256]{1,0:T(2,128)S(1)}, f32[2,256]{1,0:T(2,128)S(1)}, u32[]{:S(2)}, u32[]{:S(2)}) collective-permute-start(f32[2,256]{1,0:T(2,128)S(1)} %get-tuple-element.104.refs_20_), channel_id=1, source_target_pairs={{0,254},{1,255},{2,0},{3,1},{4,2},{5,3},{6,4},{7,5},{8,6},{9,7},{1... | collective-permute-start | bytes 6152 | tf_op jit(solution)/shard_map/ppermute | solution.py:26
  218.2 8.4 %collective-permute-start.17 = (f32[2,256]{1,0:T(2,128)S(1)}, f32[2,256]{1,0:T(2,128)S(1)}, u32[]{:S(2)}, u32[]{:S(2)}) collective-permute-start(f32[2,256]{1,0:T(2,128)S(1)} %get-tuple-element.104.refs_20_), channel_id=1, source_target_pairs={{0,1},{1,2},{2,3},{3,4},{4,5},{5,6},{6,7},{7,8},{8,9},{9,10},{10,1... | collective-permute-start | bytes 6152 | tf_op jit(solution)/shard_map/ppermute | solution.py:26
  219.7 7.0 %collective-permute-start.16 = (f32[2,256]{1,0:T(2,128)S(1)}, f32[2,256]{1,0:T(2,128)S(1)}, u32[]{:S(2)}, u32[]{:S(2)}) collective-permute-start(f32[2,256]{1,0:T(2,128)S(1)} %get-tuple-element.104.refs_20_), channel_id=1, source_target_pairs={{0,255},{1,0},{2,1},{3,2},{4,3},{5,4},{6,5},{7,6},{8,7},{9,8},{10,... | collective-permute-start | bytes 6152 | tf_op jit(solution)/shard_map/ppermute | solution.py:26
  (5 other events, 4.8 us)

commit v5 on v3

--- a/solution.py
+++ b/solution.py
@@ -11,8 +11,8 @@
 NEGATIVE = -1e30
 CHUNK = 512
 SLOTS = 4
-VMEM_LIMIT = 20 * 1024 * 1024
-SMALL_LIMIT = 14 * 1024 * 1024
+VMEM_LIMIT = 46 * 1024 * 1024
+SMALL_LIMIT = 16 * 1024 * 1024
 
 
 def contract(left_rows, right_rows):
@@ -100,30 +100,43 @@
 
 def lse_kernel(scale, place, qq_edge, dq_edge, q_max, q_sum, d_max, d_sum, positive, *refs):
     own_q, own_d, q_diag, d_low, d_high, q_swap = refs[:6]
-    qq_diag, cross_diag, dd_diag, qq_swap, dq_swap, lse, row_terms = refs[6:]
+    qq_diag, cross_diag, dd_diag, qq_swap, dq_swap, lse, row_terms = refs[6:13]
+    held, arrived = refs[13:]
     even, first, last, edge = [place[k] == 1 for k in range(4)]
     half = d_low.shape[1]
-
-    def with_documents(own):
-        return scale * (contract(own[:, :half], d_low[...]) + contract(own[:, half:], d_high[...]))
-
-    qq_diag[...] = jnp.where(edge, qq_edge[...], scale * contract(own_q[...], q_diag[...]))
-    dd_diag[...] = with_documents(own_d)
+    crossed = first | last
+
+    def copy(source, k, columns=slice(None)):
+        return pltpu.make_async_copy(source, held.at[k, :, columns], arrived.at[k])
+
+    copy(d_low, 0, slice(0, half)).start()
+    copy(d_high, 0, slice(half, 2 * half)).start()
+    copy(q_diag, 1).start()
+    pl.when(crossed)(lambda: copy(q_swap, 2).start())
+
+    def product(own, k):
+        return scale * contract(own[...], held[k])
+
+    pltpu.make_async_copy(held.at[0], held.at[0], arrived.at[0]).wait()
+    dd_diag[...] = product(own_d, 0)
+    copy(q_diag, 1).wait()
+    qq_diag[...] = jnp.where(edge, qq_edge[...], product(own_q, 1))
 
     @pl.when(even)
     def _():
-        cross_diag[...] = jnp.where(edge, dq_edge[...], scale * contract(own_d[...], q_diag[...]))
+        cross_diag[...] = jnp.where(edge, dq_edge[...], product(own_d, 1))
 
     @pl.when(jnp.logical_not(even))
     def _():
-        cross_diag[...] = with_documents(own_q)
-
-    @pl.when(first | last)
-    def _():
-        qq_swap[...] = scale * contract(own_q[...], q_swap[...])
-        dq_swap[...] = scale * contract(own_d[...], q_swap[...])
-
-    @pl.when(jnp.logical_not(first | last))
+        cross_diag[...] = product(own_q, 0)
+
+    @pl.when(crossed)
+    def _():
+        copy(q_swap, 2).wait()
+        qq_swap[...] = product(own_q, 2)
+        dq_swap[...] = product(own_d, 2)
+
+    @pl.when(jnp.logical_not(crossed))
     def _():
         qq_swap[...] = jnp.full(qq_swap.shape, NEGATIVE, jnp.float32)
         dq_swap[...] = jnp.full(dq_swap.shape, NEGATIVE, jnp.float32)
@@ -157,7 +170,7 @@
     lse, lse_n1, lse_p1, lse_n2, lse_p2 = refs[:5]
     own_q, own_d, q_n2, d_n2, q_p2, d_p2, q_pair, d_pair = refs[5:13]
     q_edge, d_low, d_high, q_diag, q_swap = refs[13:18]
-    grad_q, grad_d, coef_q, coef_d, rows, arrived = refs[18:]
+    grad_q, grad_d, coef_both, coef_q, coef_d, rows, arrived = refs[18:]
     step = pl.program_id(0)
     size = grad_q.shape[0]
     width = own_q.shape[1]
@@ -216,7 +229,14 @@
             value = jnp.exp(tile - column) + jnp.exp(tile - row)
             if taken is not None:
                 value = value - jnp.where(taken, 2.0, 0.0)
-            target[:, slot * size : (slot + 1) * size] = value.astype(jnp.bfloat16)
+            taken_rows = slice(0, size)
+            if target is coef_q and slot >= 2:
+                target, slot = coef_both, slot - 2
+            elif target is coef_d and slot < 6:
+                target, taken_rows = coef_both, slice(size, 2 * size)
+            elif target is coef_d:
+                slot = slot - 6
+            target[taken_rows, slot * size : (slot + 1) * size] = value.astype(jnp.bfloat16)
 
         def q_of(ref):
             return ref[0:1, :]
@@ -250,13 +270,14 @@
 
     held = step % SLOTS
     pltpu.make_async_copy(rows.at[held], rows.at[held], arrived.at[held]).wait()
-    depth = coef_q.shape[1]
-    grad_q[...] = factor * jnp.dot(
-        coef_q[...], rows[held, 0:depth, :], preferred_element_type=jnp.float32
-    )
-    grad_d[...] = factor * jnp.dot(
-        coef_d[...], rows[held, 2 * size :, :], preferred_element_type=jnp.float32
-    )
+    lone = 2 * size
+    both = jnp.dot(
+        coef_both[...], rows[held, lone : 4 * lone, :], preferred_element_type=jnp.float32
+    )
+    only_q = jnp.dot(coef_q[...], rows[held, 0:lone, :], preferred_element_type=jnp.float32)
+    only_d = jnp.dot(coef_d[...], rows[held, 4 * lone :, :], preferred_element_type=jnp.float32)
+    grad_q[...] = factor * (both[:size] + only_q)
+    grad_d[...] = factor * (both[size:] + only_d)
 
 
 def per_device(queries, documents, positives):
@@ -302,15 +323,13 @@
     q_down, d_up, own_tiles = barrier((q_down, d_up, own_tiles))
     q_pair = sent(q_down, down)
     d_pair = sent(d_up, up)
-    q_own, q_edge = barrier((queries, q_edge))
-    q_p2 = sent(q_own, lambda i: i + 2, [i for i in range(count) if i % half < half - 2])
-    q_own, d_n2 = barrier((queries, d_n2))
-    q_n2 = sent(q_own, lambda i: i - 2, [i for i in range(count) if i % half >= 2])
-    q_own, d_p2, d_n2, q_down, d_up = barrier((queries, d_p2, d_n2, q_down, d_up))
+    q_own, d_p2, d_n2, q_edge, q_down, d_up = barrier((queries, d_p2, d_n2, q_edge, q_down, d_up))
     crossing = [i for i in range(count) if i % half < 2 or i % half >= half - 2]
     q_swap = sent(
         q_own, lambda i: i + half + (inner - 2 if i % half < 2 else 2 - inner), crossing
     )
+    q_p2 = sent(q_own, lambda i: i + 2, [i for i in range(count) if i % half < half - 2])
+    q_n2 = sent(q_own, lambda i: i - 2, [i for i in range(count) if i % half >= 2])
     far_tiles = [
         tile(queries, d_n2),
         tile(documents, d_n2),
@@ -321,14 +340,16 @@
     cut = width // 2
     d_low = jnp.where(is_even, d_n2[:, :cut], d_p2[:, :cut])
     d_high = jnp.where(is_even, d_n2[:, cut:], d_p2[:, cut:])
-    d_low, d_high, q_pair, d_pair, q_p2, q_n2, far_tiles = barrier(
-        (d_low, d_high, q_pair, d_pair, q_p2, q_n2, far_tiles)
-    )
-    q_diag = sent(q_pair, lambda i: i - i % half + (i + (-2 if i % 2 else 2)) % half)
+    d_low, d_high, q_pair, d_pair, far_tiles = barrier((d_low, d_high, q_pair, d_pair, far_tiles))
     d_low = sent(d_low, up)
     d_high = sent(d_high, down)
-    d_low, d_high, q_swap, q_pair, d_pair, q_p2, q_n2 = barrier(
-        (d_low, d_high, q_swap, q_pair, d_pair, q_p2, q_n2)
+    q_diag = sent(
+        q_pair,
+        lambda i: i - 2 if i % 2 else i + 2,
+        [i for i in range(count) if i % half != 1 and i % half != half - 2],
+    )
+    d_low, d_high, q_pair, d_pair, q_p2, q_n2 = barrier(
+        (d_low, d_high, q_pair, d_pair, q_p2, q_n2)
     )
     d_low = sent(d_low, up)
     d_high = sent(d_high, down)
@@ -378,9 +399,13 @@
     *late, lse, row_terms = pl.pallas_call(
         last_tiles,
         out_shape=(square,) * 5 + (jax.ShapeDtypeStruct((2, size), jnp.float32), row),
-        in_specs=[in_smem] + [in_vmem] * 13,
+        in_specs=[in_smem] + [in_vmem] * 9 + [anywhere] * 4,
         out_specs=(in_vmem,) * 7,
-        compiler_params=pltpu.CompilerParams(vmem_limit_bytes=SMALL_LIMIT),
+        scratch_shapes=[
+            pltpu.VMEM((3, size, width), jnp.bfloat16),
+            pltpu.SemaphoreType.DMA((3,)),
+        ],
+        compiler_params=pltpu.CompilerParams(vmem_limit_bytes=VMEM_LIMIT),
         cost_estimate=pl.CostEstimate(
             flops=6 * size * size * width,
             bytes_accessed=8 * size * width,
@@ -422,8 +447,9 @@
         in_specs=[in_smem] + [in_vmem] * (6 + TILES) + [anywhere] * len(sources),
         out_specs=(grad_block, grad_block),
         scratch_shapes=[
-            pltpu.VMEM((size, 8 * size), jnp.bfloat16),
-            pltpu.VMEM((size, 8 * size), jnp.bfloat16),
+            pltpu.VMEM((2 * size, 6 * size), jnp.bfloat16),
+            pltpu.VMEM((size, 2 * size), jnp.bfloat16),
+            pltpu.VMEM((size, 2 * size), jnp.bfloat16),
             pltpu.VMEM((SLOTS, 10 * size, CHUNK), jnp.bfloat16),
             pltpu.SemaphoreType.DMA((SLOTS,)),
         ],

time: 240 us -> 226 us (0.942)
  waiting for transfers between devices: 132 us -> 102 us
  starting transfers between devices: 42.4 us -> 54.3 us
    ppermute x20, waiting for transfers between devices: 132 us -> 102 us  [sent(): return lax.ppermute(value, AXES, [(i, target(i) % count) for i in senders])]
    ppermute x20, starting transfers between devices: 42.4 us -> 54.3 us  [sent(): return lax.ppermute(value, AXES, [(i, target(i) % count) for i in senders])]
    unnamed x40 -> x32, local copies, waits for them, and re-layouts: 12.2 us -> 12.7 us
  transfers between devices with their start and end apart: 20 -> 20, of which waited for: 10 -> 9; matrix products, arithmetic and copies ran while one was open for 10% -> 11% of each run, Pallas kernels for 3% -> 3%
where the time goes in v5:
time: 226 us; the launch traced here: 224 us
  waiting for transfers between devices  102 us (45%)
  starting transfers between devices  54.3 us (24%)
  Pallas kernels  30 us (13%)
  matrix products  20.5 us (9%)
  local copies, waits for them, and re-layouts  14.1 us (6%)
  other arithmetic  2.47 us (1%)
    ppermute x20, waiting for transfers between devices, sent(): return lax.ppermute(value, AXES, [(i, target(i) % count) for i in senders])  102 us
    ppermute x20, starting transfers between devices, sent(): return lax.ppermute(value, AXES, [(i, target(i) % count) for i in senders])  54.3 us
    dot_general x9, matrix products, contract(): lax.dot_general(left_rows, right_rows, (((1,), (1,)), ((), ())), preferre...  20.5 us
    pallas_call x1, Pallas kernels, per_device(): pl.pallas_call(kernel, grid=(parts,), out_shape=(jax.ShapeDtypeStruct((si...  14.7 us
    unnamed x32, local copies, waits for them, and re-layouts  12.7 us
    pallas_call x1, Pallas kernels, per_device(): pl.pallas_call(last_tiles, out_shape=(square,) * 5 + (jax.ShapeDtypeStruc...  9.23 us
    pallas_call x1, Pallas kernels, per_device(): pl.pallas_call(early_tiles, out_shape=(square,) * 6 + (column,) * 4 + (ro...  6.1 us
  transfers between devices with their start and end apart: 20, of which 9 were waited for; matrix products, arithmetic and copies ran while one was open for 11% of the time, Pallas kernels for 3%

profile of v5, /device:TPU:0, one launch (start us, length us, event | category | flops | bytes accessed | tf_op | source)
XLA Modules:
  0.0 224.4 jit_solution(8870388854120710374)
XLA Ops:
  2.7 10.8 %collective-permute-start.2 = (bf16[256,4096]{1,0:T(8,128)(2,1)}, bf16[256,4096]{1,0:T(8,128)(2,1)}, u32[]{:S(2)}, u32[]{:S(2)}) collective-permute-start(bf16[256,4096]{1,0:T(8,128)(2,1)} %refs_25_.1), channel_id=1, source_target_pairs={{0,255},{127,128},{128,127},{255,0}} | collective-permute-start | bytes 6291464 | tf_op jit(solution)/shard_map/ppermute | solution.py:27
  15.6 3.1 %convolution_multiply_fusion.6 = f32[256,256]{0,1:T(8,128)S(1)} fusion(bf16[256,4096]{1,0:T(8,128)(2,1)} %refs_26_.1, bf16[256,4096]{1,0:T(8,128)(2,1)} %refs_25_.1), kind=kOutput, calls=%fused_computation.12 | convolution fusion | flops 536936448 | bytes 4456448 | tf_op jit(solution)/shard_map/dot_general | solution.py:19
  22.0 47.0 %collective-permute-done.3 = bf16[256,4096]{1,0:T(8,128)(2,1)} collective-permute-done((bf16[256,4096]{1,0:T(8,128)(2,1)}, bf16[256,4096]{1,0:T(8,128)(2,1)}, u32[]{:S(2)}, u32[]{:S(2)}) %collective-permute-start.3) | collective-permute-done | bytes 2097184 | tf_op jit(solution)/shard_map/ppermute | solution.py:27
  69.0 4.1 %collective-permute-done.4 = bf16[256,4096]{1,0:T(8,128)(2,1)} collective-permute-done((bf16[256,4096]{1,0:T(8,128)(2,1)}, bf16[256,4096]{1,0:T(8,128)(2,1)}, u32[]{:S(2)}, u32[]{:S(2)}) %collective-permute-start.4) | collective-permute-done | bytes 2097184 | tf_op jit(solution)/shard_map/ppermute | solution.py:27
  73.1 2.0 collective-permute-start.6
  75.1 2.6 %collective-permute-start.14 = (bf16[256,4096]{1,0:T(8,128)(2,1)S(1)}, bf16[256,4096]{1,0:T(8,128)(2,1)}, u32[]{:S(2)}, u32[]{:S(2)}) collective-permute-start(bf16[256,4096]{1,0:T(8,128)(2,1)S(1)} %copy-done), channel_id=1, source_target_pairs={{0,134},{1,135},{126,248},{127,249},{128,6},{129,7},{254,120},{255... | collective-permute-start | bytes 6291464 | tf_op jit(solution)/shard_map/ppermute | solution.py:27
  79.0 4.7 %collective-permute-start.9 = (bf16[256,4096]{1,0:T(8,128)(2,1)S(1)}, bf16[256,4096]{1,0:T(8,128)(2,1)S(1)}, u32[]{:S(2)}, u32[]{:S(2)}) collective-permute-start(bf16[256,4096]{1,0:T(8,128)(2,1)S(1)} %copy-done), channel_id=1, source_target_pairs={{0,2},{1,3},{2,4},{3,5},{4,6},{5,7},{6,8},{7,9},{8,10},{9,11},{10,... | collective-permute-start | bytes 6291464 | tf_op jit(solution)/shard_map/ppermute | solution.py:27
  83.7 3.0 %fusion.refs_2_ = f32[256,256]{1,0:T(8,128)} fusion(bf16[256,4096]{1,0:T(8,128)(2,1)} %collective-permute-done.2.refs_33_, bf16[256,4096]{1,0:T(8,128)(2,1)S(1)} %copy-done.1), kind=kOutput, calls=%fused_computation.1 | convolution fusion | flops 536936448 | bytes 4456448 | tf_op jit(solution)/shard_map/dot_general | solution.py:19
  86.8 3.0 %fusion.1.refs_1_ = f32[256,256]{1,0:T(8,128)} fusion(bf16[256,4096]{1,0:T(8,128)(2,1)} %collective-permute-done.2.refs_33_, bf16[256,4096]{1,0:T(8,128)(2,1)S(1)} %copy-done), kind=kOutput, calls=%fused_computation.3 | convolution fusion | flops 536936448 | bytes 4456448 | tf_op jit(solution)/shard_map/dot_general | solution.py:19
  89.8 2.3 %fusion.3.refs_7_ = f32[256,256]{1,0:T(8,128)S(1)} fusion(bf16[256,4096]{1,0:T(8,128)(2,1)} %collective-permute-done.1.refs_28_, bf16[256,4096]{1,0:T(8,128)(2,1)S(1)} %copy-done.1), kind=kOutput, calls=%fused_computation.7 | convolution fusion | flops 536936448 | bytes 4456448 | tf_op jit(solution)/shard_map/dot_general | solution.py:19
  92.1 3.1 %fusion.4.refs_6_ = f32[256,256]{1,0:T(8,128)} fusion(bf16[256,4096]{1,0:T(8,128)(2,1)} %collective-permute-done.1.refs_28_, bf16[256,4096]{1,0:T(8,128)(2,1)S(1)} %copy-done), kind=kOutput, calls=%fused_computation.9 | convolution fusion | flops 536936448 | bytes 4456448 | tf_op jit(solution)/shard_map/dot_general | solution.py:19
  95.2 3.1 %fusion.2.refs_8_ = f32[256,256]{1,0:T(8,128)} fusion(bf16[256,4096]{1,0:T(8,128)(2,1)} %collective-permute-done.refs_30_, bf16[256,4096]{1,0:T(8,128)(2,1)S(1)} %copy-done.1), kind=kOutput, calls=%fused_computation.5 | convolution fusion | flops 536936448 | bytes 4456448 | tf_op jit(solution)/shard_map/dot_general | solution.py:19
  98.2 2.4 %slice_select_fusion = (bf16[256,2048]{1,0:T(8,128)(2,1)S(1)}, bf16[256,2048]{1,0:T(8,128)(2,1)S(1)}) fusion(bf16[256,4096]{1,0:T(8,128)(2,1)} %collective-permute-done.refs_30_, bf16[256,4096]{1,0:T(8,128)(2,1)} %collective-permute-done.1.refs_28_, pred[]{:T(512)} %eq.31), kind=kLoop, calls=%fused_computation.16 | loop fusion | flops 1048576 | bytes 6291457 | tf_op jit(solution)/shard_map/jit(_where)/select_n | solution.py:342
  100.6 18.9 %collective-permute-done.5.refs_13_.refs_31_ = bf16[256,4096]{1,0:T(8,128)(2,1)} collective-permute-done((bf16[256,4096]{1,0:T(8,128)(2,1)}, bf16[256,4096]{1,0:T(8,128)(2,1)}, u32[]{:S(2)}, u32[]{:S(2)}) %collective-permute-start.5) | collective-permute-done | bytes 2097184 | tf_op jit(solution)/shard_map/ppermute | solution.py:27
  122.6 2.7 %collective-permute-start.8 = (bf16[256,2048]{1,0:T(8,128)(2,1)S(1)}, bf16[256,2048]{1,0:T(8,128)(2,1)}, u32[]{:S(2)}, u32[]{:S(2)}) collective-permute-start(bf16[256,2048]{1,0:T(8,128)(2,1)S(1)} %get-tuple-element.63), channel_id=1, source_target_pairs={{0,129},{1,128},{2,131},{3,130},{4,133},{5,132},{6,135},{7,134},{8... | collective-permute-start | bytes 3145736 | tf_op jit(solution)/shard_map/ppermute | solution.py:27
  126.4 2.6 %collective-permute-start.11 = (bf16[256,4096]{1,0:T(8,128)(2,1)}, bf16[256,4096]{1,0:T(8,128)(2,1)}, u32[]{:S(2)}, u32[]{:S(2)}) collective-permute-start(bf16[256,4096]{1,0:T(8,128)(2,1)} %collective-permute-done.5.refs_13_.refs_31_), channel_id=1, source_target_pairs={{0,2},{2,4},{3,1},{4,6},{5,3},{6,8},{7,5},{8,10},{9,7},{10,12},{11... | collective-permute-start | bytes 6291464 | tf_op jit(solution)/shard_map/ppermute | solution.py:27
  132.9 13.2 %collective-permute-done.7 = bf16[256,2048]{1,0:T(8,128)(2,1)} collective-permute-done((bf16[256,2048]{1,0:T(8,128)(2,1)S(1)}, bf16[256,2048]{1,0:T(8,128)(2,1)}, u32[]{:S(2)}, u32[]{:S(2)}) %collective-permute-start.7) | collective-permute-done | bytes 1048608 | tf_op jit(solution)/shard_map/ppermute | solution.py:27
  146.2 8.4 %collective-permute-start.13 = (bf16[256,2048]{1,0:T(8,128)(2,1)}, bf16[256,2048]{1,0:T(8,128)(2,1)}, u32[]{:S(2)}, u32[]{:S(2)}) collective-permute-start(bf16[256,2048]{1,0:T(8,128)(2,1)} %collective-permute-done.8), channel_id=1, source_target_pairs={{0,129},{1,128},{2,131},{3,130},{4,133},{5,132},{6,135},{7,134},{8... | collective-permute-start | bytes 3145736 | tf_op jit(solution)/shard_map/ppermute | solution.py:27
  164.4 6.1 %shard_map.58 = (f32[256,256]{1,0:T(8,128)S(1)}, f32[256,256]{1,0:T(8,128)S(1)}, f32[256,256]{1,0:T(8,128)S(1)}, f32[256,256]{1,0:T(8,128)S(1)}, f32[256,256]{1,...) custom-call(s32[4]{0:T(128)S(1)} %add_convert_fusion.refs_0_, ...), custom_call_target="tpu_custom_call" | custom-call | flops 3221225472 | bytes 12582912 | tf_op jit(solution)/shard_map/pallas_call | solution.py:372
  170.8 14.8 %collective-permute-done.15.refs_13_.refs_37_ = bf16[256,4096]{1,0:T(8,128)(2,1)} collective-permute-done((bf16[256,4096]{1,0:T(8,128)(2,1)}, bf16[256,4096]{1,0:T(8,128)(2,1)}, u32[]{:S(2)}, u32[]{:S(2)}) %collective-permute-start.15) | collective-permute-done | bytes 2097184 | tf_op jit(solution)/shard_map/ppermute | solution.py:27
  185.7 9.2 %shard_map.59 = (f32[256,256]{1,0:T(8,128)S(1)}, f32[256,256]{1,0:T(8,128)S(1)}, f32[256,256]{1,0:T(8,128)S(1)}, f32[256,256]{1,0:T(8,128)S(1)}, f32[256,256]{1,...) custom-call(s32[4]{0:T(128)S(1)} %add_convert_fusion.refs_0_, f32[256,256]{1,0:T(8,128)S(1)} %copy-done.14, ...), custom_call_target="tpu_custom_call" | custom-call | flops 1610612736 | bytes 8388608 | tf_op jit(solution)/shard_map/pallas_call | solution.py:399
  195.0 6.0 %collective-permute-start.18 = (f32[2,256]{1,0:T(2,128)S(1)}, f32[2,256]{1,0:T(2,128)S(1)}, u32[]{:S(2)}, u32[]{:S(2)}) collective-permute-start(f32[2,256]{1,0:T(2,128)S(1)} %get-tuple-element.90.refs_20_), channel_id=1, source_target_pairs={{0,254},{1,255},{2,0},{3,1},{4,2},{5,3},{6,4},{7,5},{8,6},{9,7},{1... | collective-permute-start | bytes 6152 | tf_op jit(solution)/shard_map/ppermute | solution.py:27
  201.0 7.2 %collective-permute-start.16 = (f32[2,256]{1,0:T(2,128)S(1)}, f32[2,256]{1,0:T(2,128)S(1)}, u32[]{:S(2)}, u32[]{:S(2)}) collective-permute-start(f32[2,256]{1,0:T(2,128)S(1)} %get-tuple-element.90.refs_20_), channel_id=1, source_target_pairs={{0,255},{1,0},{2,1},{3,2},{4,3},{5,4},{6,5},{7,6},{8,7},{9,8},{10,... | collective-permute-start | bytes 6152 | tf_op jit(solution)/shard_map/ppermute | solution.py:27
  209.5 14.7 %shard_map.60 = (f32[256,4096]{1,0:T(8,128)}, f32[256,4096]{1,0:T(8,128)}) custom-call(s32[4]{0:T(128)S(1)} %add_convert_fusion.refs_0_, s32[1,256]{1,0:T(1,128)S(1)} %bitcast.35, f32[256,256]{1,0:T(8,128)S(1)} %copy.15.refs_2_, f32[256,256]{1,0:T(8,128)S(1)} %copy.16.refs_3_, f32[256,256]{1,0:T(8,128)S(1)} %copy.17.refs_4_, f32[256,256]{1,0:T(8,128)S(1)} %copy.18.refs_5_, ...), custom_call_target="tpu_custom_call" | custom-call | flops 8589934592 | bytes 29360128 | tf_op jit(solution)/shard_map/pallas_call | solution.py:443
  (67 shorter events, 28.3 us)
Async XLA Ops:
  0.6 68.3 %collective-permute-start.3 = (bf16[256,4096]{1,0:T(8,128)(2,1)}, bf16[256,4096]{1,0:T(8,128)(2,1)}, u32[]{:S(2)}, u32[]{:S(2)}) collective-permute-start(bf16[256,4096]{1,0:T(8,128)(2,1)} %refs_25_.1), channel_id=1, source_target_pairs={{0,129},{1,128},{2,131},{3,130},{4,133},{5,132},{6,135},{7,134},{8... | collective-permute-start | bytes 6291464 | tf_op jit(solution)/shard_map/ppermute | solution.py:27
  2.0 71.1 %collective-permute-start.4 = (bf16[256,4096]{1,0:T(8,128)(2,1)}, bf16[256,4096]{1,0:T(8,128)(2,1)}, u32[]{:S(2)}, u32[]{:S(2)}) collective-permute-start(bf16[256,4096]{1,0:T(8,128)(2,1)} %refs_26_.1), channel_id=1, source_target_pairs={{0,128},{1,129},{2,130},{3,131},{4,132},{5,133},{6,134},{7,135},{8... | collective-permute-start | bytes 6291464 | tf_op jit(solution)/shard_map/ppermute | solution.py:27
  2.7 72.4 %collective-permute-start.2 = (bf16[256,4096]{1,0:T(8,128)(2,1)}, bf16[256,4096]{1,0:T(8,128)(2,1)}, u32[]{:S(2)}, u32[]{:S(2)}) collective-permute-start(bf16[256,4096]{1,0:T(8,128)(2,1)} %refs_25_.1), channel_id=1, source_target_pairs={{0,255},{127,128},{128,127},{255,0}} | collective-permute-start | bytes 6291464 | tf_op jit(solution)/shard_map/ppermute | solution.py:27
  13.5 61.6 %collective-permute-start.1 = (bf16[256,4096]{1,0:T(8,128)(2,1)}, bf16[256,4096]{1,0:T(8,128)(2,1)}, u32[]{:S(2)}, u32[]{:S(2)}) collective-permute-start(bf16[256,4096]{1,0:T(8,128)(2,1)} %refs_26_.1), channel_id=1, source_target_pairs={{0,254},{1,255},{2,0},{3,1},{4,2},{5,3},{6,4},{7,5},{8,6},{9,7},{1... | collective-permute-start | bytes 6291464 | tf_op jit(solution)/shard_map/ppermute | solution.py:27
  13.6 61.5 %collective-permute-start = (bf16[256,4096]{1,0:T(8,128)(2,1)}, bf16[256,4096]{1,0:T(8,128)(2,1)}, u32[]{:S(2)}, u32[]{:S(2)}) collective-permute-start(bf16[256,4096]{1,0:T(8,128)(2,1)} %refs_26_.1), channel_id=1, source_target_pairs={{0,2},{1,3},{2,4},{3,5},{4,6},{5,7},{6,8},{7,9},{8,10},{9,11},{10,... | collective-permute-start | bytes 6291464 | tf_op jit(solution)/shard_map/ppermute | solution.py:27
  73.1 46.5 %collective-permute-start.5 = (bf16[256,4096]{1,0:T(8,128)(2,1)}, bf16[256,4096]{1,0:T(8,128)(2,1)}, u32[]{:S(2)}, u32[]{:S(2)}) collective-permute-start(bf16[256,4096]{1,0:T(8,128)(2,1)} %collective-permute-done.3), channel_id=1, source_target_pairs={{0,129},{1,128},{2,131},{3,130},{4,133},{5,132},{6,135},{7,134},{8... | collective-permute-start | bytes 6291464 | tf_op jit(solution)/shard_map/ppermute | solution.py:27
  73.1 47.6 %collective-permute-start.6 = (bf16[256,4096]{1,0:T(8,128)(2,1)}, bf16[256,4096]{1,0:T(8,128)(2,1)S(1)}, u32[]{:S(2)}, u32[]{:S(2)}) collective-permute-start(bf16[256,4096]{1,0:T(8,128)(2,1)} %collective-permute-done.4), channel_id=1, source_target_pairs={{0,128},{1,129},{2,130},{3,131},{4,132},{5,133},{6,134},{7,135},{8... | collective-permute-start | bytes 6291464 | tf_op jit(solution)/shard_map/ppermute | solution.py:27
  75.1 51.3 %collective-permute-start.14 = (bf16[256,4096]{1,0:T(8,128)(2,1)S(1)}, bf16[256,4096]{1,0:T(8,128)(2,1)}, u32[]{:S(2)}, u32[]{:S(2)}) collective-permute-start(bf16[256,4096]{1,0:T(8,128)(2,1)S(1)} %copy-done), channel_id=1, source_target_pairs={{0,134},{1,135},{126,248},{127,249},{128,6},{129,7},{254,120},{255... | collective-permute-start | bytes 6291464 | tf_op jit(solution)/shard_map/ppermute | solution.py:27
  77.7 51.2 %collective-permute-start.10 = (bf16[256,4096]{1,0:T(8,128)(2,1)S(1)}, bf16[256,4096]{1,0:T(8,128)(2,1)S(1)}, u32[]{:S(2)}, u32[]{:S(2)}) collective-permute-start(bf16[256,4096]{1,0:T(8,128)(2,1)S(1)} %copy-done), channel_id=1, source_target_pairs={{2,0},{3,1},{4,2},{5,3},{6,4},{7,5},{8,6},{9,7},{10,8},{11,9},{12,... | collective-permute-start | bytes 6291464 | tf_op jit(solution)/shard_map/ppermute | solution.py:27
  79.0 52.6 %collective-permute-start.9 = (bf16[256,4096]{1,0:T(8,128)(2,1)S(1)}, bf16[256,4096]{1,0:T(8,128)(2,1)S(1)}, u32[]{:S(2)}, u32[]{:S(2)}) collective-permute-start(bf16[256,4096]{1,0:T(8,128)(2,1)S(1)} %copy-done), channel_id=1, source_target_pairs={{0,2},{1,3},{2,4},{3,5},{4,6},{5,7},{6,8},{7,9},{8,10},{9,11},{10,... | collective-permute-start | bytes 6291464 | tf_op jit(solution)/shard_map/ppermute | solution.py:27
  98.2 56.4 %copy-start.15 = (s32[256]{0:T(256)S(1)}, s32[256]{0:T(256)}, u32[]{:S(2)}) copy-start(s32[256]{0:T(256)} %param.5) | copy-start | bytes 3076
  122.1 24.1 %collective-permute-start.7 = (bf16[256,2048]{1,0:T(8,128)(2,1)S(1)}, bf16[256,2048]{1,0:T(8,128)(2,1)}, u32[]{:S(2)}, u32[]{:S(2)}) collective-permute-start(bf16[256,2048]{1,0:T(8,128)(2,1)S(1)} %get-tuple-element.62), channel_id=1, source_target_pairs={{0,128},{1,129},{2,130},{3,131},{4,132},{5,133},{6,134},{7,135},{8... | collective-permute-start | bytes 3145736 | tf_op jit(solution)/shard_map/ppermute | solution.py:27
  122.6 23.6 %collective-permute-start.8 = (bf16[256,2048]{1,0:T(8,128)(2,1)S(1)}, bf16[256,2048]{1,0:T(8,128)(2,1)}, u32[]{:S(2)}, u32[]{:S(2)}) collective-permute-start(bf16[256,2048]{1,0:T(8,128)(2,1)S(1)} %get-tuple-element.63), channel_id=1, source_target_pairs={{0,129},{1,128},{2,131},{3,130},{4,133},{5,132},{6,135},{7,134},{8... | collective-permute-start | bytes 3145736 | tf_op jit(solution)/shard_map/ppermute | solution.py:27
  126.4 44.5 %collective-permute-start.11 = (bf16[256,4096]{1,0:T(8,128)(2,1)}, bf16[256,4096]{1,0:T(8,128)(2,1)}, u32[]{:S(2)}, u32[]{:S(2)}) collective-permute-start(bf16[256,4096]{1,0:T(8,128)(2,1)} %collective-permute-done.5.refs_13_.refs_31_), channel_id=1, source_target_pairs={{0,2},{2,4},{3,1},{4,6},{5,3},{6,8},{7,5},{8,10},{9,7},{10,12},{11... | collective-permute-start | bytes 6291464 | tf_op jit(solution)/shard_map/ppermute | solution.py:27
  130.3 55.3 %collective-permute-start.15 = (bf16[256,4096]{1,0:T(8,128)(2,1)}, bf16[256,4096]{1,0:T(8,128)(2,1)}, u32[]{:S(2)}, u32[]{:S(2)}) collective-permute-start(bf16[256,4096]{1,0:T(8,128)(2,1)} %collective-permute-done.14), channel_id=1, source_target_pairs={{6,126},{7,127},{120,0},{121,1},{134,254},{135,255},{248,128},{249... | collective-permute-start | bytes 6291464 | tf_op jit(solution)/shard_map/ppermute | solution.py:27
  146.2 39.5 %collective-permute-start.12 = (bf16[256,2048]{1,0:T(8,128)(2,1)}, bf16[256,2048]{1,0:T(8,128)(2,1)}, u32[]{:S(2)}, u32[]{:S(2)}) collective-permute-start(bf16[256,2048]{1,0:T(8,128)(2,1)} %collective-permute-done.7), channel_id=1, source_target_pairs={{0,128},{1,129},{2,130},{3,131},{4,132},{5,133},{6,134},{7,135},{8... | collective-permute-start | bytes 3145736 | tf_op jit(solution)/shard_map/ppermute | solution.py:27
  146.2 39.5 %collective-permute-start.13 = (bf16[256,2048]{1,0:T(8,128)(2,1)}, bf16[256,2048]{1,0:T(8,128)(2,1)}, u32[]{:S(2)}, u32[]{:S(2)}) collective-permute-start(bf16[256,2048]{1,0:T(8,128)(2,1)} %collective-permute-done.8), channel_id=1, source_target_pairs={{0,129},{1,128},{2,131},{3,130},{4,133},{5,132},{6,135},{7,134},{8... | collective-permute-start | bytes 3145736 | tf_op jit(solution)/shard_map/ppermute | solution.py:27
  164.4 21.2 %copy-start.14 = (f32[256,256]{1,0:T(8,128)S(1)}, f32[256,256]{1,0:T(8,128)}, u32[]{:S(2)}) copy-start(f32[256,256]{1,0:T(8,128)} %fusion.1.refs_1_) | copy-start | bytes 786436
  185.7 23.8 %copy-start.10 = (f32[256,256]{1,0:T(8,128)S(1)}, f32[256,256]{1,0:T(8,128)}, u32[]{:S(2)}) copy-start(f32[256,256]{1,0:T(8,128)} %fusion.4.refs_6_) | copy-start | bytes 786436
  185.7 23.8 %copy-start.12 = (f32[256,256]{1,0:T(8,128)S(1)}, f32[256,256]{1,0:T(8,128)}, u32[]{:S(2)}) copy-start(f32[256,256]{1,0:T(8,128)} %fusion.2.refs_8_) | copy-start | bytes 786436
  194.9 13.2 %collective-permute-start.19 = (f32[2,256]{1,0:T(2,128)S(1)}, f32[2,256]{1,0:T(2,128)S(1)}, u32[]{:S(2)}, u32[]{:S(2)}) collective-permute-start(f32[2,256]{1,0:T(2,128)S(1)} %get-tuple-element.90.refs_20_), channel_id=1, source_target_pairs={{0,2},{1,3},{2,4},{3,5},{4,6},{5,7},{6,8},{7,9},{8,10},{9,11},{10,... | collective-permute-start | bytes 6152 | tf_op jit(solution)/shard_map/ppermute | solution.py:27
  195.0 13.1 %collective-permute-start.18 = (f32[2,256]{1,0:T(2,128)S(1)}, f32[2,256]{1,0:T(2,128)S(1)}, u32[]{:S(2)}, u32[]{:S(2)}) collective-permute-start(f32[2,256]{1,0:T(2,128)S(1)} %get-tuple-element.90.refs_20_), channel_id=1, source_target_pairs={{0,254},{1,255},{2,0},{3,1},{4,2},{5,3},{6,4},{7,5},{8,6},{9,7},{1... | collective-permute-start | bytes 6152 | tf_op jit(solution)/shard_map/ppermute | solution.py:27
  201.0 8.4 %collective-permute-start.17 = (f32[2,256]{1,0:T(2,128)S(1)}, f32[2,256]{1,0:T(2,128)S(1)}, u32[]{:S(2)}, u32[]{:S(2)}) collective-permute-start(f32[2,256]{1,0:T(2,128)S(1)} %get-tuple-element.90.refs_20_), channel_id=1, source_target_pairs={{0,1},{1,2},{2,3},{3,4},{4,5},{5,6},{6,7},{7,8},{8,9},{9,10},{10,1... | collective-permute-start | bytes 6152 | tf_op jit(solution)/shard_map/ppermute | solution.py:27
  201.0 8.5 %collective-permute-start.16 = (f32[2,256]{1,0:T(2,128)S(1)}, f32[2,256]{1,0:T(2,128)S(1)}, u32[]{:S(2)}, u32[]{:S(2)}) collective-permute-start(f32[2,256]{1,0:T(2,128)S(1)} %get-tuple-element.90.refs_20_), channel_id=1, source_target_pairs={{0,255},{1,0},{2,1},{3,2},{4,3},{5,4},{6,5},{7,6},{8,7},{9,8},{10,... | collective-permute-start | bytes 6152 | tf_op jit(solution)/shard_map/ppermute | solution.py:27
  (12 other events, 40.2 us)

commit v6 on v3

--- a/solution.py
+++ b/solution.py
@@ -11,8 +11,8 @@
 NEGATIVE = -1e30
 CHUNK = 512
 SLOTS = 4
-VMEM_LIMIT = 20 * 1024 * 1024
-SMALL_LIMIT = 14 * 1024 * 1024
+VMEM_LIMIT = 40 * 1024 * 1024
+SMALL_LIMIT = 12 * 1024 * 1024
 
 
 def contract(left_rows, right_rows):
@@ -53,23 +53,40 @@
 
 def early_kernel(scale, place, pos, *refs):
     qq, qd, dq, dd, qd_n2, dd_n2, dd_p2 = refs[:7]
-    own_q, own_d, q_n2, q_p2, q_pair, d_pair = refs[7:13]
+    sources = refs[7:13]
     qq_n2, dq_p2, qq_p2, qq_pair, cross_pair, dd_pair = refs[13:19]
-    q_max, q_sum, d_max, d_sum, positive = refs[19:]
+    q_max, q_sum, d_max, d_sum, positive = refs[19:24]
+    held, arrived = refs[24:]
     even, first, last = [place[k] == 1 for k in range(3)]
-    qq_pair[...] = scale * contract(own_q[...], q_pair[...])
-    dd_pair[...] = scale * contract(own_d[...], d_pair[...])
-    qq_n2[...] = scale * contract(own_q[...], q_n2[...])
-    qq_p2[...] = scale * contract(own_q[...], q_p2[...])
-    dq_p2[...] = scale * contract(own_d[...], q_p2[...])
+    copies = [
+        pltpu.make_async_copy(source, held.at[k], arrived.at[k])
+        for k, source in enumerate(sources)
+    ]
+    for copy in copies:
+        copy.start()
+    own_q, own_d, q_n2, q_p2, q_pair, d_pair = range(6)
+
+    def product(left, right):
+        return scale * contract(held[left], held[right])
+
+    for k in (own_q, own_d, q_n2):
+        copies[k].wait()
+    qq_n2[...] = product(own_q, q_n2)
+    copies[q_p2].wait()
+    qq_p2[...] = product(own_q, q_p2)
+    dq_p2[...] = product(own_d, q_p2)
+    copies[q_pair].wait()
+    qq_pair[...] = product(own_q, q_pair)
+    copies[d_pair].wait()
+    dd_pair[...] = product(own_d, d_pair)
 
     @pl.when(even)
     def _():
-        cross_pair[...] = scale * contract(own_q[...], d_pair[...])
+        cross_pair[...] = product(own_q, d_pair)
 
     @pl.when(jnp.logical_not(even))
     def _():
-        cross_pair[...] = scale * contract(own_d[...], q_pair[...])
+        cross_pair[...] = product(own_d, q_pair)
 
     cross = cross_pair[...]
     q_tiles = [
@@ -100,9 +117,11 @@
 
 def lse_kernel(scale, place, qq_edge, dq_edge, q_max, q_sum, d_max, d_sum, positive, *refs):
     own_q, own_d, q_diag, d_low, d_high, q_swap = refs[:6]
-    qq_diag, cross_diag, dd_diag, qq_swap, dq_swap, lse, row_terms = refs[6:]
+    qq_diag, cross_diag, dd_diag, qq_swap, dq_swap, lse, row_terms, held, arrived = refs[6:]
     even, first, last, edge = [place[k] == 1 for k in range(4)]
     half = d_low.shape[1]
+    copy = pltpu.make_async_copy(q_swap, held, arrived)
+    pl.when(first | last)(copy.start)
 
     def with_documents(own):
         return scale * (contract(own[:, :half], d_low[...]) + contract(own[:, half:], d_high[...]))
@@ -120,8 +139,9 @@
 
     @pl.when(first | last)
     def _():
-        qq_swap[...] = scale * contract(own_q[...], q_swap[...])
-        dq_swap[...] = scale * contract(own_d[...], q_swap[...])
+        copy.wait()
+        qq_swap[...] = scale * contract(own_q[...], held[...])
+        dq_swap[...] = scale * contract(own_d[...], held[...])
 
     @pl.when(jnp.logical_not(first | last))
     def _():
@@ -302,15 +322,13 @@
     q_down, d_up, own_tiles = barrier((q_down, d_up, own_tiles))
     q_pair = sent(q_down, down)
     d_pair = sent(d_up, up)
-    q_own, q_edge = barrier((queries, q_edge))
-    q_p2 = sent(q_own, lambda i: i + 2, [i for i in range(count) if i % half < half - 2])
-    q_own, d_n2 = barrier((queries, d_n2))
-    q_n2 = sent(q_own, lambda i: i - 2, [i for i in range(count) if i % half >= 2])
-    q_own, d_p2, d_n2, q_down, d_up = barrier((queries, d_p2, d_n2, q_down, d_up))
+    q_own, d_p2, d_n2, q_edge, q_down, d_up = barrier((queries, d_p2, d_n2, q_edge, q_down, d_up))
     crossing = [i for i in range(count) if i % half < 2 or i % half >= half - 2]
     q_swap = sent(
         q_own, lambda i: i + half + (inner - 2 if i % half < 2 else 2 - inner), crossing
     )
+    q_p2 = sent(q_own, lambda i: i + 2, [i for i in range(count) if i % half < half - 2])
+    q_n2 = sent(q_own, lambda i: i - 2, [i for i in range(count) if i % half >= 2])
     far_tiles = [
         tile(queries, d_n2),
         tile(documents, d_n2),
@@ -321,12 +339,14 @@
     cut = width // 2
     d_low = jnp.where(is_even, d_n2[:, :cut], d_p2[:, :cut])
     d_high = jnp.where(is_even, d_n2[:, cut:], d_p2[:, cut:])
-    d_low, d_high, q_pair, d_pair, q_p2, q_n2, far_tiles = barrier(
-        (d_low, d_high, q_pair, d_pair, q_p2, q_n2, far_tiles)
-    )
-    q_diag = sent(q_pair, lambda i: i - i % half + (i + (-2 if i % 2 else 2)) % half)
+    d_low, d_high, q_pair, d_pair, far_tiles = barrier((d_low, d_high, q_pair, d_pair, far_tiles))
     d_low = sent(d_low, up)
     d_high = sent(d_high, down)
+    q_diag = sent(
+        q_pair,
+        lambda i: i - 2 if i % 2 else i + 2,
+        [i for i in range(count) if i % half != 1 and i % half != half - 2],
+    )
     d_low, d_high, q_swap, q_pair, d_pair, q_p2, q_n2 = barrier(
         (d_low, d_high, q_swap, q_pair, d_pair, q_p2, q_n2)
     )
@@ -351,9 +371,13 @@
     *early, q_max, q_sum, d_max, d_sum, positive = pl.pallas_call(
         early_tiles,
         out_shape=(square,) * 6 + (column,) * 4 + (row,),
-        in_specs=[in_smem] + [in_vmem] * 14,
+        in_specs=[in_smem] + [in_vmem] * 8 + [anywhere] * 6,
         out_specs=(in_vmem,) * 11,
-        compiler_params=pltpu.CompilerParams(vmem_limit_bytes=SMALL_LIMIT),
+        scratch_shapes=[
+            pltpu.VMEM((6, size, width), jnp.bfloat16),
+            pltpu.SemaphoreType.DMA((6,)),
+        ],
+        compiler_params=pltpu.CompilerParams(vmem_limit_bytes=VMEM_LIMIT),
         cost_estimate=pl.CostEstimate(
             flops=12 * size * size * width,
             bytes_accessed=12 * size * width,
@@ -378,8 +402,9 @@
     *late, lse, row_terms = pl.pallas_call(
         last_tiles,
         out_shape=(square,) * 5 + (jax.ShapeDtypeStruct((2, size), jnp.float32), row),
-        in_specs=[in_smem] + [in_vmem] * 13,
+        in_specs=[in_smem] + [in_vmem] * 12 + [anywhere],
         out_specs=(in_vmem,) * 7,
+        scratch_shapes=[pltpu.VMEM((size, width), jnp.bfloat16), pltpu.SemaphoreType.DMA],
         compiler_params=pltpu.CompilerParams(vmem_limit_bytes=SMALL_LIMIT),
         cost_estimate=pl.CostEstimate(
             flops=6 * size * size * width,

time: 240 us -> 224 us (0.933)
  waiting for transfers between devices: 132 us -> 106 us
  starting transfers between devices: 42.4 us -> 53.4 us
  local copies, waits for them, and re-layouts: 13.7 us -> 11.2 us
    ppermute x20, waiting for transfers between devices: 132 us -> 106 us  [sent(): return lax.ppermute(value, AXES, [(i, target(i) % count) for i in senders])]
    ppermute x20, starting transfers between devices: 42.4 us -> 53.4 us  [sent(): return lax.ppermute(value, AXES, [(i, target(i) % count) for i in senders])]
    unnamed x40 -> x32, local copies, waits for them, and re-layouts: 12.2 us -> 9.72 us
  transfers between devices with their start and end apart: 20 -> 20, of which waited for: 10 -> 9; matrix products, arithmetic and copies ran while one was open for 10% -> 11% of each run, Pallas kernels for 3% -> 3%
where the time goes in v6:
time: 224 us; the launch traced here: 223 us
  waiting for transfers between devices  106 us (47%)
  starting transfers between devices  53.4 us (24%)
  Pallas kernels  28.1 us (13%)
  matrix products  20.5 us (9%)
  local copies, waits for them, and re-layouts  11.2 us (5%)
  other arithmetic  2.47 us (1%)
    ppermute x20, waiting for transfers between devices, sent(): return lax.ppermute(value, AXES, [(i, target(i) % count) for i in senders])  106 us
    ppermute x20, starting transfers between devices, sent(): return lax.ppermute(value, AXES, [(i, target(i) % count) for i in senders])  53.4 us
    dot_general x9, matrix products, contract(): lax.dot_general(left_rows, right_rows, (((1,), (1,)), ((), ())), preferre...  20.5 us
    pallas_call x1, Pallas kernels, per_device(): pl.pallas_call(kernel, grid=(parts,), out_shape=(jax.ShapeDtypeStruct((si...  13.7 us
    unnamed x32, local copies, waits for them, and re-layouts  9.72 us
    pallas_call x1, Pallas kernels, per_device(): pl.pallas_call(early_tiles, out_shape=(square,) * 6 + (column,) * 4 + (ro...  7.24 us
    pallas_call x1, Pallas kernels, per_device(): pl.pallas_call(last_tiles, out_shape=(square,) * 5 + (jax.ShapeDtypeStruc...  7.13 us
  transfers between devices with their start and end apart: 20, of which 9 were waited for; matrix products, arithmetic and copies ran while one was open for 11% of the time, Pallas kernels for 3%

profile of v6, /device:TPU:0, one launch (start us, length us, event | category | flops | bytes accessed | tf_op | source)
XLA Modules:
  0.0 223.0 jit_solution(2739085149957145291)
XLA Ops:
  2.7 10.8 %collective-permute-start.2 = (bf16[256,4096]{1,0:T(8,128)(2,1)}, bf16[256,4096]{1,0:T(8,128)(2,1)}, u32[]{:S(2)}, u32[]{:S(2)}) collective-permute-start(bf16[256,4096]{1,0:T(8,128)(2,1)} %refs_25_.1), channel_id=1, source_target_pairs={{0,255},{127,128},{128,127},{255,0}} | collective-permute-start | bytes 6291464 | tf_op jit(solution)/shard_map/ppermute | solution.py:27
  15.6 3.1 %convolution_multiply_fusion.6 = f32[256,256]{0,1:T(8,128)S(1)} fusion(bf16[256,4096]{1,0:T(8,128)(2,1)} %refs_26_.1, bf16[256,4096]{1,0:T(8,128)(2,1)} %refs_25_.1), kind=kOutput, calls=%fused_computation.12 | convolution fusion | flops 536936448 | bytes 4456448 | tf_op jit(solution)/shard_map/dot_general | solution.py:19
  22.0 46.9 %collective-permute-done.3 = bf16[256,4096]{1,0:T(8,128)(2,1)} collective-permute-done((bf16[256,4096]{1,0:T(8,128)(2,1)}, bf16[256,4096]{1,0:T(8,128)(2,1)}, u32[]{:S(2)}, u32[]{:S(2)}) %collective-permute-start.3) | collective-permute-done | bytes 2097184 | tf_op jit(solution)/shard_map/ppermute | solution.py:27
  69.0 4.1 %collective-permute-done.4 = bf16[256,4096]{1,0:T(8,128)(2,1)} collective-permute-done((bf16[256,4096]{1,0:T(8,128)(2,1)}, bf16[256,4096]{1,0:T(8,128)(2,1)}, u32[]{:S(2)}, u32[]{:S(2)}) %collective-permute-start.4) | collective-permute-done | bytes 2097184 | tf_op jit(solution)/shard_map/ppermute | solution.py:27
  76.4 4.7 %collective-permute-start.10 = (bf16[256,4096]{1,0:T(8,128)(2,1)S(1)}, bf16[256,4096]{1,0:T(8,128)(2,1)S(1)}, u32[]{:S(2)}, u32[]{:S(2)}) collective-permute-start(bf16[256,4096]{1,0:T(8,128)(2,1)S(1)} %copy-done), channel_id=1, source_target_pairs={{0,2},{1,3},{2,4},{3,5},{4,6},{5,7},{6,8},{7,9},{8,10},{9,11},{10,... | collective-permute-start | bytes 6291464 | tf_op jit(solution)/shard_map/ppermute | solution.py:27
  81.1 2.6 %collective-permute-start.9 = (bf16[256,4096]{1,0:T(8,128)(2,1)S(1)}, bf16[256,4096]{1,0:T(8,128)(2,1)}, u32[]{:S(2)}, u32[]{:S(2)}) collective-permute-start(bf16[256,4096]{1,0:T(8,128)(2,1)S(1)} %copy-done), channel_id=1, source_target_pairs={{0,134},{1,135},{126,248},{127,249},{128,6},{129,7},{254,120},{255... | collective-permute-start | bytes 6291464 | tf_op jit(solution)/shard_map/ppermute | solution.py:27
  83.7 3.0 %fusion.refs_2_ = f32[256,256]{1,0:T(8,128)} fusion(bf16[256,4096]{1,0:T(8,128)(2,1)} %collective-permute-done.2.refs_33_, bf16[256,4096]{1,0:T(8,128)(2,1)S(1)} %copy-done.1), kind=kOutput, calls=%fused_computation.1 | convolution fusion | flops 536936448 | bytes 4456448 | tf_op jit(solution)/shard_map/dot_general | solution.py:19
  86.7 3.0 %fusion.1.refs_1_ = f32[256,256]{1,0:T(8,128)} fusion(bf16[256,4096]{1,0:T(8,128)(2,1)} %collective-permute-done.2.refs_33_, bf16[256,4096]{1,0:T(8,128)(2,1)S(1)} %copy-done), kind=kOutput, calls=%fused_computation.3 | convolution fusion | flops 536936448 | bytes 4456448 | tf_op jit(solution)/shard_map/dot_general | solution.py:19
  89.8 2.3 %fusion.3.refs_7_ = f32[256,256]{1,0:T(8,128)S(1)} fusion(bf16[256,4096]{1,0:T(8,128)(2,1)} %collective-permute-done.1.refs_28_, bf16[256,4096]{1,0:T(8,128)(2,1)S(1)} %copy-done.1), kind=kOutput, calls=%fused_computation.7 | convolution fusion | flops 536936448 | bytes 4456448 | tf_op jit(solution)/shard_map/dot_general | solution.py:19
  92.1 3.0 %fusion.4.refs_6_ = f32[256,256]{1,0:T(8,128)} fusion(bf16[256,4096]{1,0:T(8,128)(2,1)} %collective-permute-done.1.refs_28_, bf16[256,4096]{1,0:T(8,128)(2,1)S(1)} %copy-done), kind=kOutput, calls=%fused_computation.9 | convolution fusion | flops 536936448 | bytes 4456448 | tf_op jit(solution)/shard_map/dot_general | solution.py:19
  95.2 3.0 %fusion.2.refs_8_ = f32[256,256]{1,0:T(8,128)} fusion(bf16[256,4096]{1,0:T(8,128)(2,1)} %collective-permute-done.refs_30_, bf16[256,4096]{1,0:T(8,128)(2,1)S(1)} %copy-done.1), kind=kOutput, calls=%fused_computation.5 | convolution fusion | flops 536936448 | bytes 4456448 | tf_op jit(solution)/shard_map/dot_general | solution.py:19
  98.2 2.4 %slice_select_fusion = (bf16[256,2048]{1,0:T(8,128)(2,1)S(1)}, bf16[256,2048]{1,0:T(8,128)(2,1)S(1)}) fusion(bf16[256,4096]{1,0:T(8,128)(2,1)} %collective-permute-done.refs_30_, bf16[256,4096]{1,0:T(8,128)(2,1)} %collective-permute-done.1.refs_28_, pred[]{:T(512)} %eq.31), kind=kLoop, calls=%fused_computation.16 | loop fusion | flops 1048576 | bytes 6291457 | tf_op jit(solution)/shard_map/jit(_where)/select_n | solution.py:341
  100.6 19.0 %collective-permute-done.5.refs_13_.refs_31_ = bf16[256,4096]{1,0:T(8,128)(2,1)} collective-permute-done((bf16[256,4096]{1,0:T(8,128)(2,1)}, bf16[256,4096]{1,0:T(8,128)(2,1)}, u32[]{:S(2)}, u32[]{:S(2)}) %collective-permute-start.5) | collective-permute-done | bytes 2097184 | tf_op jit(solution)/shard_map/ppermute | solution.py:27
  121.2 2.7 %collective-permute-start.8 = (bf16[256,2048]{1,0:T(8,128)(2,1)S(1)}, bf16[256,2048]{1,0:T(8,128)(2,1)}, u32[]{:S(2)}, u32[]{:S(2)}) collective-permute-start(bf16[256,2048]{1,0:T(8,128)(2,1)S(1)} %get-tuple-element.64), channel_id=1, source_target_pairs={{0,129},{1,128},{2,131},{3,130},{4,133},{5,132},{6,135},{7,134},{8... | collective-permute-start | bytes 3145736 | tf_op jit(solution)/shard_map/ppermute | solution.py:27
  125.2 2.6 %collective-permute-start.12 = (bf16[256,4096]{1,0:T(8,128)(2,1)}, bf16[256,4096]{1,0:T(8,128)(2,1)}, u32[]{:S(2)}, u32[]{:S(2)}) collective-permute-start(bf16[256,4096]{1,0:T(8,128)(2,1)} %collective-permute-done.5.refs_13_.refs_31_), channel_id=1, source_target_pairs={{0,2},{2,4},{3,1},{4,6},{5,3},{6,8},{7,5},{8,10},{9,7},{10,12},{11... | collective-permute-start | bytes 6291464 | tf_op jit(solution)/shard_map/ppermute | solution.py:27
  129.2 15.6 %collective-permute-done.7 = bf16[256,2048]{1,0:T(8,128)(2,1)} collective-permute-done((bf16[256,2048]{1,0:T(8,128)(2,1)S(1)}, bf16[256,2048]{1,0:T(8,128)(2,1)}, u32[]{:S(2)}, u32[]{:S(2)}) %collective-permute-start.7) | collective-permute-done | bytes 1048608 | tf_op jit(solution)/shard_map/ppermute | solution.py:27
  146.2 7.4 %collective-permute-start.14 = (bf16[256,2048]{1,0:T(8,128)(2,1)}, bf16[256,2048]{1,0:T(8,128)(2,1)}, u32[]{:S(2)}, u32[]{:S(2)}) collective-permute-start(bf16[256,2048]{1,0:T(8,128)(2,1)} %collective-permute-done.8), channel_id=1, source_target_pairs={{0,129},{1,128},{2,131},{3,130},{4,133},{5,132},{6,135},{7,134},{8... | collective-permute-start | bytes 3145736 | tf_op jit(solution)/shard_map/ppermute | solution.py:27
  161.8 7.2 %shard_map.58 = (f32[256,256]{1,0:T(8,128)S(1)}, f32[256,256]{1,0:T(8,128)S(1)}, f32[256,256]{1,0:T(8,128)S(1)}, f32[256,256]{1,0:T(8,128)S(1)}, f32[256,256]{1,...) custom-call(s32[4]{0:T(128)S(1)} %add_convert_fusion.refs_0_, ...), custom_call_target="tpu_custom_call" | custom-call | flops 3221225472 | bytes 12582912 | tf_op jit(solution)/shard_map/pallas_call | solution.py:371
  169.9 5.6 %collective-permute-done.13.refs_11_.refs_34_ = bf16[256,2048]{1,0:T(8,128)(2,1)} collective-permute-done((bf16[256,2048]{1,0:T(8,128)(2,1)}, bf16[256,2048]{1,0:T(8,128)(2,1)}, u32[]{:S(2)}, u32[]{:S(2)}) %collective-permute-start.13) | collective-permute-done | bytes 1048608 | tf_op jit(solution)/shard_map/ppermute | solution.py:27
  175.5 11.9 %collective-permute-done.15.refs_13_.refs_37_ = bf16[256,4096]{1,0:T(8,128)(2,1)} collective-permute-done((bf16[256,4096]{1,0:T(8,128)(2,1)}, bf16[256,4096]{1,0:T(8,128)(2,1)}, u32[]{:S(2)}, u32[]{:S(2)}) %collective-permute-start.15) | collective-permute-done | bytes 2097184 | tf_op jit(solution)/shard_map/ppermute | solution.py:27
  187.5 7.1 %shard_map.59 = (f32[256,256]{1,0:T(8,128)S(1)}, f32[256,256]{1,0:T(8,128)S(1)}, f32[256,256]{1,0:T(8,128)S(1)}, f32[256,256]{1,0:T(8,128)S(1)}, f32[256,256]{1,...) custom-call(s32[4]{0:T(128)S(1)} %add_convert_fusion.refs_0_, f32[256,256]{1,0:T(8,128)S(1)} %copy-done.13, ...), custom_call_target="tpu_custom_call" | custom-call | flops 1610612736 | bytes 8388608 | tf_op jit(solution)/shard_map/pallas_call | solution.py:402
  194.7 6.0 %collective-permute-start.18 = (f32[2,256]{1,0:T(2,128)S(1)}, f32[2,256]{1,0:T(2,128)S(1)}, u32[]{:S(2)}, u32[]{:S(2)}) collective-permute-start(f32[2,256]{1,0:T(2,128)S(1)} %get-tuple-element.92.refs_20_), channel_id=1, source_target_pairs={{0,254},{1,255},{2,0},{3,1},{4,2},{5,3},{6,4},{7,5},{8,6},{9,7},{1... | collective-permute-start | bytes 6152 | tf_op jit(solution)/shard_map/ppermute | solution.py:27
  200.6 7.2 %collective-permute-start.16 = (f32[2,256]{1,0:T(2,128)S(1)}, f32[2,256]{1,0:T(2,128)S(1)}, u32[]{:S(2)}, u32[]{:S(2)}) collective-permute-start(f32[2,256]{1,0:T(2,128)S(1)} %get-tuple-element.92.refs_20_), channel_id=1, source_target_pairs={{0,255},{1,0},{2,1},{3,2},{4,3},{5,4},{6,5},{7,6},{8,7},{9,8},{10,... | collective-permute-start | bytes 6152 | tf_op jit(solution)/shard_map/ppermute | solution.py:27
  209.1 13.7 %shard_map.60 = (f32[256,4096]{1,0:T(8,128)}, f32[256,4096]{1,0:T(8,128)}) custom-call(s32[4]{0:T(128)S(1)} %add_convert_fusion.refs_0_, s32[1,256]{1,0:T(1,128)S(1)} %bitcast.35, f32[256,256]{1,0:T(8,128)S(1)} %copy.15.refs_2_, f32[256,256]{1,0:T(8,128)S(1)} %copy.16.refs_3_, f32[256,256]{1,0:T(8,128)S(1)} %copy.17.refs_4_, f32[256,256]{1,0:T(8,128)S(1)} %copy.18.refs_5_, ...), custom_call_target="tpu_custom_call" | custom-call | flops 8589934592 | bytes 29360128 | tf_op jit(solution)/shard_map/pallas_call | solution.py:443
  (67 shorter events, 27.0 us)
Async XLA Ops:
  0.6 68.3 %collective-permute-start.3 = (bf16[256,4096]{1,0:T(8,128)(2,1)}, bf16[256,4096]{1,0:T(8,128)(2,1)}, u32[]{:S(2)}, u32[]{:S(2)}) collective-permute-start(bf16[256,4096]{1,0:T(8,128)(2,1)} %refs_25_.1), channel_id=1, source_target_pairs={{0,129},{1,128},{2,131},{3,130},{4,133},{5,132},{6,135},{7,134},{8... | collective-permute-start | bytes 6291464 | tf_op jit(solution)/shard_map/ppermute | solution.py:27
  2.0 71.1 %collective-permute-start.4 = (bf16[256,4096]{1,0:T(8,128)(2,1)}, bf16[256,4096]{1,0:T(8,128)(2,1)}, u32[]{:S(2)}, u32[]{:S(2)}) collective-permute-start(bf16[256,4096]{1,0:T(8,128)(2,1)} %refs_26_.1), channel_id=1, source_target_pairs={{0,128},{1,129},{2,130},{3,131},{4,132},{5,133},{6,134},{7,135},{8... | collective-permute-start | bytes 6291464 | tf_op jit(solution)/shard_map/ppermute | solution.py:27
  2.7 72.4 %collective-permute-start.2 = (bf16[256,4096]{1,0:T(8,128)(2,1)}, bf16[256,4096]{1,0:T(8,128)(2,1)}, u32[]{:S(2)}, u32[]{:S(2)}) collective-permute-start(bf16[256,4096]{1,0:T(8,128)(2,1)} %refs_25_.1), channel_id=1, source_target_pairs={{0,255},{127,128},{128,127},{255,0}} | collective-permute-start | bytes 6291464 | tf_op jit(solution)/shard_map/ppermute | solution.py:27
  13.5 61.6 %collective-permute-start.1 = (bf16[256,4096]{1,0:T(8,128)(2,1)}, bf16[256,4096]{1,0:T(8,128)(2,1)}, u32[]{:S(2)}, u32[]{:S(2)}) collective-permute-start(bf16[256,4096]{1,0:T(8,128)(2,1)} %refs_26_.1), channel_id=1, source_target_pairs={{0,254},{1,255},{2,0},{3,1},{4,2},{5,3},{6,4},{7,5},{8,6},{9,7},{1... | collective-permute-start | bytes 6291464 | tf_op jit(solution)/shard_map/ppermute | solution.py:27
  13.6 61.5 %collective-permute-start = (bf16[256,4096]{1,0:T(8,128)(2,1)}, bf16[256,4096]{1,0:T(8,128)(2,1)}, u32[]{:S(2)}, u32[]{:S(2)}) collective-permute-start(bf16[256,4096]{1,0:T(8,128)(2,1)} %refs_26_.1), channel_id=1, source_target_pairs={{0,2},{1,3},{2,4},{3,5},{4,6},{5,7},{6,8},{7,9},{8,10},{9,11},{10,... | collective-permute-start | bytes 6291464 | tf_op jit(solution)/shard_map/ppermute | solution.py:27
  73.1 46.5 %collective-permute-start.5 = (bf16[256,4096]{1,0:T(8,128)(2,1)}, bf16[256,4096]{1,0:T(8,128)(2,1)}, u32[]{:S(2)}, u32[]{:S(2)}) collective-permute-start(bf16[256,4096]{1,0:T(8,128)(2,1)} %collective-permute-done.3), channel_id=1, source_target_pairs={{0,129},{1,128},{2,131},{3,130},{4,133},{5,132},{6,135},{7,134},{8... | collective-permute-start | bytes 6291464 | tf_op jit(solution)/shard_map/ppermute | solution.py:27
  73.1 47.6 %collective-permute-start.6 = (bf16[256,4096]{1,0:T(8,128)(2,1)}, bf16[256,4096]{1,0:T(8,128)(2,1)S(1)}, u32[]{:S(2)}, u32[]{:S(2)}) collective-permute-start(bf16[256,4096]{1,0:T(8,128)(2,1)} %collective-permute-done.4), channel_id=1, source_target_pairs={{0,128},{1,129},{2,130},{3,131},{4,132},{5,133},{6,134},{7,135},{8... | collective-permute-start | bytes 6291464 | tf_op jit(solution)/shard_map/ppermute | solution.py:27
  75.1 48.8 %collective-permute-start.11 = (bf16[256,4096]{1,0:T(8,128)(2,1)S(1)}, bf16[256,4096]{1,0:T(8,128)(2,1)S(1)}, u32[]{:S(2)}, u32[]{:S(2)}) collective-permute-start(bf16[256,4096]{1,0:T(8,128)(2,1)S(1)} %copy-done), channel_id=1, source_target_pairs={{2,0},{3,1},{4,2},{5,3},{6,4},{7,5},{8,6},{9,7},{10,8},{11,9},{12,... | collective-permute-start | bytes 6291464 | tf_op jit(solution)/shard_map/ppermute | solution.py:27
  76.4 51.4 %collective-permute-start.10 = (bf16[256,4096]{1,0:T(8,128)(2,1)S(1)}, bf16[256,4096]{1,0:T(8,128)(2,1)S(1)}, u32[]{:S(2)}, u32[]{:S(2)}) collective-permute-start(bf16[256,4096]{1,0:T(8,128)(2,1)S(1)} %copy-done), channel_id=1, source_target_pairs={{0,2},{1,3},{2,4},{3,5},{4,6},{5,7},{6,8},{7,9},{8,10},{9,11},{10,... | collective-permute-start | bytes 6291464 | tf_op jit(solution)/shard_map/ppermute | solution.py:27
  81.1 48.1 %collective-permute-start.9 = (bf16[256,4096]{1,0:T(8,128)(2,1)S(1)}, bf16[256,4096]{1,0:T(8,128)(2,1)}, u32[]{:S(2)}, u32[]{:S(2)}) collective-permute-start(bf16[256,4096]{1,0:T(8,128)(2,1)S(1)} %copy-done), channel_id=1, source_target_pairs={{0,134},{1,135},{126,248},{127,249},{128,6},{129,7},{254,120},{255... | collective-permute-start | bytes 6291464 | tf_op jit(solution)/shard_map/ppermute | solution.py:27
  98.2 55.5 %copy-start.15 = (s32[256]{0:T(256)S(1)}, s32[256]{0:T(256)}, u32[]{:S(2)}) copy-start(s32[256]{0:T(256)} %param.5) | copy-start | bytes 3076
  120.7 24.1 %collective-permute-start.7 = (bf16[256,2048]{1,0:T(8,128)(2,1)S(1)}, bf16[256,2048]{1,0:T(8,128)(2,1)}, u32[]{:S(2)}, u32[]{:S(2)}) collective-permute-start(bf16[256,2048]{1,0:T(8,128)(2,1)S(1)} %get-tuple-element.63), channel_id=1, source_target_pairs={{0,128},{1,129},{2,130},{3,131},{4,132},{5,133},{6,134},{7,135},{8... | collective-permute-start | bytes 3145736 | tf_op jit(solution)/shard_map/ppermute | solution.py:27
  121.2 23.6 %collective-permute-start.8 = (bf16[256,2048]{1,0:T(8,128)(2,1)S(1)}, bf16[256,2048]{1,0:T(8,128)(2,1)}, u32[]{:S(2)}, u32[]{:S(2)}) collective-permute-start(bf16[256,2048]{1,0:T(8,128)(2,1)S(1)} %get-tuple-element.64), channel_id=1, source_target_pairs={{0,129},{1,128},{2,131},{3,130},{4,133},{5,132},{6,135},{7,134},{8... | collective-permute-start | bytes 3145736 | tf_op jit(solution)/shard_map/ppermute | solution.py:27
  125.2 44.7 %collective-permute-start.12 = (bf16[256,4096]{1,0:T(8,128)(2,1)}, bf16[256,4096]{1,0:T(8,128)(2,1)}, u32[]{:S(2)}, u32[]{:S(2)}) collective-permute-start(bf16[256,4096]{1,0:T(8,128)(2,1)} %collective-permute-done.5.refs_13_.refs_31_), channel_id=1, source_target_pairs={{0,2},{2,4},{3,1},{4,6},{5,3},{6,8},{7,5},{8,10},{9,7},{10,12},{11... | collective-permute-start | bytes 6291464 | tf_op jit(solution)/shard_map/ppermute | solution.py:27
  144.8 42.6 %collective-permute-start.15 = (bf16[256,4096]{1,0:T(8,128)(2,1)}, bf16[256,4096]{1,0:T(8,128)(2,1)}, u32[]{:S(2)}, u32[]{:S(2)}) collective-permute-start(bf16[256,4096]{1,0:T(8,128)(2,1)} %collective-permute-done.9), channel_id=1, source_target_pairs={{6,126},{7,127},{120,0},{121,1},{134,254},{135,255},{248,128},{249... | collective-permute-start | bytes 6291464 | tf_op jit(solution)/shard_map/ppermute | solution.py:27
  146.1 29.4 %collective-permute-start.13 = (bf16[256,2048]{1,0:T(8,128)(2,1)}, bf16[256,2048]{1,0:T(8,128)(2,1)}, u32[]{:S(2)}, u32[]{:S(2)}) collective-permute-start(bf16[256,2048]{1,0:T(8,128)(2,1)} %collective-permute-done.7), channel_id=1, source_target_pairs={{0,128},{1,129},{2,130},{3,131},{4,132},{5,133},{6,134},{7,135},{8... | collective-permute-start | bytes 3145736 | tf_op jit(solution)/shard_map/ppermute | solution.py:27
  146.2 29.3 %collective-permute-start.14 = (bf16[256,2048]{1,0:T(8,128)(2,1)}, bf16[256,2048]{1,0:T(8,128)(2,1)}, u32[]{:S(2)}, u32[]{:S(2)}) collective-permute-start(bf16[256,2048]{1,0:T(8,128)(2,1)} %collective-permute-done.8), channel_id=1, source_target_pairs={{0,129},{1,128},{2,131},{3,130},{4,133},{5,132},{6,135},{7,134},{8... | collective-permute-start | bytes 3145736 | tf_op jit(solution)/shard_map/ppermute | solution.py:27
  161.8 25.6 %copy-start.12 = (f32[256,256]{1,0:T(8,128)S(1)}, f32[256,256]{1,0:T(8,128)}, u32[]{:S(2)}) copy-start(f32[256,256]{1,0:T(8,128)} %fusion.refs_2_) | copy-start | bytes 786436
  161.8 25.6 %copy-start.13 = (f32[256,256]{1,0:T(8,128)S(1)}, f32[256,256]{1,0:T(8,128)}, u32[]{:S(2)}) copy-start(f32[256,256]{1,0:T(8,128)} %fusion.1.refs_1_) | copy-start | bytes 786436
  187.4 21.7 %copy-start.9 = (f32[256,256]{1,0:T(8,128)S(1)}, f32[256,256]{1,0:T(8,128)}, u32[]{:S(2)}) copy-start(f32[256,256]{1,0:T(8,128)} %fusion.4.refs_6_) | copy-start | bytes 786436
  194.6 13.2 %collective-permute-start.19 = (f32[2,256]{1,0:T(2,128)S(1)}, f32[2,256]{1,0:T(2,128)S(1)}, u32[]{:S(2)}, u32[]{:S(2)}) collective-permute-start(f32[2,256]{1,0:T(2,128)S(1)} %get-tuple-element.92.refs_20_), channel_id=1, source_target_pairs={{0,2},{1,3},{2,4},{3,5},{4,6},{5,7},{6,8},{7,9},{8,10},{9,11},{10,... | collective-permute-start | bytes 6152 | tf_op jit(solution)/shard_map/ppermute | solution.py:27
  194.7 13.1 %collective-permute-start.18 = (f32[2,256]{1,0:T(2,128)S(1)}, f32[2,256]{1,0:T(2,128)S(1)}, u32[]{:S(2)}, u32[]{:S(2)}) collective-permute-start(f32[2,256]{1,0:T(2,128)S(1)} %get-tuple-element.92.refs_20_), channel_id=1, source_target_pairs={{0,254},{1,255},{2,0},{3,1},{4,2},{5,3},{6,4},{7,5},{8,6},{9,7},{1... | collective-permute-start | bytes 6152 | tf_op jit(solution)/shard_map/ppermute | solution.py:27
  200.6 8.4 %collective-permute-start.17 = (f32[2,256]{1,0:T(2,128)S(1)}, f32[2,256]{1,0:T(2,128)S(1)}, u32[]{:S(2)}, u32[]{:S(2)}) collective-permute-start(f32[2,256]{1,0:T(2,128)S(1)} %get-tuple-element.92.refs_20_), channel_id=1, source_target_pairs={{0,1},{1,2},{2,3},{3,4},{4,5},{5,6},{6,7},{7,8},{8,9},{9,10},{10,1... | collective-permute-start | bytes 6152 | tf_op jit(solution)/shard_map/ppermute | solution.py:27
  200.6 8.5 %collective-permute-start.16 = (f32[2,256]{1,0:T(2,128)S(1)}, f32[2,256]{1,0:T(2,128)S(1)}, u32[]{:S(2)}, u32[]{:S(2)}) collective-permute-start(f32[2,256]{1,0:T(2,128)S(1)} %get-tuple-element.92.refs_20_), channel_id=1, source_target_pairs={{0,255},{1,0},{2,1},{3,2},{4,3},{5,4},{6,5},{7,6},{8,7},{9,8},{10,... | collective-permute-start | bytes 6152 | tf_op jit(solution)/shard_map/ppermute | solution.py:27
  (12 other events, 67.9 us)

commit v7 on v6

--- a/solution.py
+++ b/solution.py
@@ -11,7 +11,7 @@
 NEGATIVE = -1e30
 CHUNK = 512
 SLOTS = 4
-VMEM_LIMIT = 40 * 1024 * 1024
+VMEM_LIMIT = 20 * 1024 * 1024
 SMALL_LIMIT = 12 * 1024 * 1024
 
 
@@ -141,12 +141,18 @@
     def _():
         copy.wait()
         qq_swap[...] = scale * contract(own_q[...], held[...])
+
+    @pl.when(first)
+    def _():
         dq_swap[...] = scale * contract(own_d[...], held[...])
 
+    @pl.when(jnp.logical_not(first))
+    def _():
+        dq_swap[...] = jnp.full(dq_swap.shape, NEGATIVE, jnp.float32)
+
     @pl.when(jnp.logical_not(first | last))
     def _():
         qq_swap[...] = jnp.full(qq_swap.shape, NEGATIVE, jnp.float32)
-        dq_swap[...] = jnp.full(dq_swap.shape, NEGATIVE, jnp.float32)
 
     def finished(early_max, early_sum, tiles):
         largest = early_max[:, :1]

time: 224 us -> 224 us (level)
  local copies, waits for them, and re-layouts: 11.2 us -> 14 us
    unnamed x32 -> x38, local copies, waits for them, and re-layouts: 9.72 us -> 12.6 us
where the time goes in v7:
time: 224 us
  waiting for transfers between devices  105 us (47%)
  starting transfers between devices  52.2 us (23%)
  Pallas kernels  28.9 us (13%)
  matrix products  20.6 us (9%)
  local copies, waits for them, and re-layouts  14 us (6%)
  other arithmetic  2.47 us (1%)
    ppermute x20, waiting for transfers between devices, sent(): return lax.ppermute(value, AXES, [(i, target(i) % count) for i in senders])  105 us
    ppermute x20, starting transfers between devices, sent(): return lax.ppermute(value, AXES, [(i, target(i) % count) for i in senders])  52.2 us
    dot_general x9, matrix products, contract(): lax.dot_general(left_rows, right_rows, (((1,), (1,)), ((), ())), preferre...  20.6 us
    pallas_call x1, Pallas kernels, per_device(): pl.pallas_call(kernel, grid=(parts,), out_shape=(jax.ShapeDtypeStruct((si...  13.9 us
    unnamed x38, local copies, waits for them, and re-layouts  12.6 us
    pallas_call x1, Pallas kernels, per_device(): pl.pallas_call(last_tiles, out_shape=(square,) * 5 + (jax.ShapeDtypeStruc...  7.69 us
    pallas_call x1, Pallas kernels, per_device(): pl.pallas_call(early_tiles, out_shape=(square,) * 6 + (column,) * 4 + (ro...  7.38 us
  transfers between devices with their start and end apart: 20, of which 9 were waited for; matrix products, arithmetic and copies ran while one was open for 11% of the time, Pallas kernels for 3%

profile of v7, /device:TPU:0, one launch (start us, length us, event | category | flops | bytes accessed | tf_op | source)
XLA Modules:
  0.0 223.8 jit_solution(15057193231086948754)
XLA Ops:
  2.7 10.8 %collective-permute-start.2 = (bf16[256,4096]{1,0:T(8,128)(2,1)}, bf16[256,4096]{1,0:T(8,128)(2,1)}, u32[]{:S(2)}, u32[]{:S(2)}) collective-permute-start(bf16[256,4096]{1,0:T(8,128)(2,1)} %refs_25_.1), channel_id=1, source_target_pairs={{0,255},{127,128},{128,127},{255,0}} | collective-permute-start | bytes 6291464 | tf_op jit(solution)/shard_map/ppermute | solution.py:27
  15.6 3.1 %convolution_multiply_fusion.6 = f32[256,256]{0,1:T(8,128)S(1)} fusion(bf16[256,4096]{1,0:T(8,128)(2,1)} %refs_26_.1, bf16[256,4096]{1,0:T(8,128)(2,1)} %refs_25_.1), kind=kOutput, calls=%fused_computation.12 | convolution fusion | flops 536936448 | bytes 4456448 | tf_op jit(solution)/shard_map/dot_general | solution.py:19
  22.0 46.9 %collective-permute-done.3 = bf16[256,4096]{1,0:T(8,128)(2,1)} collective-permute-done((bf16[256,4096]{1,0:T(8,128)(2,1)}, bf16[256,4096]{1,0:T(8,128)(2,1)}, u32[]{:S(2)}, u32[]{:S(2)}) %collective-permute-start.3) | collective-permute-done | bytes 2097184 | tf_op jit(solution)/shard_map/ppermute | solution.py:27
  69.0 4.1 %collective-permute-done.4 = bf16[256,4096]{1,0:T(8,128)(2,1)} collective-permute-done((bf16[256,4096]{1,0:T(8,128)(2,1)}, bf16[256,4096]{1,0:T(8,128)(2,1)}, u32[]{:S(2)}, u32[]{:S(2)}) %collective-permute-start.4) | collective-permute-done | bytes 2097184 | tf_op jit(solution)/shard_map/ppermute | solution.py:27
  76.4 4.7 %collective-permute-start.10 = (bf16[256,4096]{1,0:T(8,128)(2,1)S(1)}, bf16[256,4096]{1,0:T(8,128)(2,1)S(1)}, u32[]{:S(2)}, u32[]{:S(2)}) collective-permute-start(bf16[256,4096]{1,0:T(8,128)(2,1)S(1)} %copy-done), channel_id=1, source_target_pairs={{0,2},{1,3},{2,4},{3,5},{4,6},{5,7},{6,8},{7,9},{8,10},{9,11},{10,... | collective-permute-start | bytes 6291464 | tf_op jit(solution)/shard_map/ppermute | solution.py:27
  81.1 2.7 %collective-permute-start.9 = (bf16[256,4096]{1,0:T(8,128)(2,1)S(1)}, bf16[256,4096]{1,0:T(8,128)(2,1)}, u32[]{:S(2)}, u32[]{:S(2)}) collective-permute-start(bf16[256,4096]{1,0:T(8,128)(2,1)S(1)} %copy-done), channel_id=1, source_target_pairs={{0,134},{1,135},{126,248},{127,249},{128,6},{129,7},{254,120},{255... | collective-permute-start | bytes 6291464 | tf_op jit(solution)/shard_map/ppermute | solution.py:27
  83.8 3.0 %fusion.refs_2_ = f32[256,256]{1,0:T(8,128)} fusion(bf16[256,4096]{1,0:T(8,128)(2,1)} %collective-permute-done.2.refs_33_, bf16[256,4096]{1,0:T(8,128)(2,1)S(1)} %copy-done.1), kind=kOutput, calls=%fused_computation.1 | convolution fusion | flops 536936448 | bytes 4456448 | tf_op jit(solution)/shard_map/dot_general | solution.py:19
  86.8 3.0 %fusion.1.refs_1_ = f32[256,256]{1,0:T(8,128)} fusion(bf16[256,4096]{1,0:T(8,128)(2,1)} %collective-permute-done.2.refs_33_, bf16[256,4096]{1,0:T(8,128)(2,1)S(1)} %copy-done), kind=kOutput, calls=%fused_computation.3 | convolution fusion | flops 536936448 | bytes 4456448 | tf_op jit(solution)/shard_map/dot_general | solution.py:19
  89.8 2.3 %fusion.3.refs_7_ = f32[256,256]{1,0:T(8,128)S(1)} fusion(bf16[256,4096]{1,0:T(8,128)(2,1)} %collective-permute-done.1.refs_28_, bf16[256,4096]{1,0:T(8,128)(2,1)S(1)} %copy-done.1), kind=kOutput, calls=%fused_computation.7 | convolution fusion | flops 536936448 | bytes 4456448 | tf_op jit(solution)/shard_map/dot_general | solution.py:19
  92.2 3.1 %fusion.4.refs_6_ = f32[256,256]{1,0:T(8,128)} fusion(bf16[256,4096]{1,0:T(8,128)(2,1)} %collective-permute-done.1.refs_28_, bf16[256,4096]{1,0:T(8,128)(2,1)S(1)} %copy-done), kind=kOutput, calls=%fused_computation.9 | convolution fusion | flops 536936448 | bytes 4456448 | tf_op jit(solution)/shard_map/dot_general | solution.py:19
  95.2 3.0 %fusion.2.refs_8_ = f32[256,256]{1,0:T(8,128)} fusion(bf16[256,4096]{1,0:T(8,128)(2,1)} %collective-permute-done.refs_30_, bf16[256,4096]{1,0:T(8,128)(2,1)S(1)} %copy-done.1), kind=kOutput, calls=%fused_computation.5 | convolution fusion | flops 536936448 | bytes 4456448 | tf_op jit(solution)/shard_map/dot_general | solution.py:19
  98.3 2.4 %slice_select_fusion = (bf16[256,2048]{1,0:T(8,128)(2,1)S(1)}, bf16[256,2048]{1,0:T(8,128)(2,1)S(1)}) fusion(bf16[256,4096]{1,0:T(8,128)(2,1)} %collective-permute-done.refs_30_, bf16[256,4096]{1,0:T(8,128)(2,1)} %collective-permute-done.1.refs_28_, pred[]{:T(512)} %eq.31), kind=kLoop, calls=%fused_computation.16 | loop fusion | flops 1048576 | bytes 6291457 | tf_op jit(solution)/shard_map/jit(_where)/select_n | solution.py:347
  100.7 18.9 %collective-permute-done.5.refs_13_.refs_31_ = bf16[256,4096]{1,0:T(8,128)(2,1)} collective-permute-done((bf16[256,4096]{1,0:T(8,128)(2,1)}, bf16[256,4096]{1,0:T(8,128)(2,1)}, u32[]{:S(2)}, u32[]{:S(2)}) %collective-permute-start.5) | collective-permute-done | bytes 2097184 | tf_op jit(solution)/shard_map/ppermute | solution.py:27
  122.5 2.7 %collective-permute-start.8 = (bf16[256,2048]{1,0:T(8,128)(2,1)S(1)}, bf16[256,2048]{1,0:T(8,128)(2,1)}, u32[]{:S(2)}, u32[]{:S(2)}) collective-permute-start(bf16[256,2048]{1,0:T(8,128)(2,1)S(1)} %get-tuple-element.64), channel_id=1, source_target_pairs={{0,129},{1,128},{2,131},{3,130},{4,133},{5,132},{6,135},{7,134},{8... | collective-permute-start | bytes 3145736 | tf_op jit(solution)/shard_map/ppermute | solution.py:27
  126.5 2.7 %collective-permute-start.12 = (bf16[256,4096]{1,0:T(8,128)(2,1)}, bf16[256,4096]{1,0:T(8,128)(2,1)}, u32[]{:S(2)}, u32[]{:S(2)}) collective-permute-start(bf16[256,4096]{1,0:T(8,128)(2,1)} %collective-permute-done.5.refs_13_.refs_31_), channel_id=1, source_target_pairs={{0,2},{2,4},{3,1},{4,6},{5,3},{6,8},{7,5},{8,10},{9,7},{10,12},{11... | collective-permute-start | bytes 6291464 | tf_op jit(solution)/shard_map/ppermute | solution.py:27
  130.5 15.5 %collective-permute-done.7 = bf16[256,2048]{1,0:T(8,128)(2,1)} collective-permute-done((bf16[256,2048]{1,0:T(8,128)(2,1)S(1)}, bf16[256,2048]{1,0:T(8,128)(2,1)}, u32[]{:S(2)}, u32[]{:S(2)}) %collective-permute-start.7) | collective-permute-done | bytes 1048608 | tf_op jit(solution)/shard_map/ppermute | solution.py:27
  147.5 6.1 %collective-permute-start.14 = (bf16[256,2048]{1,0:T(8,128)(2,1)}, bf16[256,2048]{1,0:T(8,128)(2,1)}, u32[]{:S(2)}, u32[]{:S(2)}) collective-permute-start(bf16[256,2048]{1,0:T(8,128)(2,1)} %collective-permute-done.8), channel_id=1, source_target_pairs={{0,129},{1,128},{2,131},{3,130},{4,133},{5,132},{6,135},{7,134},{8... | collective-permute-start | bytes 3145736 | tf_op jit(solution)/shard_map/ppermute | solution.py:27
  163.4 7.4 %shard_map.58 = (f32[256,256]{1,0:T(8,128)S(1)}, f32[256,256]{1,0:T(8,128)S(1)}, f32[256,256]{1,0:T(8,128)S(1)}, f32[256,256]{1,0:T(8,128)S(1)}, f32[256,256]{1,...) custom-call(s32[4]{0:T(128)S(1)} %add_convert_fusion.refs_0_, ...), custom_call_target="tpu_custom_call" | custom-call | flops 3221225472 | bytes 12582912 | tf_op jit(solution)/shard_map/pallas_call | solution.py:377
  171.3 4.3 %collective-permute-done.13.refs_11_.refs_34_ = bf16[256,2048]{1,0:T(8,128)(2,1)} collective-permute-done((bf16[256,2048]{1,0:T(8,128)(2,1)}, bf16[256,2048]{1,0:T(8,128)(2,1)}, u32[]{:S(2)}, u32[]{:S(2)}) %collective-permute-start.13) | collective-permute-done | bytes 1048608 | tf_op jit(solution)/shard_map/ppermute | solution.py:27
  175.6 11.8 %collective-permute-done.15.refs_13_.refs_37_ = bf16[256,4096]{1,0:T(8,128)(2,1)} collective-permute-done((bf16[256,4096]{1,0:T(8,128)(2,1)}, bf16[256,4096]{1,0:T(8,128)(2,1)}, u32[]{:S(2)}, u32[]{:S(2)}) %collective-permute-start.15) | collective-permute-done | bytes 2097184 | tf_op jit(solution)/shard_map/ppermute | solution.py:27
  187.5 7.7 %shard_map.59 = (f32[256,256]{1,0:T(8,128)S(1)}, f32[256,256]{1,0:T(8,128)S(1)}, f32[256,256]{1,0:T(8,128)S(1)}, f32[256,256]{1,0:T(8,128)S(1)}, f32[256,256]{1,...) custom-call(s32[4]{0:T(128)S(1)} %add_convert_fusion.refs_0_, f32[256,256]{1,0:T(8,128)S(1)} %copy-done.17, ...), custom_call_target="tpu_custom_call" | custom-call | flops 1610612736 | bytes 8388608 | tf_op jit(solution)/shard_map/pallas_call | solution.py:408
  195.3 6.0 %collective-permute-start.18 = (f32[2,256]{1,0:T(2,128)S(1)}, f32[2,256]{1,0:T(2,128)S(1)}, u32[]{:S(2)}, u32[]{:S(2)}) collective-permute-start(f32[2,256]{1,0:T(2,128)S(1)} %get-tuple-element.92.refs_20_), channel_id=1, source_target_pairs={{0,254},{1,255},{2,0},{3,1},{4,2},{5,3},{6,4},{7,5},{8,6},{9,7},{1... | collective-permute-start | bytes 6152 | tf_op jit(solution)/shard_map/ppermute | solution.py:27
  201.2 7.2 %collective-permute-start.16 = (f32[2,256]{1,0:T(2,128)S(1)}, f32[2,256]{1,0:T(2,128)S(1)}, u32[]{:S(2)}, u32[]{:S(2)}) collective-permute-start(f32[2,256]{1,0:T(2,128)S(1)} %get-tuple-element.92.refs_20_), channel_id=1, source_target_pairs={{0,255},{1,0},{2,1},{3,2},{4,3},{5,4},{6,5},{7,6},{8,7},{9,8},{10,... | collective-permute-start | bytes 6152 | tf_op jit(solution)/shard_map/ppermute | solution.py:27
  209.7 13.9 %shard_map.60 = (f32[256,4096]{1,0:T(8,128)}, f32[256,4096]{1,0:T(8,128)}) custom-call(s32[4]{0:T(128)S(1)} %add_convert_fusion.refs_0_, s32[1,256]{1,0:T(1,128)S(1)} %bitcast.35, f32[256,256]{1,0:T(8,128)S(1)} %copy.15.refs_2_, f32[256,256]{1,0:T(8,128)S(1)} %copy.16.refs_3_, f32[256,256]{1,0:T(8,128)S(1)} %copy.17.refs_4_, f32[256,256]{1,0:T(8,128)S(1)} %copy.18.refs_5_, ...), custom_call_target="tpu_custom_call" | custom-call | flops 8589934592 | bytes 29360128 | tf_op jit(solution)/shard_map/pallas_call | solution.py:449
  (73 shorter events, 29.5 us)
Async XLA Ops:
  0.6 68.3 %collective-permute-start.3 = (bf16[256,4096]{1,0:T(8,128)(2,1)}, bf16[256,4096]{1,0:T(8,128)(2,1)}, u32[]{:S(2)}, u32[]{:S(2)}) collective-permute-start(bf16[256,4096]{1,0:T(8,128)(2,1)} %refs_25_.1), channel_id=1, source_target_pairs={{0,129},{1,128},{2,131},{3,130},{4,133},{5,132},{6,135},{7,134},{8... | collective-permute-start | bytes 6291464 | tf_op jit(solution)/shard_map/ppermute | solution.py:27
  2.0 71.1 %collective-permute-start.4 = (bf16[256,4096]{1,0:T(8,128)(2,1)}, bf16[256,4096]{1,0:T(8,128)(2,1)}, u32[]{:S(2)}, u32[]{:S(2)}) collective-permute-start(bf16[256,4096]{1,0:T(8,128)(2,1)} %refs_26_.1), channel_id=1, source_target_pairs={{0,128},{1,129},{2,130},{3,131},{4,132},{5,133},{6,134},{7,135},{8... | collective-permute-start | bytes 6291464 | tf_op jit(solution)/shard_map/ppermute | solution.py:27
  2.7 72.4 %collective-permute-start.2 = (bf16[256,4096]{1,0:T(8,128)(2,1)}, bf16[256,4096]{1,0:T(8,128)(2,1)}, u32[]{:S(2)}, u32[]{:S(2)}) collective-permute-start(bf16[256,4096]{1,0:T(8,128)(2,1)} %refs_25_.1), channel_id=1, source_target_pairs={{0,255},{127,128},{128,127},{255,0}} | collective-permute-start | bytes 6291464 | tf_op jit(solution)/shard_map/ppermute | solution.py:27
  13.5 61.6 %collective-permute-start.1 = (bf16[256,4096]{1,0:T(8,128)(2,1)}, bf16[256,4096]{1,0:T(8,128)(2,1)}, u32[]{:S(2)}, u32[]{:S(2)}) collective-permute-start(bf16[256,4096]{1,0:T(8,128)(2,1)} %refs_26_.1), channel_id=1, source_target_pairs={{0,254},{1,255},{2,0},{3,1},{4,2},{5,3},{6,4},{7,5},{8,6},{9,7},{1... | collective-permute-start | bytes 6291464 | tf_op jit(solution)/shard_map/ppermute | solution.py:27
  13.6 61.5 %collective-permute-start = (bf16[256,4096]{1,0:T(8,128)(2,1)}, bf16[256,4096]{1,0:T(8,128)(2,1)}, u32[]{:S(2)}, u32[]{:S(2)}) collective-permute-start(bf16[256,4096]{1,0:T(8,128)(2,1)} %refs_26_.1), channel_id=1, source_target_pairs={{0,2},{1,3},{2,4},{3,5},{4,6},{5,7},{6,8},{7,9},{8,10},{9,11},{10,... | collective-permute-start | bytes 6291464 | tf_op jit(solution)/shard_map/ppermute | solution.py:27
  73.1 46.5 %collective-permute-start.5 = (bf16[256,4096]{1,0:T(8,128)(2,1)}, bf16[256,4096]{1,0:T(8,128)(2,1)}, u32[]{:S(2)}, u32[]{:S(2)}) collective-permute-start(bf16[256,4096]{1,0:T(8,128)(2,1)} %collective-permute-done.3), channel_id=1, source_target_pairs={{0,129},{1,128},{2,131},{3,130},{4,133},{5,132},{6,135},{7,134},{8... | collective-permute-start | bytes 6291464 | tf_op jit(solution)/shard_map/ppermute | solution.py:27
  73.1 47.6 %collective-permute-start.6 = (bf16[256,4096]{1,0:T(8,128)(2,1)}, bf16[256,4096]{1,0:T(8,128)(2,1)S(1)}, u32[]{:S(2)}, u32[]{:S(2)}) collective-permute-start(bf16[256,4096]{1,0:T(8,128)(2,1)} %collective-permute-done.4), channel_id=1, source_target_pairs={{0,128},{1,129},{2,130},{3,131},{4,132},{5,133},{6,134},{7,135},{8... | collective-permute-start | bytes 6291464 | tf_op jit(solution)/shard_map/ppermute | solution.py:27
  75.1 50.1 %collective-permute-start.11 = (bf16[256,4096]{1,0:T(8,128)(2,1)S(1)}, bf16[256,4096]{1,0:T(8,128)(2,1)S(1)}, u32[]{:S(2)}, u32[]{:S(2)}) collective-permute-start(bf16[256,4096]{1,0:T(8,128)(2,1)S(1)} %copy-done), channel_id=1, source_target_pairs={{2,0},{3,1},{4,2},{5,3},{6,4},{7,5},{8,6},{9,7},{10,8},{11,9},{12,... | collective-permute-start | bytes 6291464 | tf_op jit(solution)/shard_map/ppermute | solution.py:27
  76.4 52.8 %collective-permute-start.10 = (bf16[256,4096]{1,0:T(8,128)(2,1)S(1)}, bf16[256,4096]{1,0:T(8,128)(2,1)S(1)}, u32[]{:S(2)}, u32[]{:S(2)}) collective-permute-start(bf16[256,4096]{1,0:T(8,128)(2,1)S(1)} %copy-done), channel_id=1, source_target_pairs={{0,2},{1,3},{2,4},{3,5},{4,6},{5,7},{6,8},{7,9},{8,10},{9,11},{10,... | collective-permute-start | bytes 6291464 | tf_op jit(solution)/shard_map/ppermute | solution.py:27
  81.1 49.4 %collective-permute-start.9 = (bf16[256,4096]{1,0:T(8,128)(2,1)S(1)}, bf16[256,4096]{1,0:T(8,128)(2,1)}, u32[]{:S(2)}, u32[]{:S(2)}) collective-permute-start(bf16[256,4096]{1,0:T(8,128)(2,1)S(1)} %copy-done), channel_id=1, source_target_pairs={{0,134},{1,135},{126,248},{127,249},{128,6},{129,7},{254,120},{255... | collective-permute-start | bytes 6291464 | tf_op jit(solution)/shard_map/ppermute | solution.py:27
  98.3 55.4 %copy-start.18 = (s32[256]{0:T(256)S(1)}, s32[256]{0:T(256)}, u32[]{:S(2)}) copy-start(s32[256]{0:T(256)} %param.5) | copy-start | bytes 3076
  122.0 24.1 %collective-permute-start.7 = (bf16[256,2048]{1,0:T(8,128)(2,1)S(1)}, bf16[256,2048]{1,0:T(8,128)(2,1)}, u32[]{:S(2)}, u32[]{:S(2)}) collective-permute-start(bf16[256,2048]{1,0:T(8,128)(2,1)S(1)} %get-tuple-element.63), channel_id=1, source_target_pairs={{0,128},{1,129},{2,130},{3,131},{4,132},{5,133},{6,134},{7,135},{8... | collective-permute-start | bytes 3145736 | tf_op jit(solution)/shard_map/ppermute | solution.py:27
  122.5 23.6 %collective-permute-start.8 = (bf16[256,2048]{1,0:T(8,128)(2,1)S(1)}, bf16[256,2048]{1,0:T(8,128)(2,1)}, u32[]{:S(2)}, u32[]{:S(2)}) collective-permute-start(bf16[256,2048]{1,0:T(8,128)(2,1)S(1)} %get-tuple-element.64), channel_id=1, source_target_pairs={{0,129},{1,128},{2,131},{3,130},{4,133},{5,132},{6,135},{7,134},{8... | collective-permute-start | bytes 3145736 | tf_op jit(solution)/shard_map/ppermute | solution.py:27
  126.5 44.7 %collective-permute-start.12 = (bf16[256,4096]{1,0:T(8,128)(2,1)}, bf16[256,4096]{1,0:T(8,128)(2,1)}, u32[]{:S(2)}, u32[]{:S(2)}) collective-permute-start(bf16[256,4096]{1,0:T(8,128)(2,1)} %collective-permute-done.5.refs_13_.refs_31_), channel_id=1, source_target_pairs={{0,2},{2,4},{3,1},{4,6},{5,3},{6,8},{7,5},{8,10},{9,7},{10,12},{11... | collective-permute-start | bytes 6291464 | tf_op jit(solution)/shard_map/ppermute | solution.py:27
  146.1 41.3 %collective-permute-start.15 = (bf16[256,4096]{1,0:T(8,128)(2,1)}, bf16[256,4096]{1,0:T(8,128)(2,1)}, u32[]{:S(2)}, u32[]{:S(2)}) collective-permute-start(bf16[256,4096]{1,0:T(8,128)(2,1)} %collective-permute-done.9), channel_id=1, source_target_pairs={{6,126},{7,127},{120,0},{121,1},{134,254},{135,255},{248,128},{249... | collective-permute-start | bytes 6291464 | tf_op jit(solution)/shard_map/ppermute | solution.py:27
  147.4 28.2 %collective-permute-start.13 = (bf16[256,2048]{1,0:T(8,128)(2,1)}, bf16[256,2048]{1,0:T(8,128)(2,1)}, u32[]{:S(2)}, u32[]{:S(2)}) collective-permute-start(bf16[256,2048]{1,0:T(8,128)(2,1)} %collective-permute-done.7), channel_id=1, source_target_pairs={{0,128},{1,129},{2,130},{3,131},{4,132},{5,133},{6,134},{7,135},{8... | collective-permute-start | bytes 3145736 | tf_op jit(solution)/shard_map/ppermute | solution.py:27
  147.5 28.1 %collective-permute-start.14 = (bf16[256,2048]{1,0:T(8,128)(2,1)}, bf16[256,2048]{1,0:T(8,128)(2,1)}, u32[]{:S(2)}, u32[]{:S(2)}) collective-permute-start(bf16[256,2048]{1,0:T(8,128)(2,1)} %collective-permute-done.8), channel_id=1, source_target_pairs={{0,129},{1,128},{2,131},{3,130},{4,133},{5,132},{6,135},{7,134},{8... | collective-permute-start | bytes 3145736 | tf_op jit(solution)/shard_map/ppermute | solution.py:27
  163.4 24.0 %copy-start.16 = (f32[256,256]{1,0:T(8,128)S(1)}, f32[256,256]{1,0:T(8,128)}, u32[]{:S(2)}) copy-start(f32[256,256]{1,0:T(8,128)} %fusion.refs_2_) | copy-start | bytes 786436
  163.4 24.0 %copy-start.17 = (f32[256,256]{1,0:T(8,128)S(1)}, f32[256,256]{1,0:T(8,128)}, u32[]{:S(2)}) copy-start(f32[256,256]{1,0:T(8,128)} %fusion.1.refs_1_) | copy-start | bytes 786436
  187.4 22.3 %copy-start.8 = (bf16[256,4096]{1,0:T(8,128)(2,1)S(1)}, bf16[256,4096]{1,0:T(8,128)(2,1)}, u32[]{:S(2)}) copy-start(bf16[256,4096]{1,0:T(8,128)(2,1)} %copy-done.6) | copy-start | bytes 6291460
  195.2 13.2 %collective-permute-start.19 = (f32[2,256]{1,0:T(2,128)S(1)}, f32[2,256]{1,0:T(2,128)S(1)}, u32[]{:S(2)}, u32[]{:S(2)}) collective-permute-start(f32[2,256]{1,0:T(2,128)S(1)} %get-tuple-element.92.refs_20_), channel_id=1, source_target_pairs={{0,2},{1,3},{2,4},{3,5},{4,6},{5,7},{6,8},{7,9},{8,10},{9,11},{10,... | collective-permute-start | bytes 6152 | tf_op jit(solution)/shard_map/ppermute | solution.py:27
  195.3 13.1 %collective-permute-start.18 = (f32[2,256]{1,0:T(2,128)S(1)}, f32[2,256]{1,0:T(2,128)S(1)}, u32[]{:S(2)}, u32[]{:S(2)}) collective-permute-start(f32[2,256]{1,0:T(2,128)S(1)} %get-tuple-element.92.refs_20_), channel_id=1, source_target_pairs={{0,254},{1,255},{2,0},{3,1},{4,2},{5,3},{6,4},{7,5},{8,6},{9,7},{1... | collective-permute-start | bytes 6152 | tf_op jit(solution)/shard_map/ppermute | solution.py:27
  201.2 8.4 %collective-permute-start.17 = (f32[2,256]{1,0:T(2,128)S(1)}, f32[2,256]{1,0:T(2,128)S(1)}, u32[]{:S(2)}, u32[]{:S(2)}) collective-permute-start(f32[2,256]{1,0:T(2,128)S(1)} %get-tuple-element.92.refs_20_), channel_id=1, source_target_pairs={{0,1},{1,2},{2,3},{3,4},{4,5},{5,6},{6,7},{7,8},{8,9},{9,10},{10,1... | collective-permute-start | bytes 6152 | tf_op jit(solution)/shard_map/ppermute | solution.py:27
  201.2 8.5 %collective-permute-start.16 = (f32[2,256]{1,0:T(2,128)S(1)}, f32[2,256]{1,0:T(2,128)S(1)}, u32[]{:S(2)}, u32[]{:S(2)}) collective-permute-start(f32[2,256]{1,0:T(2,128)S(1)} %get-tuple-element.92.refs_20_), channel_id=1, source_target_pairs={{0,255},{1,0},{2,1},{3,2},{4,3},{5,4},{6,5},{7,6},{8,7},{9,8},{10,... | collective-permute-start | bytes 6152 | tf_op jit(solution)/shard_map/ppermute | solution.py:27
  (15 other events, 107.9 us)

commit v8 on v6

--- a/solution.py
+++ b/solution.py
@@ -174,7 +174,7 @@
 
 def grad_kernel(factor, place, pos, *refs):
     tiles, refs = refs[:TILES], refs[TILES:]
-    lse, lse_n1, lse_p1, lse_n2, lse_p2 = refs[:5]
+    lse, lse_n2, lse_p2, lse_n1, lse_p1 = refs[:5]
     own_q, own_d, q_n2, d_n2, q_p2, d_p2, q_pair, d_pair = refs[5:13]
     q_edge, d_low, d_high, q_diag, q_swap = refs[13:18]
     grad_q, grad_d, coef_q, coef_d, rows, arrived = refs[18:]
@@ -428,10 +428,10 @@
         q_swap,
     )
     tiles = [*own_tiles, *far_tiles[:3], *early, *late]
+    lse_n2 = sent(lse, lambda i: i - 2)
+    lse_p2 = sent(lse, lambda i: i + 2)
     lse_n1 = sent(lse, lambda i: i - 1)
     lse_p1 = sent(lse, lambda i: i + 1)
-    lse_n2 = sent(lse, lambda i: i - 2)
-    lse_p2 = sent(lse, lambda i: i + 2)
     sources = [queries, documents, q_n2, d_n2, q_p2, d_p2, q_pair, d_pair]
     sources += [q_edge, d_low, d_high, q_diag, q_swap]
     parts = width // CHUNK
@@ -458,7 +458,7 @@
             bytes_accessed=(20 + 8) * size * width,
             transcendentals=32 * size * size,
         ),
-    )(place, pos, *tiles, lse, lse_n1, lse_p1, lse_n2, lse_p2, *sources)
+    )(place, pos, *tiles, lse, lse_n2, lse_p2, lse_n1, lse_p1, *sources)
     return (row_terms.reshape(size), grad_q, grad_d)
 
 

time: 224 us -> 224 us (level)
  no operation moved by 1% of the time
where the time goes in v8:
time: 224 us; the launch traced here: 223 us
  waiting for transfers between devices  106 us (47%)
  starting transfers between devices  53.4 us (24%)
  Pallas kernels  28.1 us (13%)
  matrix products  20.5 us (9%)
  local copies, waits for them, and re-layouts  11.2 us (5%)
  other arithmetic  2.47 us (1%)
    ppermute x20, waiting for transfers between devices, sent(): return lax.ppermute(value, AXES, [(i, target(i) % count) for i in senders])  106 us
    ppermute x20, starting transfers between devices, sent(): return lax.ppermute(value, AXES, [(i, target(i) % count) for i in senders])  53.4 us
    dot_general x9, matrix products, contract(): lax.dot_general(left_rows, right_rows, (((1,), (1,)), ((), ())), preferre...  20.5 us
    pallas_call x1, Pallas kernels, per_device(): pl.pallas_call(kernel, grid=(parts,), out_shape=(jax.ShapeDtypeStruct((si...  13.7 us
    unnamed x32, local copies, waits for them, and re-layouts  9.72 us
    pallas_call x1, Pallas kernels, per_device(): pl.pallas_call(early_tiles, out_shape=(square,) * 6 + (column,) * 4 + (ro...  7.24 us
    pallas_call x1, Pallas kernels, per_device(): pl.pallas_call(last_tiles, out_shape=(square,) * 5 + (jax.ShapeDtypeStruc...  7.13 us
  transfers between devices with their start and end apart: 20, of which 9 were waited for; matrix products, arithmetic and copies ran while one was open for 11% of the time, Pallas kernels for 3%

profile of v8, /device:TPU:0, one launch (start us, length us, event | category | flops | bytes accessed | tf_op | source)
XLA Modules:
  0.0 223.0 jit_solution(15917325435349141819)
XLA Ops:
  2.7 10.8 %collective-permute-start.2 = (bf16[256,4096]{1,0:T(8,128)(2,1)}, bf16[256,4096]{1,0:T(8,128)(2,1)}, u32[]{:S(2)}, u32[]{:S(2)}) collective-permute-start(bf16[256,4096]{1,0:T(8,128)(2,1)} %refs_25_.1), channel_id=1, source_target_pairs={{0,255},{127,128},{128,127},{255,0}} | collective-permute-start | bytes 6291464 | tf_op jit(solution)/shard_map/ppermute | solution.py:27
  15.6 3.1 %convolution_multiply_fusion.6 = f32[256,256]{0,1:T(8,128)S(1)} fusion(bf16[256,4096]{1,0:T(8,128)(2,1)} %refs_26_.1, bf16[256,4096]{1,0:T(8,128)(2,1)} %refs_25_.1), kind=kOutput, calls=%fused_computation.12 | convolution fusion | flops 536936448 | bytes 4456448 | tf_op jit(solution)/shard_map/dot_general | solution.py:19
  22.0 46.9 %collective-permute-done.3 = bf16[256,4096]{1,0:T(8,128)(2,1)} collective-permute-done((bf16[256,4096]{1,0:T(8,128)(2,1)}, bf16[256,4096]{1,0:T(8,128)(2,1)}, u32[]{:S(2)}, u32[]{:S(2)}) %collective-permute-start.3) | collective-permute-done | bytes 2097184 | tf_op jit(solution)/shard_map/ppermute | solution.py:27
  69.0 4.1 %collective-permute-done.4 = bf16[256,4096]{1,0:T(8,128)(2,1)} collective-permute-done((bf16[256,4096]{1,0:T(8,128)(2,1)}, bf16[256,4096]{1,0:T(8,128)(2,1)}, u32[]{:S(2)}, u32[]{:S(2)}) %collective-permute-start.4) | collective-permute-done | bytes 2097184 | tf_op jit(solution)/shard_map/ppermute | solution.py:27
  76.4 4.7 %collective-permute-start.10 = (bf16[256,4096]{1,0:T(8,128)(2,1)S(1)}, bf16[256,4096]{1,0:T(8,128)(2,1)S(1)}, u32[]{:S(2)}, u32[]{:S(2)}) collective-permute-start(bf16[256,4096]{1,0:T(8,128)(2,1)S(1)} %copy-done), channel_id=1, source_target_pairs={{0,2},{1,3},{2,4},{3,5},{4,6},{5,7},{6,8},{7,9},{8,10},{9,11},{10,... | collective-permute-start | bytes 6291464 | tf_op jit(solution)/shard_map/ppermute | solution.py:27
  81.1 2.6 %collective-permute-start.9 = (bf16[256,4096]{1,0:T(8,128)(2,1)S(1)}, bf16[256,4096]{1,0:T(8,128)(2,1)}, u32[]{:S(2)}, u32[]{:S(2)}) collective-permute-start(bf16[256,4096]{1,0:T(8,128)(2,1)S(1)} %copy-done), channel_id=1, source_target_pairs={{0,134},{1,135},{126,248},{127,249},{128,6},{129,7},{254,120},{255... | collective-permute-start | bytes 6291464 | tf_op jit(solution)/shard_map/ppermute | solution.py:27
  83.7 3.0 %fusion.refs_2_ = f32[256,256]{1,0:T(8,128)} fusion(bf16[256,4096]{1,0:T(8,128)(2,1)} %collective-permute-done.2.refs_33_, bf16[256,4096]{1,0:T(8,128)(2,1)S(1)} %copy-done.1), kind=kOutput, calls=%fused_computation.1 | convolution fusion | flops 536936448 | bytes 4456448 | tf_op jit(solution)/shard_map/dot_general | solution.py:19
  86.7 3.0 %fusion.1.refs_1_ = f32[256,256]{1,0:T(8,128)} fusion(bf16[256,4096]{1,0:T(8,128)(2,1)} %collective-permute-done.2.refs_33_, bf16[256,4096]{1,0:T(8,128)(2,1)S(1)} %copy-done), kind=kOutput, calls=%fused_computation.3 | convolution fusion | flops 536936448 | bytes 4456448 | tf_op jit(solution)/shard_map/dot_general | solution.py:19
  89.8 2.3 %fusion.3.refs_7_ = f32[256,256]{1,0:T(8,128)S(1)} fusion(bf16[256,4096]{1,0:T(8,128)(2,1)} %collective-permute-done.1.refs_28_, bf16[256,4096]{1,0:T(8,128)(2,1)S(1)} %copy-done.1), kind=kOutput, calls=%fused_computation.7 | convolution fusion | flops 536936448 | bytes 4456448 | tf_op jit(solution)/shard_map/dot_general | solution.py:19
  92.1 3.0 %fusion.4.refs_6_ = f32[256,256]{1,0:T(8,128)} fusion(bf16[256,4096]{1,0:T(8,128)(2,1)} %collective-permute-done.1.refs_28_, bf16[256,4096]{1,0:T(8,128)(2,1)S(1)} %copy-done), kind=kOutput, calls=%fused_computation.9 | convolution fusion | flops 536936448 | bytes 4456448 | tf_op jit(solution)/shard_map/dot_general | solution.py:19
  95.2 3.0 %fusion.2.refs_8_ = f32[256,256]{1,0:T(8,128)} fusion(bf16[256,4096]{1,0:T(8,128)(2,1)} %collective-permute-done.refs_30_, bf16[256,4096]{1,0:T(8,128)(2,1)S(1)} %copy-done.1), kind=kOutput, calls=%fused_computation.5 | convolution fusion | flops 536936448 | bytes 4456448 | tf_op jit(solution)/shard_map/dot_general | solution.py:19
  98.2 2.4 %slice_select_fusion = (bf16[256,2048]{1,0:T(8,128)(2,1)S(1)}, bf16[256,2048]{1,0:T(8,128)(2,1)S(1)}) fusion(bf16[256,4096]{1,0:T(8,128)(2,1)} %collective-permute-done.refs_30_, bf16[256,4096]{1,0:T(8,128)(2,1)} %collective-permute-done.1.refs_28_, pred[]{:T(512)} %eq.31), kind=kLoop, calls=%fused_computation.16 | loop fusion | flops 1048576 | bytes 6291457 | tf_op jit(solution)/shard_map/jit(_where)/select_n | solution.py:341
  100.6 19.0 %collective-permute-done.5.refs_13_.refs_31_ = bf16[256,4096]{1,0:T(8,128)(2,1)} collective-permute-done((bf16[256,4096]{1,0:T(8,128)(2,1)}, bf16[256,4096]{1,0:T(8,128)(2,1)}, u32[]{:S(2)}, u32[]{:S(2)}) %collective-permute-start.5) | collective-permute-done | bytes 2097184 | tf_op jit(solution)/shard_map/ppermute | solution.py:27
  121.2 2.7 %collective-permute-start.8 = (bf16[256,2048]{1,0:T(8,128)(2,1)S(1)}, bf16[256,2048]{1,0:T(8,128)(2,1)}, u32[]{:S(2)}, u32[]{:S(2)}) collective-permute-start(bf16[256,2048]{1,0:T(8,128)(2,1)S(1)} %get-tuple-element.64), channel_id=1, source_target_pairs={{0,129},{1,128},{2,131},{3,130},{4,133},{5,132},{6,135},{7,134},{8... | collective-permute-start | bytes 3145736 | tf_op jit(solution)/shard_map/ppermute | solution.py:27
  125.2 2.6 %collective-permute-start.12 = (bf16[256,4096]{1,0:T(8,128)(2,1)}, bf16[256,4096]{1,0:T(8,128)(2,1)}, u32[]{:S(2)}, u32[]{:S(2)}) collective-permute-start(bf16[256,4096]{1,0:T(8,128)(2,1)} %collective-permute-done.5.refs_13_.refs_31_), channel_id=1, source_target_pairs={{0,2},{2,4},{3,1},{4,6},{5,3},{6,8},{7,5},{8,10},{9,7},{10,12},{11... | collective-permute-start | bytes 6291464 | tf_op jit(solution)/shard_map/ppermute | solution.py:27
  129.2 15.6 %collective-permute-done.7 = bf16[256,2048]{1,0:T(8,128)(2,1)} collective-permute-done((bf16[256,2048]{1,0:T(8,128)(2,1)S(1)}, bf16[256,2048]{1,0:T(8,128)(2,1)}, u32[]{:S(2)}, u32[]{:S(2)}) %collective-permute-start.7) | collective-permute-done | bytes 1048608 | tf_op jit(solution)/shard_map/ppermute | solution.py:27
  146.2 7.4 %collective-permute-start.14 = (bf16[256,2048]{1,0:T(8,128)(2,1)}, bf16[256,2048]{1,0:T(8,128)(2,1)}, u32[]{:S(2)}, u32[]{:S(2)}) collective-permute-start(bf16[256,2048]{1,0:T(8,128)(2,1)} %collective-permute-done.8), channel_id=1, source_target_pairs={{0,129},{1,128},{2,131},{3,130},{4,133},{5,132},{6,135},{7,134},{8... | collective-permute-start | bytes 3145736 | tf_op jit(solution)/shard_map/ppermute | solution.py:27
  161.8 7.2 %shard_map.58 = (f32[256,256]{1,0:T(8,128)S(1)}, f32[256,256]{1,0:T(8,128)S(1)}, f32[256,256]{1,0:T(8,128)S(1)}, f32[256,256]{1,0:T(8,128)S(1)}, f32[256,256]{1,...) custom-call(s32[4]{0:T(128)S(1)} %add_convert_fusion.refs_0_, ...), custom_call_target="tpu_custom_call" | custom-call | flops 3221225472 | bytes 12582912 | tf_op jit(solution)/shard_map/pallas_call | solution.py:371
  169.9 5.6 %collective-permute-done.13.refs_11_.refs_34_ = bf16[256,2048]{1,0:T(8,128)(2,1)} collective-permute-done((bf16[256,2048]{1,0:T(8,128)(2,1)}, bf16[256,2048]{1,0:T(8,128)(2,1)}, u32[]{:S(2)}, u32[]{:S(2)}) %collective-permute-start.13) | collective-permute-done | bytes 1048608 | tf_op jit(solution)/shard_map/ppermute | solution.py:27
  175.5 11.9 %collective-permute-done.15.refs_13_.refs_37_ = bf16[256,4096]{1,0:T(8,128)(2,1)} collective-permute-done((bf16[256,4096]{1,0:T(8,128)(2,1)}, bf16[256,4096]{1,0:T(8,128)(2,1)}, u32[]{:S(2)}, u32[]{:S(2)}) %collective-permute-start.15) | collective-permute-done | bytes 2097184 | tf_op jit(solution)/shard_map/ppermute | solution.py:27
  187.5 7.1 %shard_map.59 = (f32[256,256]{1,0:T(8,128)S(1)}, f32[256,256]{1,0:T(8,128)S(1)}, f32[256,256]{1,0:T(8,128)S(1)}, f32[256,256]{1,0:T(8,128)S(1)}, f32[256,256]{1,...) custom-call(s32[4]{0:T(128)S(1)} %add_convert_fusion.refs_0_, f32[256,256]{1,0:T(8,128)S(1)} %copy-done.13, ...), custom_call_target="tpu_custom_call" | custom-call | flops 1610612736 | bytes 8388608 | tf_op jit(solution)/shard_map/pallas_call | solution.py:402
  194.7 7.2 %collective-permute-start.18 = (f32[2,256]{1,0:T(2,128)S(1)}, f32[2,256]{1,0:T(2,128)S(1)}, u32[]{:S(2)}, u32[]{:S(2)}) collective-permute-start(f32[2,256]{1,0:T(2,128)S(1)} %get-tuple-element.92.refs_20_), channel_id=1, source_target_pairs={{0,255},{1,0},{2,1},{3,2},{4,3},{5,4},{6,5},{7,6},{8,7},{9,8},{10,... | collective-permute-start | bytes 6152 | tf_op jit(solution)/shard_map/ppermute | solution.py:27
  201.9 6.0 %collective-permute-start.16 = (f32[2,256]{1,0:T(2,128)S(1)}, f32[2,256]{1,0:T(2,128)S(1)}, u32[]{:S(2)}, u32[]{:S(2)}) collective-permute-start(f32[2,256]{1,0:T(2,128)S(1)} %get-tuple-element.92.refs_20_), channel_id=1, source_target_pairs={{0,254},{1,255},{2,0},{3,1},{4,2},{5,3},{6,4},{7,5},{8,6},{9,7},{1... | collective-permute-start | bytes 6152 | tf_op jit(solution)/shard_map/ppermute | solution.py:27
  209.1 13.7 %shard_map.60 = (f32[256,4096]{1,0:T(8,128)}, f32[256,4096]{1,0:T(8,128)}) custom-call(s32[4]{0:T(128)S(1)} %add_convert_fusion.refs_0_, s32[1,256]{1,0:T(1,128)S(1)} %bitcast.35, f32[256,256]{1,0:T(8,128)S(1)} %copy.15.refs_2_, f32[256,256]{1,0:T(8,128)S(1)} %copy.16.refs_3_, f32[256,256]{1,0:T(8,128)S(1)} %copy.17.refs_4_, f32[256,256]{1,0:T(8,128)S(1)} %copy.18.refs_5_, ...), custom_call_target="tpu_custom_call" | custom-call | flops 8589934592 | bytes 29360128 | tf_op jit(solution)/shard_map/pallas_call | solution.py:443
  (67 shorter events, 27.0 us)
Async XLA Ops:
  0.6 68.3 %collective-permute-start.3 = (bf16[256,4096]{1,0:T(8,128)(2,1)}, bf16[256,4096]{1,0:T(8,128)(2,1)}, u32[]{:S(2)}, u32[]{:S(2)}) collective-permute-start(bf16[256,4096]{1,0:T(8,128)(2,1)} %refs_25_.1), channel_id=1, source_target_pairs={{0,129},{1,128},{2,131},{3,130},{4,133},{5,132},{6,135},{7,134},{8... | collective-permute-start | bytes 6291464 | tf_op jit(solution)/shard_map/ppermute | solution.py:27
  2.0 71.1 %collective-permute-start.4 = (bf16[256,4096]{1,0:T(8,128)(2,1)}, bf16[256,4096]{1,0:T(8,128)(2,1)}, u32[]{:S(2)}, u32[]{:S(2)}) collective-permute-start(bf16[256,4096]{1,0:T(8,128)(2,1)} %refs_26_.1), channel_id=1, source_target_pairs={{0,128},{1,129},{2,130},{3,131},{4,132},{5,133},{6,134},{7,135},{8... | collective-permute-start | bytes 6291464 | tf_op jit(solution)/shard_map/ppermute | solution.py:27
  2.7 72.4 %collective-permute-start.2 = (bf16[256,4096]{1,0:T(8,128)(2,1)}, bf16[256,4096]{1,0:T(8,128)(2,1)}, u32[]{:S(2)}, u32[]{:S(2)}) collective-permute-start(bf16[256,4096]{1,0:T(8,128)(2,1)} %refs_25_.1), channel_id=1, source_target_pairs={{0,255},{127,128},{128,127},{255,0}} | collective-permute-start | bytes 6291464 | tf_op jit(solution)/shard_map/ppermute | solution.py:27
  13.5 61.6 %collective-permute-start.1 = (bf16[256,4096]{1,0:T(8,128)(2,1)}, bf16[256,4096]{1,0:T(8,128)(2,1)}, u32[]{:S(2)}, u32[]{:S(2)}) collective-permute-start(bf16[256,4096]{1,0:T(8,128)(2,1)} %refs_26_.1), channel_id=1, source_target_pairs={{0,254},{1,255},{2,0},{3,1},{4,2},{5,3},{6,4},{7,5},{8,6},{9,7},{1... | collective-permute-start | bytes 6291464 | tf_op jit(solution)/shard_map/ppermute | solution.py:27
  13.6 61.5 %collective-permute-start = (bf16[256,4096]{1,0:T(8,128)(2,1)}, bf16[256,4096]{1,0:T(8,128)(2,1)}, u32[]{:S(2)}, u32[]{:S(2)}) collective-permute-start(bf16[256,4096]{1,0:T(8,128)(2,1)} %refs_26_.1), channel_id=1, source_target_pairs={{0,2},{1,3},{2,4},{3,5},{4,6},{5,7},{6,8},{7,9},{8,10},{9,11},{10,... | collective-permute-start | bytes 6291464 | tf_op jit(solution)/shard_map/ppermute | solution.py:27
  73.1 46.5 %collective-permute-start.5 = (bf16[256,4096]{1,0:T(8,128)(2,1)}, bf16[256,4096]{1,0:T(8,128)(2,1)}, u32[]{:S(2)}, u32[]{:S(2)}) collective-permute-start(bf16[256,4096]{1,0:T(8,128)(2,1)} %collective-permute-done.3), channel_id=1, source_target_pairs={{0,129},{1,128},{2,131},{3,130},{4,133},{5,132},{6,135},{7,134},{8... | collective-permute-start | bytes 6291464 | tf_op jit(solution)/shard_map/ppermute | solution.py:27
  73.1 47.6 %collective-permute-start.6 = (bf16[256,4096]{1,0:T(8,128)(2,1)}, bf16[256,4096]{1,0:T(8,128)(2,1)S(1)}, u32[]{:S(2)}, u32[]{:S(2)}) collective-permute-start(bf16[256,4096]{1,0:T(8,128)(2,1)} %collective-permute-done.4), channel_id=1, source_target_pairs={{0,128},{1,129},{2,130},{3,131},{4,132},{5,133},{6,134},{7,135},{8... | collective-permute-start | bytes 6291464 | tf_op jit(solution)/shard_map/ppermute | solution.py:27
  75.1 48.8 %collective-permute-start.11 = (bf16[256,4096]{1,0:T(8,128)(2,1)S(1)}, bf16[256,4096]{1,0:T(8,128)(2,1)S(1)}, u32[]{:S(2)}, u32[]{:S(2)}) collective-permute-start(bf16[256,4096]{1,0:T(8,128)(2,1)S(1)} %copy-done), channel_id=1, source_target_pairs={{2,0},{3,1},{4,2},{5,3},{6,4},{7,5},{8,6},{9,7},{10,8},{11,9},{12,... | collective-permute-start | bytes 6291464 | tf_op jit(solution)/shard_map/ppermute | solution.py:27
  76.4 51.4 %collective-permute-start.10 = (bf16[256,4096]{1,0:T(8,128)(2,1)S(1)}, bf16[256,4096]{1,0:T(8,128)(2,1)S(1)}, u32[]{:S(2)}, u32[]{:S(2)}) collective-permute-start(bf16[256,4096]{1,0:T(8,128)(2,1)S(1)} %copy-done), channel_id=1, source_target_pairs={{0,2},{1,3},{2,4},{3,5},{4,6},{5,7},{6,8},{7,9},{8,10},{9,11},{10,... | collective-permute-start | bytes 6291464 | tf_op jit(solution)/shard_map/ppermute | solution.py:27
  81.1 48.1 %collective-permute-start.9 = (bf16[256,4096]{1,0:T(8,128)(2,1)S(1)}, bf16[256,4096]{1,0:T(8,128)(2,1)}, u32[]{:S(2)}, u32[]{:S(2)}) collective-permute-start(bf16[256,4096]{1,0:T(8,128)(2,1)S(1)} %copy-done), channel_id=1, source_target_pairs={{0,134},{1,135},{126,248},{127,249},{128,6},{129,7},{254,120},{255... | collective-permute-start | bytes 6291464 | tf_op jit(solution)/shard_map/ppermute | solution.py:27
  98.2 55.5 %copy-start.15 = (s32[256]{0:T(256)S(1)}, s32[256]{0:T(256)}, u32[]{:S(2)}) copy-start(s32[256]{0:T(256)} %param.5) | copy-start | bytes 3076
  120.7 24.1 %collective-permute-start.7 = (bf16[256,2048]{1,0:T(8,128)(2,1)S(1)}, bf16[256,2048]{1,0:T(8,128)(2,1)}, u32[]{:S(2)}, u32[]{:S(2)}) collective-permute-start(bf16[256,2048]{1,0:T(8,128)(2,1)S(1)} %get-tuple-element.63), channel_id=1, source_target_pairs={{0,128},{1,129},{2,130},{3,131},{4,132},{5,133},{6,134},{7,135},{8... | collective-permute-start | bytes 3145736 | tf_op jit(solution)/shard_map/ppermute | solution.py:27
  121.2 23.6 %collective-permute-start.8 = (bf16[256,2048]{1,0:T(8,128)(2,1)S(1)}, bf16[256,2048]{1,0:T(8,128)(2,1)}, u32[]{:S(2)}, u32[]{:S(2)}) collective-permute-start(bf16[256,2048]{1,0:T(8,128)(2,1)S(1)} %get-tuple-element.64), channel_id=1, source_target_pairs={{0,129},{1,128},{2,131},{3,130},{4,133},{5,132},{6,135},{7,134},{8... | collective-permute-start | bytes 3145736 | tf_op jit(solution)/shard_map/ppermute | solution.py:27
  125.2 44.7 %collective-permute-start.12 = (bf16[256,4096]{1,0:T(8,128)(2,1)}, bf16[256,4096]{1,0:T(8,128)(2,1)}, u32[]{:S(2)}, u32[]{:S(2)}) collective-permute-start(bf16[256,4096]{1,0:T(8,128)(2,1)} %collective-permute-done.5.refs_13_.refs_31_), channel_id=1, source_target_pairs={{0,2},{2,4},{3,1},{4,6},{5,3},{6,8},{7,5},{8,10},{9,7},{10,12},{11... | collective-permute-start | bytes 6291464 | tf_op jit(solution)/shard_map/ppermute | solution.py:27
  144.8 42.6 %collective-permute-start.15 = (bf16[256,4096]{1,0:T(8,128)(2,1)}, bf16[256,4096]{1,0:T(8,128)(2,1)}, u32[]{:S(2)}, u32[]{:S(2)}) collective-permute-start(bf16[256,4096]{1,0:T(8,128)(2,1)} %collective-permute-done.9), channel_id=1, source_target_pairs={{6,126},{7,127},{120,0},{121,1},{134,254},{135,255},{248,128},{249... | collective-permute-start | bytes 6291464 | tf_op jit(solution)/shard_map/ppermute | solution.py:27
  146.1 29.4 %collective-permute-start.13 = (bf16[256,2048]{1,0:T(8,128)(2,1)}, bf16[256,2048]{1,0:T(8,128)(2,1)}, u32[]{:S(2)}, u32[]{:S(2)}) collective-permute-start(bf16[256,2048]{1,0:T(8,128)(2,1)} %collective-permute-done.7), channel_id=1, source_target_pairs={{0,128},{1,129},{2,130},{3,131},{4,132},{5,133},{6,134},{7,135},{8... | collective-permute-start | bytes 3145736 | tf_op jit(solution)/shard_map/ppermute | solution.py:27
  146.2 29.3 %collective-permute-start.14 = (bf16[256,2048]{1,0:T(8,128)(2,1)}, bf16[256,2048]{1,0:T(8,128)(2,1)}, u32[]{:S(2)}, u32[]{:S(2)}) collective-permute-start(bf16[256,2048]{1,0:T(8,128)(2,1)} %collective-permute-done.8), channel_id=1, source_target_pairs={{0,129},{1,128},{2,131},{3,130},{4,133},{5,132},{6,135},{7,134},{8... | collective-permute-start | bytes 3145736 | tf_op jit(solution)/shard_map/ppermute | solution.py:27
  161.8 25.6 %copy-start.12 = (f32[256,256]{1,0:T(8,128)S(1)}, f32[256,256]{1,0:T(8,128)}, u32[]{:S(2)}) copy-start(f32[256,256]{1,0:T(8,128)} %fusion.refs_2_) | copy-start | bytes 786436
  161.8 25.6 %copy-start.13 = (f32[256,256]{1,0:T(8,128)S(1)}, f32[256,256]{1,0:T(8,128)}, u32[]{:S(2)}) copy-start(f32[256,256]{1,0:T(8,128)} %fusion.1.refs_1_) | copy-start | bytes 786436
  187.4 21.7 %copy-start.9 = (f32[256,256]{1,0:T(8,128)S(1)}, f32[256,256]{1,0:T(8,128)}, u32[]{:S(2)}) copy-start(f32[256,256]{1,0:T(8,128)} %fusion.4.refs_6_) | copy-start | bytes 786436
  194.6 13.2 %collective-permute-start.19 = (f32[2,256]{1,0:T(2,128)S(1)}, f32[2,256]{1,0:T(2,128)S(1)}, u32[]{:S(2)}, u32[]{:S(2)}) collective-permute-start(f32[2,256]{1,0:T(2,128)S(1)} %get-tuple-element.92.refs_20_), channel_id=1, source_target_pairs={{0,1},{1,2},{2,3},{3,4},{4,5},{5,6},{6,7},{7,8},{8,9},{9,10},{10,1... | collective-permute-start | bytes 6152 | tf_op jit(solution)/shard_map/ppermute | solution.py:27
  194.7 13.1 %collective-permute-start.18 = (f32[2,256]{1,0:T(2,128)S(1)}, f32[2,256]{1,0:T(2,128)S(1)}, u32[]{:S(2)}, u32[]{:S(2)}) collective-permute-start(f32[2,256]{1,0:T(2,128)S(1)} %get-tuple-element.92.refs_20_), channel_id=1, source_target_pairs={{0,255},{1,0},{2,1},{3,2},{4,3},{5,4},{6,5},{7,6},{8,7},{9,8},{10,... | collective-permute-start | bytes 6152 | tf_op jit(solution)/shard_map/ppermute | solution.py:27
  201.9 7.2 %collective-permute-start.17 = (f32[2,256]{1,0:T(2,128)S(1)}, f32[2,256]{1,0:T(2,128)S(1)}, u32[]{:S(2)}, u32[]{:S(2)}) collective-permute-start(f32[2,256]{1,0:T(2,128)S(1)} %get-tuple-element.92.refs_20_), channel_id=1, source_target_pairs={{0,2},{1,3},{2,4},{3,5},{4,6},{5,7},{6,8},{7,9},{8,10},{9,11},{10,... | collective-permute-start | bytes 6152 | tf_op jit(solution)/shard_map/ppermute | solution.py:27
  201.9 7.3 %collective-permute-start.16 = (f32[2,256]{1,0:T(2,128)S(1)}, f32[2,256]{1,0:T(2,128)S(1)}, u32[]{:S(2)}, u32[]{:S(2)}) collective-permute-start(f32[2,256]{1,0:T(2,128)S(1)} %get-tuple-element.92.refs_20_), channel_id=1, source_target_pairs={{0,254},{1,255},{2,0},{3,1},{4,2},{5,3},{6,4},{7,5},{8,6},{9,7},{1... | collective-permute-start | bytes 6152 | tf_op jit(solution)/shard_map/ppermute | solution.py:27
  (12 other events, 67.9 us)
